TPU v7x, 256 devices: a whole 4x4x8 slice. The times are simulated.
256 devices in a mesh: dp: 4 (over x), mp: 64 (over y, z, core).
Axes of the slice: x: 4, y: 4, z: 8, core: 2. Of those that a mesh axis runs over, the one named last changes fastest.
Arguments:
- tokens: bfloat16 [1024, 8192], P('dp', 'mp'), may hold values from -6 to 6
- cotangent: bfloat16 [1024, 8192], P('dp', 'mp'), may hold values from -6 to 6
- weight_codes: int32 [192, 48, 128, 128], P('mp'), may hold values from 0 to 4095
- block_scales: float32 [3, 192, 48, 128], P(None, 'mp'), may hold values from 0.0011 to 0.01
- block_index: int32 [192, 48], P('mp'), may hold values from 0 to 63, as said below
- block_count: int32 [192], P('mp'), may hold values from 16 to 48, as said below
- ia3_scale: float32 [24576], P('mp'), may hold values from 0.1 to 1.9
Outputs:
- input_grad: bfloat16 [1024, 8192], P('dp', 'mp')
- ia3_grad: float32 [24576], P('mp')
Inputs may be any that keep to these rules, and one draw needn't show every extreme that they name: `block_index`: each row holds 48 different block numbers; only its first block_count entries are live. `block_count`: some hidden block has exactly 48 live slots and another exactly 16.
All inputs are finite; a program needn't handle non-finite values.
Results may differ from a plain program's by a relative error of at most 0.0072.
Values may be sent and summed in bfloat16 or wider, within the bound.
No kernel may reach another device: no remote copies, remote signals or barrier semaphores. Data moves between devices by JAX's collectives and lax.ppermute only.
A program may use at most 128 MiB of HBM per device.

v0:
```python
import functools

import jax
import jax.numpy as jnp
from jax import lax
from jax.experimental import pallas as pl
from jax.experimental.pallas import tpu as pltpu
from jax.sharding import PartitionSpec as P

NY, NZ = 4, 8
MB = 1 << 20
F32, BF16 = jnp.float32, jnp.bfloat16
VMEM = pl.BlockSpec(memory_space=pltpu.VMEM)
ANY = pl.BlockSpec(memory_space=pl.ANY)
SMEM = pl.BlockSpec(memory_space=pltpu.SMEM)


def dev(y, z, c):
    return ((y % NY) * NZ + z % NZ) * 2 + c


def send(a, dy=0, dz=0, flip=False, signed=False):
    pairs = []
    for y in range(NY):
        for z in range(NZ):
            for c in range(2):
                s = -1 if signed and c else 1
                pairs.append((dev(y, z, c), dev(y + s * dy, z + s * dz, 1 - c if flip else c)))
    return lax.ppermute(a, "mp", pairs)


def swap(a):
    return send(a, flip=True)


def array(shape, dtype):
    return jax.ShapeDtypeStruct(shape, dtype)


FLAG = array((1,), jnp.int32)


def call(kernel, name, ins, outs, scratch=(), limit=6, flops=0, after=(), keep=()):
    def space(a):
        return SMEM if a.dtype == jnp.int32 and a.size < 1024 else VMEM

    skip = len(after) + len(keep)
    size = sum(a.size * a.dtype.itemsize for a in tuple(ins) + tuple(outs))
    return pl.pallas_call(
        (lambda *refs: kernel(*refs[skip:])) if skip else kernel,
        in_specs=[ANY] * len(after) + [VMEM] * len(keep) + [space(a) for a in ins],
        out_specs=[space(a) for a in outs],
        out_shape=list(outs),
        scratch_shapes=list(scratch),
        compiler_params=pltpu.CompilerParams(vmem_limit_bytes=limit * MB),
        cost_estimate=pl.CostEstimate(flops=flops, bytes_accessed=size, transcendentals=0),
        name=name,
    )(*after, *keep, *ins)


CHUNK = 16


def dequant_kernel(h, codes_ref, index_ref, count_ref, scales_ref, gu_ref, down_ref, flag_ref, words, sems):
    flag_ref[0] = 0
    count = count_ref[h]
    cuts = range(0, 48, CHUNK)

    def copy(kc):
        b = kc // CHUNK
        return pltpu.make_async_copy(codes_ref.at[h, pl.ds(kc, CHUNK)], words.at[b], sems.at[b])

    for kc in cuts:
        copy(kc).start()
    gu_ref[...] = jnp.zeros(gu_ref.shape, BF16)
    down_ref[...] = jnp.zeros(down_ref.shape, BF16)
    for kc in cuts:
        copy(kc).wait()

        def slots(s, carry):
            for u in range(4):
                j = 4 * s + u
                k = kc + j
                n = index_ref[h, k]
                live = jnp.where(k < count, 1.0, 0.0).astype(F32)
                coded = words[kc // CHUNK, j] ^ 0x888

                def part(p):
                    v = ((coded << (28 - 4 * p)) >> 28).astype(F32)
                    return (v * (scales_ref[p, h, pl.ds(k, 1), :] * live)).astype(BF16)

                gu_ref[n, :, 0:128] = part(0)
                gu_ref[n, :, 128:256] = part(1)
                down_ref[n] = part(2)
            return carry

        lax.fori_loop(0, jnp.clip((count - kc + 3) // 4, 0, CHUNK // 4), slots, 0)


def dequant(h, codes, scales, index, count, after=()):
    outs = (array((64, 128, 256), BF16), array((64, 128, 128), BF16), FLAG)
    kernel = functools.partial(dequant_kernel, h)
    skip = len(after)
    return pl.pallas_call(
        (lambda *refs: kernel(*refs[skip:])) if skip else kernel,
        in_specs=[ANY] * skip + [ANY, SMEM, SMEM, VMEM],
        out_specs=[VMEM, VMEM, SMEM],
        out_shape=outs,
        scratch_shapes=[pltpu.VMEM((48 // CHUNK, CHUNK, 128, 128), jnp.int32), pltpu.SemaphoreType.DMA((48 // CHUNK,))],
        compiler_params=pltpu.CompilerParams(vmem_limit_bytes=14 * MB),
        cost_estimate=pl.CostEstimate(flops=12_000_000, bytes_accessed=10 * MB, transcendentals=0),
        name="dequant",
    )(*after, codes, index, count, scales)


def chip_of(pos_ref, dy, dz):
    y, z = pos_ref[0], pos_ref[1]
    return lax.rem(y + dy + 2 * NY, NY) * NZ + lax.rem(z + dz + 2 * NZ, NZ)


def chips(pos_ref, places):
    sign = 1 - 2 * pos_ref[2]
    return [chip_of(pos_ref, dy, dz) for place in places for dy, dz in place(sign)]


def own_kernel(tok, cot, sib_t, sib_c, pos_ref, chip_t, chip_c, own_c, tv, cv, sems):
    c = pos_ref[2]
    moves = (
        pltpu.make_async_copy(cot, cv.at[0], sems.at[0]),
        pltpu.make_async_copy(sib_c, cv.at[1], sems.at[1]),
        pltpu.make_async_copy(tok, tv.at[0], sems.at[2]),
        pltpu.make_async_copy(sib_t, tv.at[1], sems.at[3]),
    )
    for move in moves:
        move.start()
    moves[0].wait()
    mine = cv[0].T
    own_c[...] = mine
    chip_c[c] = mine
    moves[1].wait()
    chip_c[1 - c] = cv[1].T
    moves[2].wait()
    chip_t[c] = tv[0]
    moves[3].wait()
    chip_t[1 - c] = tv[1]


def own(pos, tokens, cotangent, sib_t, sib_c):
    return pl.pallas_call(
        own_kernel,
        in_specs=[ANY] * 4 + [SMEM],
        out_specs=[VMEM] * 3,
        out_shape=[array((2, 256, 128), BF16), array((2, 128, 256), BF16), array((128, 256), BF16)],
        scratch_shapes=[
            pltpu.VMEM((2, 256, 128), BF16),
            pltpu.VMEM((2, 256, 128), BF16),
            pltpu.SemaphoreType.DMA((4,)),
        ],
        compiler_params=pltpu.CompilerParams(vmem_limit_bytes=6 * MB),
        cost_estimate=pl.CostEstimate(flops=0, bytes_accessed=MB, transcendentals=0),
        name="own",
    )(tokens, cotangent, sib_t, sib_c, pos)


def stack_kernel(*refs):
    out, at = refs[-1], 0
    for r in refs[:-1]:
        n = r.shape[0] if len(r.shape) == 3 else 1
        out[at : at + n] = r[...].reshape((n,) + r.shape[-2:])
        at += n


def stack(parts, after=()):
    n = sum(p.shape[0] if p.ndim == 3 else 1 for p in parts)
    return call(stack_kernel, "stack", tuple(parts), (array((n,) + parts[0].shape[-2:], BF16),), after=after)[0]


def merge_t_kernel(pos_ref, chip, mine, other, t0, t1):
    c = pos_ref[2]
    t0[0:2] = chip[...]
    t0[2 + c] = mine[2]
    t0[3 - c] = other[2]
    t1[pl.ds(2 * c, 2)] = mine[0:2]
    t1[pl.ds(2 - 2 * c, 2)] = other[0:2]


def merge_c_kernel(pos_ref, chip, mine, other, out):
    c = pos_ref[2]
    out[0:2] = chip[...]
    out[2 + c] = mine[6]
    out[3 - c] = other[6]
    for i in range(3):
        out[pl.ds(4 + 4 * i + 2 * c, 2)] = mine[2 * i : 2 * i + 2]
        out[pl.ds(6 + 4 * i - 2 * c, 2)] = other[2 * i : 2 * i + 2]


def part_kernel(pos_ref, a, out):
    n = out.shape[0]
    out[...] = a[pl.ds(n * pos_ref[2], n)]


def part_of(pos, a, after):
    return call(part_kernel, "part", (pos, a), (array((a.shape[0] // 2,) + a.shape[1:], a.dtype),), after=after, flops=15_000_000_000)[0]


def pick_kernel(pos_ref, a, b, out):
    @pl.when(pos_ref[2] == 0)
    def _():
        out[...] = a[...]

    @pl.when(pos_ref[2] == 1)
    def _():
        out[...] = b[...]


def pick(pos, a, b, after=(), keep=()):
    return call(pick_kernel, "pick", (pos, a, b), (array(a.shape, a.dtype),), after=after, keep=keep)[0]


def gate_up_kernel(places, first, last, pos_ref, w0, w1, w2, *refs):
    pieces = refs[: len(places)]
    rest = refs[len(places) :]
    out_ref, flag_ref = rest[-2], rest[-1]
    flag_ref[0] = 0
    where = chips(pos_ref, places)
    blocks = [piece[i] for piece in pieces for i in range(piece.shape[0])]
    for h, w in enumerate((w0, w1, w2)):
        acc = None if first else rest[0][h]
        for g in range(0, len(where), 8):
            cut = where[g : g + 8]
            lhs = jnp.concatenate(blocks[2 * g : 2 * g + 2 * len(cut)], axis=1)
            rhs = jnp.concatenate([w[pl.ds(2 * j, 2)].reshape(256, 256) for j in cut], axis=0)
            term = jnp.dot(lhs, rhs, preferred_element_type=F32)
            acc = term if acc is None else acc + term
        out_ref[h] = acc.T if last else acc


def gate_up(pos, ws, pieces, places, acc=None, last=False, after=()):
    ins = (pos,) + tuple(ws) + tuple(pieces) + (() if acc is None else (acc,))
    return call(
        functools.partial(gate_up_kernel, places, acc is None, last),
        "gate_up",
        ins,
        (array((3, 256, 256), F32), FLAG),
        limit=24,
        flops=sum(p.shape[0] for p in pieces) * 2 * 256 * 128 * 768,
        after=after,
    )


def hidden_kernel(places, first, last, pos_ref, w0, w1, w2, *refs):
    pieces = refs[: len(places)]
    rest = refs[len(places) :]
    where = chips(pos_ref, places)
    blocks = [piece[i] for piece in pieces for i in range(piece.shape[0])]
    acc = None if first else rest[0][...]
    for g in range(0, len(where), 8):
        cut = where[g : g + 8]
        lhs = jnp.concatenate(
            [jnp.concatenate([w[2 * j + c] for j in cut for c in range(2)], axis=1) for w in (w0, w1, w2)],
            axis=0,
        )
        rhs = jnp.concatenate([blocks[2 * i + c] for i in range(g, g + 8) for c in range(2)], axis=0)
        term = jnp.dot(lhs, rhs, preferred_element_type=F32)
        acc = term if acc is None else acc + term
    if not last:
        rest[-1][...] = acc
        return
    gu_ref, scale_ref, grad_ref, ia3_ref = rest[-4:]
    for h in range(3):
        rows = slice(128 * h, 128 * h + 128)
        hidden = acc[rows]
        gate = gu_ref[h, 0:128]
        up = gu_ref[h, 128:256]
        s = jax.nn.sigmoid(gate)
        activated = gate * s
        ia3_ref[:, rows] = jnp.sum((hidden * activated * up).T, axis=0, keepdims=True)
        scaled = hidden * scale_ref[rows, :]
        grad_ref[h, 0:128] = (scaled * up * s * (1.0 + gate * (1.0 - s))).astype(BF16)
        grad_ref[h, 128:256] = (scaled * activated).astype(BF16)


def hidden(pos, ws, pieces, places, acc=None, gu=None, scale=None):
    last = gu is not None
    ins = (pos,) + tuple(ws) + tuple(pieces) + (() if acc is None else (acc,)) + ((gu, scale) if last else ())
    outs = (array((3, 256, 256), BF16), array((1, 384), F32)) if last else (array((384, 256), F32),)
    return call(
        functools.partial(hidden_kernel, places, acc is None, last),
        "hidden",
        ins,
        outs,
        limit=16,
        flops=sum(p.shape[0] for p in pieces) * 2 * 384 * 128 * 256,
    )


def input_kernel(order, par_of, pos_ref, grad_ref, w0, w1, w2, *refs):
    par = par_of(pos_ref[2])
    where = [2 * chip_of(pos_ref, dy, dz) + par for dy, dz in order]
    added, outs = (refs[0], refs[1:]) if len(refs) > 1 else (None, refs)
    for g in range(0, len(order), 4):
        cut = where[g : g + 4]
        acc = None
        for h, w in enumerate((w0, w1, w2)):
            lhs = jnp.concatenate([w[j] for j in cut], axis=0)
            term = jnp.dot(lhs, grad_ref[h], preferred_element_type=F32)
            acc = term if acc is None else acc + term
        acc = acc.reshape(len(cut), 128, 256)
        if added is not None:
            acc = acc + added[g : g + 4].astype(F32)
            outs[g // 4][...] = acc.astype(outs[g // 4].dtype)
        else:
            outs[0][g : g + 4] = acc.astype(BF16)


def input_part(pos, grad, ws, order, added=None, after=()):
    n = len(order)
    if added is None:
        kernel = functools.partial(input_kernel, order, lambda c: 1 - c)
        outs = [array((n, 128, 256), BF16)]
    else:
        kernel = functools.partial(input_kernel, order, lambda c: c)
        outs = [array((4, 128, 256), BF16)] * (n // 4 - 2) + [array((4, 128, 256), F32)] * 2
    return call(
        kernel,
        "input_away" if added is None else "input_here",
        (pos, grad) + tuple(ws) + (() if added is None else (added,)),
        outs,
        limit=24,
        flops=n * 2 * 128 * 256 * 768,
        after=after,
    )


def add_kernel(a, r, out):
    out[...] = (a[...] + r[...].astype(F32)).astype(BF16)


def add(a, r):
    return call(add_kernel, "add", (a, r), (array(a.shape, BF16),))[0]


def y_sum_kernel(pos_ref, a0, ra1, ra3, b0, rb1, rb3, out):
    for i in range(4):
        for at, v, r, q in ((i, a0, ra1, ra3), (i + 4, b0, rb1, rb3)):
            total = v[i] + (r[i].astype(F32) + q[i].astype(F32))
            out[lax.rem(pos_ref[1] + at, NZ)] = total.astype(BF16)


def z_sum_kernel(parts, out):
    v = parts[0].astype(F32)
    for i in range(1, NZ):
        v = v + parts[i].astype(F32)
    out[...] = v.T.astype(BF16)


def on_device(tokens, cotangent, weight_codes, block_scales, block_index, block_count, ia3_scale):
    m = lax.axis_index("mp")
    pos = jnp.stack([m // (2 * NZ), lax.rem(m // 2, NZ), lax.rem(m, 2)]).astype(jnp.int32)
    block = (256, 128)

    with jax.named_scope("gather"):
        sib_t = swap(tokens)
        sib_c = swap(cotangent)
        chip_t, chip_c, own_c = own(pos, tokens, cotangent, sib_t, sib_c)
        near_t = stack([send(chip_t, dy=1, signed=True), send(tokens, dy=2)])
        t0, t1 = call(merge_t_kernel, "merge_t", (pos, chip_t, near_t, swap(near_t)), [array((4, 256, 128), BF16)] * 2)
        near_c = stack([send(chip_c, dz=d, signed=True) for d in (1, 2, 3)] + [send(own_c, dz=4)], after=(near_t,))
        c0 = call(
            merge_c_kernel, "merge_c", (pos, chip_c, near_c, swap(near_c)), [array((16, 128, 256), BF16)]
        )[0]
        e1 = send(c0, dy=1, signed=True)
        ws = [dequant(h, weight_codes, block_scales, block_index, block_count, (c0,)) for h in range(3)]
        w_gu, w_down, ready = ([w[i] for w in ws] for i in range(3))

        f0, f1, steps = t0, t1, []
        for i in range(3):
            if i:
                f1, ready[i - 1] = lax.optimization_barrier((f1, ready[i - 1]))
            f0 = send(f0, dz=1, signed=True)
            f1 = send(f1, dz=1, signed=True)
            steps.append((f0, f1))
        mine = stack(steps[0] + steps[1])
        ys = (0, 2, -1, 1)
        t_pieces = [t0, t1, mine, swap(mine)]
        t_places = [
            lambda s: ((0, 0), (2, 0)),
            lambda s: ((-1, 0), (1, 0)),
            lambda s: tuple((dy, -n * s) for n in (1, 2) for dy in ys),
            lambda s: tuple((dy, n * s) for n in (1, 2) for dy in ys),
        ]
        gu, _ = gate_up(pos, w_gu, t_pieces, t_places, after=tuple(ready))
        e2 = send(part_of(pos, e1, ()), dy=1, signed=True)
        c_pieces = [c0, e1, swap(e1), e2, swap(e2)]
        dzs = (0, 4, -1, 1, -2, 2, -3, 3)

        def chosen(sel):
            return tuple((2, (1 + sel) // 2 * u + (1 - sel) // 2 * v) for u, v in zip(dzs[:4], dzs[4:]))

        c_places = [
            lambda s: tuple((0, d) for d in dzs),
            lambda s: tuple((-s, d) for d in dzs),
            lambda s: tuple((s, d) for d in dzs),
            lambda s: chosen(s),
            lambda s: chosen(-s),
        ]
        (part,) = hidden(pos, w_down, c_pieces[:3], c_places[:3])
        f4 = send(pick(pos, f0, f1, after=(ready[2],)), dz=1, signed=True)
        f4, gu, part = lax.optimization_barrier((f4, gu, part))
        mine = stack(steps[2])
        t_pieces = [mine, swap(mine), f4, swap(f4)]
        t_places = [
            lambda s: tuple((dy, -3 * s) for dy in ys),
            lambda s: tuple((dy, 3 * s) for dy in ys),
            lambda s: (((s - 1) // 2, 4), (1 + (s + 1) // 2, 4)),
            lambda s: (((-s - 1) // 2, 4), (1 + (1 - s) // 2, 4)),
        ]
        gu, _ = gate_up(pos, w_gu, t_pieces, t_places, gu, last=True)

        grad, ia3_part = hidden(pos, w_down, c_pieces[3:], c_places[3:], part, gu, ia3_scale[:, None])

    with jax.named_scope("ia3"):
        ia3_part = ia3_part.reshape(384)
        ia3_part = ia3_part + lax.ppermute(ia3_part, "dp", [(0, 1), (1, 0), (2, 3), (3, 2)])
        ia3_grad = ia3_part + lax.ppermute(ia3_part, "dp", [(0, 3), (3, 0), (1, 2), (2, 1)])

    with jax.named_scope("scatter"):
        cuts = ((0, 1, 2, 3), (4, 5, 6, 7))
        ways = ((2, 3, 1, 0), (2, 1, 3, 0))
        orders = [[(dy, dz) for dy in way for dz in dzs] for way, dzs in zip(ways, cuts)]
        sib = [swap(input_part(pos, grad, w_gu, order)[0]) for order in orders]
        a2, a3, a1, a0 = input_part(pos, grad, w_gu, orders[0], sib[0])
        ra2 = send(a2, dy=1)
        ra3 = send(a3, dy=-1)
        b2, b1, b3, b0 = input_part(pos, grad, w_gu, orders[1], sib[1])
        rb2 = send(b2, dy=-1)
        rb1 = send(b1, dy=1)
        ra1 = send(add(a1, ra2), dy=1)
        rb3 = send(add(b3, rb2), dy=-1)
        ra1, ia3_grad = lax.optimization_barrier((ra1, ia3_grad))
        total = call(y_sum_kernel, "y_sum", (pos, a0, ra1, ra3, b0, rb1, rb3), [array((8, 128, 256), BF16)])[0]
        columns = [[dev(y, z, c) for z in range(NZ)] for y in range(NY) for c in range(2)]
        total = lax.all_to_all(total, "mp", 0, 0, axis_index_groups=columns, tiled=True)
        input_grad = call(z_sum_kernel, "z_sum", (total,), [array((256, 128), BF16)])[0]
    return (input_grad, ia3_grad)


def solution(mesh):
    return jax.shard_map(
        on_device,
        mesh=mesh,
        in_specs=(
            P("dp", "mp"),
            P("dp", "mp"),
            P("mp", None, None, None),
            P(None, "mp", None, None),
            P("mp", None),
            P("mp"),
            P("mp"),
        ),
        out_specs=(P("dp", "mp"), P("mp")),
        check_vma=False,
    )
```

profile of v0, /device:TPU:24, one launch (start us, length us, event | category | flops | bytes accessed | tf_op | source)
XLA Modules:
  0.0 137.5 jit_solution(7766243520172757968)
XLA Ops:
  0.7 1.3 collective-permute-start.3
  2.3 1.2 collective-permute-done.1.sib_c
  3.5 0.8 copy-done.2
  4.4 0.8 copy-done.3
  5.2 1.1 own.1
  6.3 2.3 %collective-permute-start.2 = (bf16[2,256,128]{2,1,0:T(8,128)(2,1)S(1)}, bf16[2,256,128]{2,1,0:T(8,128)(2,1)S(1)}, u32[]{:S(2)}, u32[]{:S(2)}) collective-permute-start(bf16[2,256,128]{2,1,0:T(8,128)(2,1)S(1)} %get-tuple-element.38.chip), channel_id=1, source_target_pairs={{0,16},{1,49},{2,18},{3,51},{4,20},{5,53},{6,22},{7,55},{8,24},{9,... | collective-permute-start | bytes 393224 | tf_op jit(solution)/shard_map/gather/ppermute | solution.py:29
  8.6 1.9 %collective-permute-start.4 = (bf16[2,128,256]{2,1,0:T(8,128)(2,1)S(1)}, bf16[2,128,256]{2,1,0:T(8,128)(2,1)S(1)}, u32[]{:S(2)}, u32[]{:S(2)}) collective-permute-start(bf16[2,128,256]{2,1,0:T(8,128)(2,1)S(1)} %get-tuple-element.37.chip), channel_id=1, source_target_pairs={{0,2},{1,15},{2,4},{3,1},{4,6},{5,3},{6,8},{7,5},{8,10},{9,7},{10,... | collective-permute-start | bytes 393224 | tf_op jit(solution)/shard_map/gather/ppermute | solution.py:29
  10.5 3.3 %collective-permute-start.5 = (bf16[2,128,256]{2,1,0:T(8,128)(2,1)S(1)}, bf16[2,128,256]{2,1,0:T(8,128)(2,1)S(1)}, u32[]{:S(2)}, u32[]{:S(2)}) collective-permute-start(bf16[2,128,256]{2,1,0:T(8,128)(2,1)S(1)} %get-tuple-element.37.chip), channel_id=1, source_target_pairs={{0,4},{1,13},{2,6},{3,15},{4,8},{5,1},{6,10},{7,3},{8,12},{9,5},{1... | collective-permute-start | bytes 393224 | tf_op jit(solution)/shard_map/gather/ppermute | solution.py:29
  13.7 4.0 %collective-permute-start.6 = (bf16[2,128,256]{2,1,0:T(8,128)(2,1)S(1)}, bf16[2,128,256]{2,1,0:T(8,128)(2,1)S(1)}, u32[]{:S(2)}, u32[]{:S(2)}) collective-permute-start(bf16[2,128,256]{2,1,0:T(8,128)(2,1)S(1)} %get-tuple-element.37.chip), channel_id=1, source_target_pairs={{0,6},{1,11},{2,8},{3,13},{4,10},{5,15},{6,12},{7,1},{8,14},{9,3},... | collective-permute-start | bytes 393224 | tf_op jit(solution)/shard_map/gather/ppermute | solution.py:29
  17.8 0.5 collective-permute-start.7
  18.3 9.0 %collective-permute-done.7.refs_4_ = bf16[128,256]{1,0:T(8,128)(2,1)S(1)} collective-permute-done((bf16[128,256]{1,0:T(8,128)(2,1)S(1)}, bf16[128,256]{1,0:T(8,128)(2,1)S(1)}, u32[]{:S(2)}, u32[]{:S(2)}) %collective-permute-start.7) | collective-permute-done | bytes 65568 | tf_op jit(solution)/shard_map/gather/ppermute | solution.py:29
  27.4 0.6 collective-permute-done.6.refs_3_
  28.1 1.8 %collective-permute-done.8.other = bf16[7,128,256]{2,1,0:T(8,128)(2,1)S(1)} collective-permute-done((bf16[7,128,256]{2,1,0:T(8,128)(2,1)S(1)}, bf16[7,128,256]{2,1,0:T(8,128)(2,1)S(1)}, u32[]{:S(2)}, u32[]{:S(2)}) %collective-permute-start.8) | collective-permute-done | bytes 458784 | tf_op jit(solution)/shard_map/gather/ppermute | solution.py:29
  29.9 0.6 merge_c.1.refs_0_
  30.5 1.2 collective-permute-start.9
  31.7 1.4 %collective-permute-done.12.other = bf16[3,256,128]{2,1,0:T(8,128)(2,1)S(1)} collective-permute-done((bf16[3,256,128]{2,1,0:T(8,128)(2,1)S(1)}, bf16[3,256,128]{2,1,0:T(8,128)(2,1)S(1)}, u32[]{:S(2)}, u32[]{:S(2)}) %collective-permute-start.12) | collective-permute-done | bytes 196640 | tf_op jit(solution)/shard_map/gather/ppermute | solution.py:29
  33.1 0.6 merge_t.1
  33.7 1.6 %collective-permute-start.16 = (bf16[4,256,128]{2,1,0:T(8,128)(2,1)S(1)}, bf16[4,256,128]{2,1,0:T(8,128)(2,1)S(1)}, u32[]{:S(2)}, u32[]{:S(2)}) collective-permute-start(bf16[4,256,128]{2,1,0:T(8,128)(2,1)S(1)} %get-tuple-element.45.refs_8_), channel_id=1, source_target_pairs={{0,2},{1,15},{2,4},{3,1},{4,6},{5,3},{6,8},{7,5},{8,10},{9,7},{10,... | collective-permute-start | bytes 786440 | tf_op jit(solution)/shard_map/gather/ppermute | solution.py:29
  35.4 2.1 %collective-permute-start.13 = (bf16[4,256,128]{2,1,0:T(8,128)(2,1)S(1)}, bf16[4,256,128]{2,1,0:T(8,128)(2,1)S(1)}, u32[]{:S(2)}, u32[]{:S(2)}) collective-permute-start(bf16[4,256,128]{2,1,0:T(8,128)(2,1)S(1)} %get-tuple-element.44.refs_7_), channel_id=1, source_target_pairs={{0,2},{1,15},{2,4},{3,1},{4,6},{5,3},{6,8},{7,5},{8,10},{9,7},{10,... | collective-permute-start | bytes 786440 | tf_op jit(solution)/shard_map/gather/ppermute | solution.py:29
  37.5 3.7 %copy-done = s32[3,48,128,128]{3,2,1,0:T(8,128)S(1)} copy-done((s32[3,48,128,128]{3,2,1,0:T(8,128)S(1)}, s32[3,48,128,128]{3,2,1,0:T(8,128)}, u32[]{:S(2)}) %copy-start) | copy-done | bytes 9437208
  41.1 2.9 %dequant.3 = (bf16[64,128,256]{2,1,0:T(8,128)(2,1)S(1)}, bf16[64,128,128]{2,1,0:T(8,128)(2,1)S(1)}, s32[1]{0:T(128)}) custom-call(bf16[16,128,256]{2,1,0:T(8,128)(2,1)S(1)} %merge_c.1.refs_0_, s32[3,48,128,128]{3,2,1,0:T(8,128)S(1)} %copy-done, s32[3,48]{1,0:T(4,128)S(1)} %copy-done.4, s32[3]{0:T(128)S(1)} %copy-done.5, f32[3,3,48,128]{3,2,1,0:T(8,128)S(1)} %copy-done.1), custom_call_target="tpu_custom_call" | custom-call | flops 12000000 | bytes 10485760 | tf_op jit(solution)/shard_map/gather/dequant/pallas_call | solution.py:104
  44.1 0.6 collective-permute-start.17
  44.7 0.8 collective-permute-start.14
  45.5 6.2 %collective-permute-done.17.refs_3_ = bf16[4,256,128]{2,1,0:T(8,128)(2,1)S(1)} collective-permute-done((bf16[4,256,128]{2,1,0:T(8,128)(2,1)S(1)}, bf16[4,256,128]{2,1,0:T(8,128)(2,1)S(1)}, u32[]{:S(2)}, u32[]{:S(2)}) %collective-permute-start.17) | collective-permute-done | bytes 262176 | tf_op jit(solution)/shard_map/gather/ppermute | solution.py:29
  51.8 2.8 %collective-permute-done.14.refs_2_ = bf16[4,256,128]{2,1,0:T(8,128)(2,1)S(1)} collective-permute-done((bf16[4,256,128]{2,1,0:T(8,128)(2,1)S(1)}, bf16[4,256,128]{2,1,0:T(8,128)(2,1)S(1)}, u32[]{:S(2)}, u32[]{:S(2)}) %collective-permute-start.14) | collective-permute-done | bytes 262176 | tf_op jit(solution)/shard_map/gather/ppermute | solution.py:29
  54.6 0.3 collective-permute-start.20
  54.9 0.5 collective-permute-start.21
  55.4 0.6 part.1
  56.0 1.5 %collective-permute-start.10 = (bf16[8,128,256]{2,1,0:T(8,128)(2,1)S(1)}, bf16[8,128,256]{2,1,0:T(8,128)(2,1)S(1)}, u32[]{:S(2)}, u32[]{:S(2)}) collective-permute-start(bf16[8,128,256]{2,1,0:T(8,128)(2,1)S(1)} %part.1), channel_id=1, source_target_pairs={{0,16},{1,49},{2,18},{3,51},{4,20},{5,53},{6,22},{7,55},{8,24},{9,... | collective-permute-start | bytes 1572872 | tf_op jit(solution)/shard_map/gather/ppermute | solution.py:29
  57.5 3.7 %dequant.4 = (bf16[64,128,256]{2,1,0:T(8,128)(2,1)S(1)}, bf16[64,128,128]{2,1,0:T(8,128)(2,1)S(1)}, s32[1]{0:T(128)}) custom-call(bf16[16,128,256]{2,1,0:T(8,128)(2,1)S(1)} %merge_c.1.refs_0_, s32[3,48,128,128]{3,2,1,0:T(8,128)S(1)} %copy-done, s32[3,48]{1,0:T(4,128)S(1)} %copy-done.4, s32[3]{0:T(128)S(1)} %copy-done.5, f32[3,3,48,128]{3,2,1,0:T(8,128)S(1)} %copy-done.1), custom_call_target="tpu_custom_call" | custom-call | flops 12000000 | bytes 10485760 | tf_op jit(solution)/shard_map/gather/dequant/pallas_call | solution.py:104
  61.4 3.0 %dequant.5 = (bf16[64,128,256]{2,1,0:T(8,128)(2,1)S(1)}, bf16[64,128,128]{2,1,0:T(8,128)(2,1)S(1)}, s32[1]{0:T(128)}) custom-call(bf16[16,128,256]{2,1,0:T(8,128)(2,1)S(1)} %merge_c.1.refs_0_, s32[3,48,128,128]{3,2,1,0:T(8,128)S(1)} %copy-done, s32[3,48]{1,0:T(4,128)S(1)} %copy-done.4, s32[3]{0:T(128)S(1)} %copy-done.5, f32[3,3,48,128]{3,2,1,0:T(8,128)S(1)} %copy-done.1), custom_call_target="tpu_custom_call" | custom-call | flops 12000000 | bytes 10485760 | tf_op jit(solution)/shard_map/gather/dequant/pallas_call | solution.py:104
  64.4 4.5 %collective-permute-done.18.refs_3_.refs_1_ = bf16[4,256,128]{2,1,0:T(8,128)(2,1)S(1)} collective-permute-done((bf16[4,256,128]{2,1,0:T(8,128)(2,1)S(1)}, bf16[4,256,128]{2,1,0:T(8,128)(2,1)S(1)}, u32[]{:S(2)}, u32[]{:S(2)}) %collective-permute-start.18) | collective-permute-done | bytes 262176 | tf_op jit(solution)/shard_map/gather/ppermute | solution.py:29
  68.9 2.8 %collective-permute-done.15.refs_2_.refs_0_ = bf16[4,256,128]{2,1,0:T(8,128)(2,1)S(1)} collective-permute-done((bf16[4,256,128]{2,1,0:T(8,128)(2,1)S(1)}, bf16[4,256,128]{2,1,0:T(8,128)(2,1)S(1)}, u32[]{:S(2)}, u32[]{:S(2)}) %collective-permute-start.15) | collective-permute-done | bytes 262176 | tf_op jit(solution)/shard_map/gather/ppermute | solution.py:29
  71.7 1.1 pick.1
  73.1 0.5 collective-permute-start.11
  73.6 4.6 %gate_up.2 = (f32[3,256,256]{2,1,0:T(8,128)S(1)}, s32[1]{0:T(128)}) custom-call(s32[1]{0:T(128)} %get-tuple-element.50.refs_0_, s32[1]{0:T(128)} %get-tuple-element.51.refs_1_, s32[1]{0:T(128)} %get-tuple-element.43.refs_0_.refs_2_, s32[3]{0:T(128)S(1)} %pad_add_fusion.pos_ref.refs_1_.refs_3_, bf16[64,128,256]{2,1,0:T(8,128)(2,1)S(1)} %get-tuple-element.52.refs_4_.w0, ...), custom_call_target="tpu_custom_call" | custom-call | flops 2013265920 | bytes 15990800 | tf_op jit(solution)/shard_map/gather/gate_up/pallas_call | solution.py:49
  78.3 1.9 %hidden.2.refs_2_ = f32[384,256]{1,0:T(8,128)S(1)} custom-call(s32[3]{0:T(128)S(1)} %pad_add_fusion.pos_ref.refs_1_.refs_3_, bf16[64,128,128]{2,1,0:T(8,128)(2,1)S(1)} %get-tuple-element.40.w0, bf16[64,128,128]{2,1,0:T(8,128)(2,1)S(1)} %get-tuple-element.41.w1, bf16[64,128,128]{2,1,0:T(8,128)(2,1)S(1)} %get-tuple-element.42.w2, ...), custom_call_target="tpu_custom_call" | custom-call | flops 1207959552 | bytes 9830412 | tf_op jit(solution)/shard_map/gather/hidden/pallas_call | solution.py:49
  80.2 0.3 collective-permute-done.19.refs_2_
  80.8 1.3 collective-permute-done.23.refs_3_
  82.1 2.2 %gate_up.3 = (f32[3,256,256]{2,1,0:T(8,128)S(1)}, s32[1]{0:T(128)}) custom-call(s32[3]{0:T(128)S(1)} %pad_add_fusion.pos_ref.refs_1_.refs_3_, bf16[64,128,256]{2,1,0:T(8,128)(2,1)S(1)} %get-tuple-element.52.refs_4_.w0, bf16[64,128,256]{2,1,0:T(8,128)(2,1)S(1)} %get-tuple-element.53.refs_5_.w1, bf16[64,128,256]{2,1,0:T(8,128)(2,1)S(1)} %get-tuple-element.54.refs_6_.w2, ...), custom_call_target="tpu_custom_call" | custom-call | flops 1207959552 | bytes 15728656 | tf_op jit(solution)/shard_map/gather/gate_up/pallas_call | solution.py:49
  84.3 1.3 hidden.3
  85.6 1.5 %input_away.2 = bf16[16,128,256]{2,1,0:T(8,128)(2,1)S(1)} custom-call(s32[3]{0:T(128)S(1)} %pad_add_fusion.pos_ref.refs_1_.refs_3_, bf16[3,256,256]{2,1,0:T(8,128)(2,1)S(1)} %get-tuple-element.60.grad_ref, bf16[64,128,256]{2,1,0:T(8,128)(2,1)S(1)} %get-tuple-element.52.refs_4_.w0, bf16[64,128,256]{2,1,0:T(8,128)(2,1)S(1)} %get-tuple-element.53.refs_5_.w1, ...), custom_call_target="tpu_custom_call" | custom-call | flops 805306368 | bytes 14024716 | tf_op jit(solution)/shard_map/scatter/input_away/pallas_call | solution.py:49
  87.2 0.2 collective-permute-start.24
  87.4 1.5 %input_away.3 = bf16[16,128,256]{2,1,0:T(8,128)(2,1)S(1)} custom-call(s32[3]{0:T(128)S(1)} %pad_add_fusion.pos_ref.refs_1_.refs_3_, bf16[3,256,256]{2,1,0:T(8,128)(2,1)S(1)} %get-tuple-element.60.grad_ref, bf16[64,128,256]{2,1,0:T(8,128)(2,1)S(1)} %get-tuple-element.52.refs_4_.w0, bf16[64,128,256]{2,1,0:T(8,128)(2,1)S(1)} %get-tuple-element.53.refs_5_.w1, ...), custom_call_target="tpu_custom_call" | custom-call | flops 805306368 | bytes 14024716 | tf_op jit(solution)/shard_map/scatter/input_away/pallas_call | solution.py:49
  88.9 0.5 collective-permute-start.30
  89.4 0.5 collective-permute-done.24.refs_0_
  89.9 1.5 %input_here.2 = (bf16[4,128,256]{2,1,0:T(8,128)(2,1)S(1)}, bf16[4,128,256]{2,1,0:T(8,128)(2,1)S(1)}, f32[4,128,256]{2,1,0:T(8,128)S(1)}, f32[4,128,256]{2,1,0:T(8,128)S(1)}) custom-call(s32[3]{0:T(128)S(1)} %pad_add_fusion.pos_ref.refs_1_.refs_3_, bf16[3,256,256]{2,1,0:T(8,128)(2,1)S(1)} %get-tuple-element.60.grad_ref, ...), custom_call_target="tpu_custom_call" | custom-call | flops 805306368 | bytes 15597580 | tf_op jit(solution)/shard_map/scatter/input_here/pallas_call | solution.py:49
  91.7 1.5 %input_here.3 = (bf16[4,128,256]{2,1,0:T(8,128)(2,1)S(1)}, bf16[4,128,256]{2,1,0:T(8,128)(2,1)S(1)}, f32[4,128,256]{2,1,0:T(8,128)S(1)}, f32[4,128,256]{2,1,0:T(8,128)S(1)}) custom-call(s32[3]{0:T(128)S(1)} %pad_add_fusion.pos_ref.refs_1_.refs_3_, bf16[3,256,256]{2,1,0:T(8,128)(2,1)S(1)} %get-tuple-element.60.grad_ref, ...), custom_call_target="tpu_custom_call" | custom-call | flops 805306368 | bytes 15597580 | tf_op jit(solution)/shard_map/scatter/input_here/pallas_call | solution.py:49
  93.2 2.0 %collective-permute-start.32 = (bf16[4,128,256]{2,1,0:T(8,128)(2,1)S(1)}, bf16[4,128,256]{2,1,0:T(8,128)(2,1)S(1)}, u32[]{:S(2)}, u32[]{:S(2)}) collective-permute-start(bf16[4,128,256]{2,1,0:T(8,128)(2,1)S(1)} %get-tuple-element.70), channel_id=1, source_target_pairs={{0,48},{1,49},{2,50},{3,51},{4,52},{5,53},{6,54},{7,55},{8,56},{9,... | collective-permute-start | bytes 786440 | tf_op jit(solution)/shard_map/scatter/ppermute | solution.py:29
  95.1 1.4 collective-permute-start.31
  96.5 4.2 %collective-permute-done.25.r = bf16[4,128,256]{2,1,0:T(8,128)(2,1)S(1)} collective-permute-done((bf16[4,128,256]{2,1,0:T(8,128)(2,1)S(1)}, bf16[4,128,256]{2,1,0:T(8,128)(2,1)S(1)}, u32[]{:S(2)}, u32[]{:S(2)}) %collective-permute-start.25) | collective-permute-done | bytes 262176 | tf_op jit(solution)/shard_map/scatter/ppermute | solution.py:29
  100.7 1.4 collective-permute-start.26
  102.1 0.7 collective-permute-start.29
  102.8 0.2 collective-permute-done.32.r
  103.1 0.2 collective-permute-start.33
  103.4 1.6 %collective-permute-start.27 = (f32[384]{0:T(512)S(1)}, f32[384]{0:T(512)S(1)}, u32[]{:S(2)}, u32[]{:S(2)}) collective-permute-start(f32[384]{0:T(512)S(1)} %reduce), channel_id=1, source_target_pairs={{0,64},{64,0},{128,192},{192,128},{1,65},{65,1},{129,193},{193,129... | collective-permute-start | bytes 4616 | tf_op jit(solution)/shard_map/ia3/ppermute | solution.py:424
  104.9 2.1 %collective-permute-done.27 = f32[384]{0:T(512)S(1)} collective-permute-done((f32[384]{0:T(512)S(1)}, f32[384]{0:T(512)S(1)}, u32[]{:S(2)}, u32[]{:S(2)}) %collective-permute-start.27) | collective-permute-done | bytes 1568 | tf_op jit(solution)/shard_map/ia3/ppermute | solution.py:424
  107.0 2.8 %collective-permute-start.28 = (f32[384]{0:T(512)S(1)}, f32[384]{0:T(512)S(1)}, u32[]{:S(2)}, u32[]{:S(2)}) collective-permute-start(f32[384]{0:T(512)S(1)} %add.10), channel_id=1, source_target_pairs={{0,192},{192,0},{64,128},{128,64},{1,193},{193,1},{65,129},{129,65... | collective-permute-start | bytes 4616 | tf_op jit(solution)/shard_map/ia3/ppermute | solution.py:425
  109.8 2.0 %collective-permute-done.28 = f32[384]{0:T(512)S(1)} collective-permute-done((f32[384]{0:T(512)S(1)}, f32[384]{0:T(512)S(1)}, u32[]{:S(2)}, u32[]{:S(2)}) %collective-permute-start.28) | collective-permute-done | bytes 1568 | tf_op jit(solution)/shard_map/ia3/ppermute | solution.py:425
  111.8 0.6 add.11
  112.5 3.3 %collective-permute-done.33.rb3 = bf16[4,128,256]{2,1,0:T(8,128)(2,1)S(1)} collective-permute-done((bf16[4,128,256]{2,1,0:T(8,128)(2,1)S(1)}, bf16[4,128,256]{2,1,0:T(8,128)(2,1)S(1)}, u32[]{:S(2)}, u32[]{:S(2)}) %collective-permute-start.33) | collective-permute-done | bytes 262176 | tf_op jit(solution)/shard_map/scatter/ppermute | solution.py:29
  115.8 0.7 y_sum.1
  116.5 20.2 %all_to_all.5.parts = bf16[8,128,256]{2,1,0:T(8,128)(2,1)S(1)} all-to-all(bf16[8,128,256]{2,1,0:T(8,128)(2,1)S(1)} %y_sum.1), channel_id=1, replica_groups={{0,2,4,6,8,10,12,14},{1,3,5,7,9,11,13,15},{16,18,20,22,24,26,28,30},{17..., dimensions={0} | all-to-all | bytes 1048576 | tf_op jit(solution)/shard_map/scatter/all_to_all | solution.py:443
  136.7 0.8 z_sum.1
  (48 shorter events, 1.7 us)
Async XLA Ops:
  0.6 36.8 %copy-start.1 = (f32[3,3,48,128]{3,2,1,0:T(8,128)S(1)}, f32[3,3,48,128]{3,2,1,0:T(8,128)}, u32[]{:S(2)}) copy-start(f32[3,3,48,128]{3,2,1,0:T(8,128)} %refs_4_.5) | copy-start | bytes 663556
  0.6 1.7 %collective-permute-start = (bf16[256,128]{1,0:T(8,128)(2,1)}, bf16[256,128]{1,0:T(8,128)(2,1)S(1)}, u32[]{:S(2)}, u32[]{:S(2)}) collective-permute-start(bf16[256,128]{1,0:T(8,128)(2,1)} %tok.1), channel_id=1, source_target_pairs={{0,1},{1,0},{2,3},{3,2},{4,5},{5,4},{6,7},{7,6},{8,9},{9,8},{10,11... | collective-permute-start | bytes 196616 | tf_op jit(solution)/shard_map/gather/ppermute | solution.py:29
  0.7 17.0 %collective-permute-start.3 = (bf16[256,128]{1,0:T(8,128)(2,1)}, bf16[256,128]{1,0:T(8,128)(2,1)S(1)}, u32[]{:S(2)}, u32[]{:S(2)}) collective-permute-start(bf16[256,128]{1,0:T(8,128)(2,1)} %tok.1), channel_id=1, source_target_pairs={{0,32},{1,33},{2,34},{3,35},{4,36},{5,37},{6,38},{7,39},{8,40},{9,... | collective-permute-start | bytes 196616 | tf_op jit(solution)/shard_map/gather/ppermute | solution.py:29
  2.1 1.5 %collective-permute-start.1 = (bf16[256,128]{1,0:T(8,128)(2,1)}, bf16[256,128]{1,0:T(8,128)(2,1)S(1)}, u32[]{:S(2)}, u32[]{:S(2)}) collective-permute-start(bf16[256,128]{1,0:T(8,128)(2,1)} %cot.1), channel_id=1, source_target_pairs={{0,1},{1,0},{2,3},{3,2},{4,5},{5,4},{6,7},{7,6},{8,9},{9,8},{10,11... | collective-permute-start | bytes 196616 | tf_op jit(solution)/shard_map/gather/ppermute | solution.py:29
  3.5 0.8 copy-start.2
  4.4 0.8 copy-start.3
  5.2 32.2 %copy-start.4 = (s32[3,48]{1,0:T(4,128)S(1)}, s32[3,48]{1,0:T(4,128)}, u32[]{:S(2)}) copy-start(s32[3,48]{1,0:T(4,128)} %refs_2_.5) | copy-start | bytes 1732
  5.2 32.2 %copy-start.5 = (s32[3]{0:T(128)S(1)}, s32[3]{0:T(128)}, u32[]{:S(2)}) copy-start(s32[3]{0:T(128)} %refs_3_.5) | copy-start | bytes 40
  6.3 12.0 %collective-permute-start.2 = (bf16[2,256,128]{2,1,0:T(8,128)(2,1)S(1)}, bf16[2,256,128]{2,1,0:T(8,128)(2,1)S(1)}, u32[]{:S(2)}, u32[]{:S(2)}) collective-permute-start(bf16[2,256,128]{2,1,0:T(8,128)(2,1)S(1)} %get-tuple-element.38.chip), channel_id=1, source_target_pairs={{0,16},{1,49},{2,18},{3,51},{4,20},{5,53},{6,22},{7,55},{8,24},{9,... | collective-permute-start | bytes 393224 | tf_op jit(solution)/shard_map/gather/ppermute | solution.py:29
  8.6 18.8 %collective-permute-start.4 = (bf16[2,128,256]{2,1,0:T(8,128)(2,1)S(1)}, bf16[2,128,256]{2,1,0:T(8,128)(2,1)S(1)}, u32[]{:S(2)}, u32[]{:S(2)}) collective-permute-start(bf16[2,128,256]{2,1,0:T(8,128)(2,1)S(1)} %get-tuple-element.37.chip), channel_id=1, source_target_pairs={{0,2},{1,15},{2,4},{3,1},{4,6},{5,3},{6,8},{7,5},{8,10},{9,7},{10,... | collective-permute-start | bytes 393224 | tf_op jit(solution)/shard_map/gather/ppermute | solution.py:29
  10.5 16.9 %collective-permute-start.5 = (bf16[2,128,256]{2,1,0:T(8,128)(2,1)S(1)}, bf16[2,128,256]{2,1,0:T(8,128)(2,1)S(1)}, u32[]{:S(2)}, u32[]{:S(2)}) collective-permute-start(bf16[2,128,256]{2,1,0:T(8,128)(2,1)S(1)} %get-tuple-element.37.chip), channel_id=1, source_target_pairs={{0,4},{1,13},{2,6},{3,15},{4,8},{5,1},{6,10},{7,3},{8,12},{9,5},{1... | collective-permute-start | bytes 393224 | tf_op jit(solution)/shard_map/gather/ppermute | solution.py:29
  13.7 14.2 %collective-permute-start.6 = (bf16[2,128,256]{2,1,0:T(8,128)(2,1)S(1)}, bf16[2,128,256]{2,1,0:T(8,128)(2,1)S(1)}, u32[]{:S(2)}, u32[]{:S(2)}) collective-permute-start(bf16[2,128,256]{2,1,0:T(8,128)(2,1)S(1)} %get-tuple-element.37.chip), channel_id=1, source_target_pairs={{0,6},{1,11},{2,8},{3,13},{4,10},{5,15},{6,12},{7,1},{8,14},{9,3},... | collective-permute-start | bytes 393224 | tf_op jit(solution)/shard_map/gather/ppermute | solution.py:29
  17.8 9.6 %collective-permute-start.7 = (bf16[128,256]{1,0:T(8,128)(2,1)S(1)}, bf16[128,256]{1,0:T(8,128)(2,1)S(1)}, u32[]{:S(2)}, u32[]{:S(2)}) collective-permute-start(bf16[128,256]{1,0:T(8,128)(2,1)S(1)} %get-tuple-element.39), channel_id=1, source_target_pairs={{0,8},{1,9},{2,10},{3,11},{4,12},{5,13},{6,14},{7,15},{8,0},{9,1},... | collective-permute-start | bytes 196616 | tf_op jit(solution)/shard_map/gather/ppermute | solution.py:29
  28.0 1.9 %collective-permute-start.8 = (bf16[7,128,256]{2,1,0:T(8,128)(2,1)S(1)}, bf16[7,128,256]{2,1,0:T(8,128)(2,1)S(1)}, u32[]{:S(2)}, u32[]{:S(2)}) collective-permute-start(bf16[7,128,256]{2,1,0:T(8,128)(2,1)S(1)} %stack.21.mine), channel_id=1, source_target_pairs={{0,1},{1,0},{2,3},{3,2},{4,5},{5,4},{6,7},{7,6},{8,9},{9,8},{10,11... | collective-permute-start | bytes 1376264 | tf_op jit(solution)/shard_map/gather/ppermute | solution.py:29
  30.5 24.4 %collective-permute-start.9 = (bf16[16,128,256]{2,1,0:T(8,128)(2,1)S(1)}, bf16[16,128,256]{2,1,0:T(8,128)(2,1)S(1)}, u32[]{:S(2)}, u32[]{:S(2)}) collective-permute-start(bf16[16,128,256]{2,1,0:T(8,128)(2,1)S(1)} %merge_c.1.refs_0_), channel_id=1, source_target_pairs={{0,16},{1,49},{2,18},{3,51},{4,20},{5,53},{6,22},{7,55},{8,24},{9,... | collective-permute-start | bytes 3145736 | tf_op jit(solution)/shard_map/gather/ppermute | solution.py:29
  31.7 1.4 %collective-permute-start.12 = (bf16[3,256,128]{2,1,0:T(8,128)(2,1)S(1)}, bf16[3,256,128]{2,1,0:T(8,128)(2,1)S(1)}, u32[]{:S(2)}, u32[]{:S(2)}) collective-permute-start(bf16[3,256,128]{2,1,0:T(8,128)(2,1)S(1)} %stack.20.refs_0_.mine), channel_id=1, source_target_pairs={{0,1},{1,0},{2,3},{3,2},{4,5},{5,4},{6,7},{7,6},{8,9},{9,8},{10,11... | collective-permute-start | bytes 589832 | tf_op jit(solution)/shard_map/gather/ppermute | solution.py:29
  33.7 10.4 %collective-permute-start.16 = (bf16[4,256,128]{2,1,0:T(8,128)(2,1)S(1)}, bf16[4,256,128]{2,1,0:T(8,128)(2,1)S(1)}, u32[]{:S(2)}, u32[]{:S(2)}) collective-permute-start(bf16[4,256,128]{2,1,0:T(8,128)(2,1)S(1)} %get-tuple-element.45.refs_8_), channel_id=1, source_target_pairs={{0,2},{1,15},{2,4},{3,1},{4,6},{5,3},{6,8},{7,5},{8,10},{9,7},{10,... | collective-permute-start | bytes 786440 | tf_op jit(solution)/shard_map/gather/ppermute | solution.py:29
  35.4 9.4 %collective-permute-start.13 = (bf16[4,256,128]{2,1,0:T(8,128)(2,1)S(1)}, bf16[4,256,128]{2,1,0:T(8,128)(2,1)S(1)}, u32[]{:S(2)}, u32[]{:S(2)}) collective-permute-start(bf16[4,256,128]{2,1,0:T(8,128)(2,1)S(1)} %get-tuple-element.44.refs_7_), channel_id=1, source_target_pairs={{0,2},{1,15},{2,4},{3,1},{4,6},{5,3},{6,8},{7,5},{8,10},{9,7},{10,... | collective-permute-start | bytes 786440 | tf_op jit(solution)/shard_map/gather/ppermute | solution.py:29
  37.5 3.7 %copy-start = (s32[3,48,128,128]{3,2,1,0:T(8,128)S(1)}, s32[3,48,128,128]{3,2,1,0:T(8,128)}, u32[]{:S(2)}) copy-start(s32[3,48,128,128]{3,2,1,0:T(8,128)} %refs_1_.5) | copy-start | bytes 28311556
  44.1 7.7 %collective-permute-start.17 = (bf16[4,256,128]{2,1,0:T(8,128)(2,1)S(1)}, bf16[4,256,128]{2,1,0:T(8,128)(2,1)S(1)}, u32[]{:S(2)}, u32[]{:S(2)}) collective-permute-start(bf16[4,256,128]{2,1,0:T(8,128)(2,1)S(1)} %collective-permute-done.16.refs_1_), channel_id=1, source_target_pairs={{0,2},{1,15},{2,4},{3,1},{4,6},{5,3},{6,8},{7,5},{8,10},{9,7},{10,... | collective-permute-start | bytes 786440 | tf_op jit(solution)/shard_map/gather/ppermute | solution.py:29
  44.7 9.9 %collective-permute-start.14 = (bf16[4,256,128]{2,1,0:T(8,128)(2,1)S(1)}, bf16[4,256,128]{2,1,0:T(8,128)(2,1)S(1)}, u32[]{:S(2)}, u32[]{:S(2)}) collective-permute-start(bf16[4,256,128]{2,1,0:T(8,128)(2,1)S(1)} %collective-permute-done.13.refs_0_), channel_id=1, source_target_pairs={{0,2},{1,15},{2,4},{3,1},{4,6},{5,3},{6,8},{7,5},{8,10},{9,7},{10,... | collective-permute-start | bytes 786440 | tf_op jit(solution)/shard_map/gather/ppermute | solution.py:29
  54.6 18.9 %collective-permute-start.20 = (bf16[16,256,128]{2,1,0:T(8,128)(2,1)S(1)}, bf16[16,256,128]{2,1,0:T(8,128)(2,1)S(1)}, u32[]{:S(2)}, u32[]{:S(2)}) collective-permute-start(bf16[16,256,128]{2,1,0:T(8,128)(2,1)S(1)} %stack.22.refs_9_), channel_id=1, source_target_pairs={{0,1},{1,0},{2,3},{3,2},{4,5},{5,4},{6,7},{7,6},{8,9},{9,8},{10,11... | collective-permute-start | bytes 3145736 | tf_op jit(solution)/shard_map/gather/ppermute | solution.py:29
  54.9 23.3 %collective-permute-start.21 = (bf16[16,128,256]{2,1,0:T(8,128)(2,1)S(1)}, bf16[16,128,256]{2,1,0:T(8,128)(2,1)S(1)}, u32[]{:S(2)}, u32[]{:S(2)}) collective-permute-start(bf16[16,128,256]{2,1,0:T(8,128)(2,1)S(1)} %collective-permute-done.9.a.refs_1_), channel_id=1, source_target_pairs={{0,1},{1,0},{2,3},{3,2},{4,5},{5,4},{6,7},{7,6},{8,9},{9,8},{10,11... | collective-permute-start | bytes 3145736 | tf_op jit(solution)/shard_map/gather/ppermute | solution.py:29
  56.0 17.1 %collective-permute-start.10 = (bf16[8,128,256]{2,1,0:T(8,128)(2,1)S(1)}, bf16[8,128,256]{2,1,0:T(8,128)(2,1)S(1)}, u32[]{:S(2)}, u32[]{:S(2)}) collective-permute-start(bf16[8,128,256]{2,1,0:T(8,128)(2,1)S(1)} %part.1), channel_id=1, source_target_pairs={{0,16},{1,49},{2,18},{3,51},{4,20},{5,53},{6,22},{7,55},{8,24},{9,... | collective-permute-start | bytes 1572872 | tf_op jit(solution)/shard_map/gather/ppermute | solution.py:29
  61.3 7.7 %collective-permute-start.18 = (bf16[4,256,128]{2,1,0:T(8,128)(2,1)S(1)}, bf16[4,256,128]{2,1,0:T(8,128)(2,1)S(1)}, u32[]{:S(2)}, u32[]{:S(2)}) collective-permute-start(bf16[4,256,128]{2,1,0:T(8,128)(2,1)S(1)} %collective-permute-done.17.refs_3_), channel_id=1, source_target_pairs={{0,2},{1,15},{2,4},{3,1},{4,6},{5,3},{6,8},{7,5},{8,10},{9,7},{10,... | collective-permute-start | bytes 786440 | tf_op jit(solution)/shard_map/gather/ppermute | solution.py:29
  61.3 10.4 %collective-permute-start.15 = (bf16[4,256,128]{2,1,0:T(8,128)(2,1)S(1)}, bf16[4,256,128]{2,1,0:T(8,128)(2,1)S(1)}, u32[]{:S(2)}, u32[]{:S(2)}) collective-permute-start(bf16[4,256,128]{2,1,0:T(8,128)(2,1)S(1)} %collective-permute-done.14.refs_2_), channel_id=1, source_target_pairs={{0,2},{1,15},{2,4},{3,1},{4,6},{5,3},{6,8},{7,5},{8,10},{9,7},{10,... | collective-permute-start | bytes 786440 | tf_op jit(solution)/shard_map/gather/ppermute | solution.py:29
  72.9 7.7 %collective-permute-start.19 = (bf16[4,256,128]{2,1,0:T(8,128)(2,1)S(1)}, bf16[4,256,128]{2,1,0:T(8,128)(2,1)S(1)}, u32[]{:S(2)}, u32[]{:S(2)}) collective-permute-start(bf16[4,256,128]{2,1,0:T(8,128)(2,1)S(1)} %pick.1), channel_id=1, source_target_pairs={{0,2},{1,15},{2,4},{3,1},{4,6},{5,3},{6,8},{7,5},{8,10},{9,7},{10,... | collective-permute-start | bytes 786440 | tf_op jit(solution)/shard_map/gather/ppermute | solution.py:29
  73.0 7.8 %collective-permute-start.22 = (bf16[8,256,128]{2,1,0:T(8,128)(2,1)S(1)}, bf16[8,256,128]{2,1,0:T(8,128)(2,1)S(1)}, u32[]{:S(2)}, u32[]{:S(2)}) collective-permute-start(bf16[8,256,128]{2,1,0:T(8,128)(2,1)S(1)} %stack.23.refs_0_), channel_id=1, source_target_pairs={{0,1},{1,0},{2,3},{3,2},{4,5},{5,4},{6,7},{7,6},{8,9},{9,8},{10,11... | collective-permute-start | bytes 1572872 | tf_op jit(solution)/shard_map/gather/ppermute | solution.py:29
  73.1 11.2 %collective-permute-start.11 = (bf16[8,128,256]{2,1,0:T(8,128)(2,1)S(1)}, bf16[8,128,256]{2,1,0:T(8,128)(2,1)S(1)}, u32[]{:S(2)}, u32[]{:S(2)}) collective-permute-start(bf16[8,128,256]{2,1,0:T(8,128)(2,1)S(1)} %collective-permute-done.10.refs_0_), channel_id=1, source_target_pairs={{0,1},{1,0},{2,3},{3,2},{4,5},{5,4},{6,7},{7,6},{8,9},{9,8},{10,11... | collective-permute-start | bytes 1572872 | tf_op jit(solution)/shard_map/gather/ppermute | solution.py:29
  78.2 2.4 %copy-start.6 = (f32[384]{0:T(512)S(1)}, f32[384]{0:T(512)}, u32[]{:S(2)}) copy-start(f32[384]{0:T(512)} %param.13) | copy-start | bytes 4612
  80.5 1.6 %collective-permute-start.23 = (bf16[4,256,128]{2,1,0:T(8,128)(2,1)S(1)}, bf16[4,256,128]{2,1,0:T(8,128)(2,1)S(1)}, u32[]{:S(2)}, u32[]{:S(2)}) collective-permute-start(bf16[4,256,128]{2,1,0:T(8,128)(2,1)S(1)} %collective-permute-done.19.refs_2_), channel_id=1, source_target_pairs={{0,1},{1,0},{2,3},{3,2},{4,5},{5,4},{6,7},{7,6},{8,9},{9,8},{10,11... | collective-permute-start | bytes 786440 | tf_op jit(solution)/shard_map/gather/ppermute | solution.py:29
  87.2 2.7 %collective-permute-start.24 = (bf16[16,128,256]{2,1,0:T(8,128)(2,1)S(1)}, bf16[16,128,256]{2,1,0:T(8,128)(2,1)S(1)}, u32[]{:S(2)}, u32[]{:S(2)}) collective-permute-start(bf16[16,128,256]{2,1,0:T(8,128)(2,1)S(1)} %input_away.2), channel_id=1, source_target_pairs={{0,1},{1,0},{2,3},{3,2},{4,5},{5,4},{6,7},{7,6},{8,9},{9,8},{10,11... | collective-permute-start | bytes 3145736 | tf_op jit(solution)/shard_map/scatter/ppermute | solution.py:29
  88.9 2.7 %collective-permute-start.30 = (bf16[16,128,256]{2,1,0:T(8,128)(2,1)S(1)}, bf16[16,128,256]{2,1,0:T(8,128)(2,1)S(1)}, u32[]{:S(2)}, u32[]{:S(2)}) collective-permute-start(bf16[16,128,256]{2,1,0:T(8,128)(2,1)S(1)} %input_away.3), channel_id=1, source_target_pairs={{0,1},{1,0},{2,3},{3,2},{4,5},{5,4},{6,7},{7,6},{8,9},{9,8},{10,11... | collective-permute-start | bytes 3145736 | tf_op jit(solution)/shard_map/scatter/ppermute | solution.py:29
  91.4 9.2 %collective-permute-start.25 = (bf16[4,128,256]{2,1,0:T(8,128)(2,1)S(1)}, bf16[4,128,256]{2,1,0:T(8,128)(2,1)S(1)}, u32[]{:S(2)}, u32[]{:S(2)}) collective-permute-start(bf16[4,128,256]{2,1,0:T(8,128)(2,1)S(1)} %get-tuple-element.63), channel_id=1, source_target_pairs={{0,16},{1,17},{2,18},{3,19},{4,20},{5,21},{6,22},{7,23},{8,24},{9,... | collective-permute-start | bytes 786440 | tf_op jit(solution)/shard_map/scatter/ppermute | solution.py:29
  93.2 9.9 %collective-permute-start.32 = (bf16[4,128,256]{2,1,0:T(8,128)(2,1)S(1)}, bf16[4,128,256]{2,1,0:T(8,128)(2,1)S(1)}, u32[]{:S(2)}, u32[]{:S(2)}) collective-permute-start(bf16[4,128,256]{2,1,0:T(8,128)(2,1)S(1)} %get-tuple-element.70), channel_id=1, source_target_pairs={{0,48},{1,49},{2,50},{3,51},{4,52},{5,53},{6,54},{7,55},{8,56},{9,... | collective-permute-start | bytes 786440 | tf_op jit(solution)/shard_map/scatter/ppermute | solution.py:29
  95.1 17.3 %collective-permute-start.31 = (bf16[4,128,256]{2,1,0:T(8,128)(2,1)S(1)}, bf16[4,128,256]{2,1,0:T(8,128)(2,1)S(1)}, u32[]{:S(2)}, u32[]{:S(2)}) collective-permute-start(bf16[4,128,256]{2,1,0:T(8,128)(2,1)S(1)} %get-tuple-element.68), channel_id=1, source_target_pairs={{0,16},{1,17},{2,18},{3,19},{4,20},{5,21},{6,22},{7,23},{8,24},{9,... | collective-permute-start | bytes 786440 | tf_op jit(solution)/shard_map/scatter/ppermute | solution.py:29
  100.7 11.7 %collective-permute-start.26 = (bf16[4,128,256]{2,1,0:T(8,128)(2,1)S(1)}, bf16[4,128,256]{2,1,0:T(8,128)(2,1)S(1)}, u32[]{:S(2)}, u32[]{:S(2)}) collective-permute-start(bf16[4,128,256]{2,1,0:T(8,128)(2,1)S(1)} %add.17), channel_id=1, source_target_pairs={{0,16},{1,17},{2,18},{3,19},{4,20},{5,21},{6,22},{7,23},{8,24},{9,... | collective-permute-start | bytes 786440 | tf_op jit(solution)/shard_map/scatter/ppermute | solution.py:29
  102.1 10.5 %collective-permute-start.29 = (bf16[4,128,256]{2,1,0:T(8,128)(2,1)S(1)}, bf16[4,128,256]{2,1,0:T(8,128)(2,1)S(1)}, u32[]{:S(2)}, u32[]{:S(2)}) collective-permute-start(bf16[4,128,256]{2,1,0:T(8,128)(2,1)S(1)} %get-tuple-element.66), channel_id=1, source_target_pairs={{0,48},{1,49},{2,50},{3,51},{4,52},{5,53},{6,54},{7,55},{8,56},{9,... | collective-permute-start | bytes 786440 | tf_op jit(solution)/shard_map/scatter/ppermute | solution.py:29
  103.1 12.7 %collective-permute-start.33 = (bf16[4,128,256]{2,1,0:T(8,128)(2,1)S(1)}, bf16[4,128,256]{2,1,0:T(8,128)(2,1)S(1)}, u32[]{:S(2)}, u32[]{:S(2)}) collective-permute-start(bf16[4,128,256]{2,1,0:T(8,128)(2,1)S(1)} %add.18), channel_id=1, source_target_pairs={{0,48},{1,49},{2,50},{3,51},{4,52},{5,53},{6,54},{7,55},{8,56},{9,... | collective-permute-start | bytes 786440 | tf_op jit(solution)/shard_map/scatter/ppermute | solution.py:29
  103.4 3.7 %collective-permute-start.27 = (f32[384]{0:T(512)S(1)}, f32[384]{0:T(512)S(1)}, u32[]{:S(2)}, u32[]{:S(2)}) collective-permute-start(f32[384]{0:T(512)S(1)} %reduce), channel_id=1, source_target_pairs={{0,64},{64,0},{128,192},{192,128},{1,65},{65,1},{129,193},{193,129... | collective-permute-start | bytes 4616 | tf_op jit(solution)/shard_map/ia3/ppermute | solution.py:424
  107.0 4.8 %collective-permute-start.28 = (f32[384]{0:T(512)S(1)}, f32[384]{0:T(512)S(1)}, u32[]{:S(2)}, u32[]{:S(2)}) collective-permute-start(f32[384]{0:T(512)S(1)} %add.10), channel_id=1, source_target_pairs={{0,192},{192,0},{64,128},{128,64},{1,193},{193,1},{65,129},{129,65... | collective-permute-start | bytes 4616 | tf_op jit(solution)/shard_map/ia3/ppermute | solution.py:425
where the time goes:
time: 138 us; the launch traced here: 137 us
  waiting for transfers between devices  44.6 us (32%)
  starting transfers between devices  34.1 us (25%)
  Pallas kernels  31.5 us (23%)
  blocking collectives  20.2 us (15%)
  local copies, waits for them, and re-layouts  5.48 us (4%)
    ppermute x32, waiting for transfers between devices, send(): return lax.ppermute(a, 'mp', pairs)  40.5 us
    ppermute x32, starting transfers between devices, send(): return lax.ppermute(a, 'mp', pairs)  29.8 us
    pallas_call x20, Pallas kernels, call(): pl.pallas_call((lambda *refs: kernel(*refs[skip:])) if skip else kernel,...  20.8 us
    all_to_all x1, blocking collectives, on_device(): lax.all_to_all(total, 'mp', 0, 0, axis_index_groups=columns, tiled=True)  20.2 us
    pallas_call x3, Pallas kernels, dequant(): pl.pallas_call((lambda *refs: kernel(*refs[skip:])) if skip else kernel,...  9.63 us
    unnamed x14, local copies, waits for them, and re-layouts  5.37 us
    ppermute x1, starting transfers between devices, on_device(): lax.ppermute(ia3_part, 'dp', [(0, 3), (3, 0), (1, 2), (2, 1)])  2.77 us
  transfers between devices with their start and end apart: 34, of which 18 were waited for; matrix products, arithmetic and copies ran while one was open for 1% of the time, Pallas kernels for 19%

commit v1 on v0

--- a/solution.py
+++ b/solution.py
@@ -375,8 +375,8 @@
 
         f0, f1, steps = t0, t1, []
         for i in range(3):
-            if i:
-                f1, ready[i - 1] = lax.optimization_barrier((f1, ready[i - 1]))
+            if i == 1:
+                f1, ready[0] = lax.optimization_barrier((f1, ready[0]))
             f0 = send(f0, dz=1, signed=True)
             f1 = send(f1, dz=1, signed=True)
             steps.append((f0, f1))
@@ -405,7 +405,7 @@
             lambda s: chosen(-s),
         ]
         (part,) = hidden(pos, w_down, c_pieces[:3], c_places[:3])
-        f4 = send(pick(pos, f0, f1, after=(ready[2],)), dz=1, signed=True)
+        f4 = send(pick(pos, f0, f1, after=(ready[1], ready[2])), dz=1, signed=True)
         f4, gu, part = lax.optimization_barrier((f4, gu, part))
         mine = stack(steps[2])
         t_pieces = [mine, swap(mine), f4, swap(f4)]

time: 138 us -> 135 us (0.978)
  waiting for transfers between devices: 44.6 us -> 41.8 us
    ppermute x32, waiting for transfers between devices: 40.5 us -> 37.7 us  [send(): return lax.ppermute(a, 'mp', pairs)]
  transfers between devices with their start and end apart: 34 -> 34, of which waited for: 18 -> 17; matrix products, arithmetic and copies ran while one was open for 1% -> 1% of each run, Pallas kernels for 19% -> 20%
where the time goes in v1:
time: 135 us
  waiting for transfers between devices  41.8 us (31%)
  starting transfers between devices  33.4 us (25%)
  Pallas kernels  32.4 us (24%)
  blocking collectives  19.8 us (15%)
  local copies, waits for them, and re-layouts  5.48 us (4%)
    ppermute x32, waiting for transfers between devices, send(): return lax.ppermute(a, 'mp', pairs)  37.7 us
    ppermute x32, starting transfers between devices, send(): return lax.ppermute(a, 'mp', pairs)  29 us
    pallas_call x20, Pallas kernels, call(): pl.pallas_call((lambda *refs: kernel(*refs[skip:])) if skip else kernel,...  21.4 us
    all_to_all x1, blocking collectives, on_device(): lax.all_to_all(total, 'mp', 0, 0, axis_index_groups=columns, tiled=True)  19.8 us
    pallas_call x3, Pallas kernels, dequant(): pl.pallas_call((lambda *refs: kernel(*refs[skip:])) if skip else kernel,...  9.92 us
    unnamed x14, local copies, waits for them, and re-layouts  5.37 us
    ppermute x1, starting transfers between devices, on_device(): lax.ppermute(ia3_part, 'dp', [(0, 3), (3, 0), (1, 2), (2, 1)])  2.77 us
  transfers between devices with their start and end apart: 34, of which 17 were waited for; matrix products, arithmetic and copies ran while one was open for 1% of the time, Pallas kernels for 20%

profile of v1, /device:TPU:24, one launch (start us, length us, event | category | flops | bytes accessed | tf_op | source)
XLA Modules:
  0.0 134.5 jit_solution(12226777555572861608)
XLA Ops:
  0.7 1.3 collective-permute-start.3
  2.3 1.2 collective-permute-done.1.sib_c
  3.5 0.8 copy-done.2
  4.4 0.8 copy-done.3
  5.2 1.1 own.1
  6.3 2.3 %collective-permute-start.2 = (bf16[2,256,128]{2,1,0:T(8,128)(2,1)S(1)}, bf16[2,256,128]{2,1,0:T(8,128)(2,1)S(1)}, u32[]{:S(2)}, u32[]{:S(2)}) collective-permute-start(bf16[2,256,128]{2,1,0:T(8,128)(2,1)S(1)} %get-tuple-element.36.chip), channel_id=1, source_target_pairs={{0,16},{1,49},{2,18},{3,51},{4,20},{5,53},{6,22},{7,55},{8,24},{9,... | collective-permute-start | bytes 393224 | tf_op jit(solution)/shard_map/gather/ppermute | solution.py:29
  8.6 1.9 %collective-permute-start.4 = (bf16[2,128,256]{2,1,0:T(8,128)(2,1)S(1)}, bf16[2,128,256]{2,1,0:T(8,128)(2,1)S(1)}, u32[]{:S(2)}, u32[]{:S(2)}) collective-permute-start(bf16[2,128,256]{2,1,0:T(8,128)(2,1)S(1)} %get-tuple-element.35.chip), channel_id=1, source_target_pairs={{0,2},{1,15},{2,4},{3,1},{4,6},{5,3},{6,8},{7,5},{8,10},{9,7},{10,... | collective-permute-start | bytes 393224 | tf_op jit(solution)/shard_map/gather/ppermute | solution.py:29
  10.5 3.3 %collective-permute-start.5 = (bf16[2,128,256]{2,1,0:T(8,128)(2,1)S(1)}, bf16[2,128,256]{2,1,0:T(8,128)(2,1)S(1)}, u32[]{:S(2)}, u32[]{:S(2)}) collective-permute-start(bf16[2,128,256]{2,1,0:T(8,128)(2,1)S(1)} %get-tuple-element.35.chip), channel_id=1, source_target_pairs={{0,4},{1,13},{2,6},{3,15},{4,8},{5,1},{6,10},{7,3},{8,12},{9,5},{1... | collective-permute-start | bytes 393224 | tf_op jit(solution)/shard_map/gather/ppermute | solution.py:29
  13.7 4.0 %collective-permute-start.6 = (bf16[2,128,256]{2,1,0:T(8,128)(2,1)S(1)}, bf16[2,128,256]{2,1,0:T(8,128)(2,1)S(1)}, u32[]{:S(2)}, u32[]{:S(2)}) collective-permute-start(bf16[2,128,256]{2,1,0:T(8,128)(2,1)S(1)} %get-tuple-element.35.chip), channel_id=1, source_target_pairs={{0,6},{1,11},{2,8},{3,13},{4,10},{5,15},{6,12},{7,1},{8,14},{9,3},... | collective-permute-start | bytes 393224 | tf_op jit(solution)/shard_map/gather/ppermute | solution.py:29
  17.8 0.5 collective-permute-start.7
  18.3 9.0 %collective-permute-done.7.refs_4_ = bf16[128,256]{1,0:T(8,128)(2,1)S(1)} collective-permute-done((bf16[128,256]{1,0:T(8,128)(2,1)S(1)}, bf16[128,256]{1,0:T(8,128)(2,1)S(1)}, u32[]{:S(2)}, u32[]{:S(2)}) %collective-permute-start.7) | collective-permute-done | bytes 65568 | tf_op jit(solution)/shard_map/gather/ppermute | solution.py:29
  27.4 0.6 collective-permute-done.6.refs_3_
  28.1 1.8 %collective-permute-done.8.other = bf16[7,128,256]{2,1,0:T(8,128)(2,1)S(1)} collective-permute-done((bf16[7,128,256]{2,1,0:T(8,128)(2,1)S(1)}, bf16[7,128,256]{2,1,0:T(8,128)(2,1)S(1)}, u32[]{:S(2)}, u32[]{:S(2)}) %collective-permute-start.8) | collective-permute-done | bytes 458784 | tf_op jit(solution)/shard_map/gather/ppermute | solution.py:29
  29.9 0.6 merge_c.1.refs_0_
  30.5 1.2 collective-permute-start.9
  31.7 1.4 %collective-permute-done.12.other = bf16[3,256,128]{2,1,0:T(8,128)(2,1)S(1)} collective-permute-done((bf16[3,256,128]{2,1,0:T(8,128)(2,1)S(1)}, bf16[3,256,128]{2,1,0:T(8,128)(2,1)S(1)}, u32[]{:S(2)}, u32[]{:S(2)}) %collective-permute-start.12) | collective-permute-done | bytes 196640 | tf_op jit(solution)/shard_map/gather/ppermute | solution.py:29
  33.1 0.6 merge_t.1
  33.7 1.6 %collective-permute-start.16 = (bf16[4,256,128]{2,1,0:T(8,128)(2,1)S(1)}, bf16[4,256,128]{2,1,0:T(8,128)(2,1)S(1)}, u32[]{:S(2)}, u32[]{:S(2)}) collective-permute-start(bf16[4,256,128]{2,1,0:T(8,128)(2,1)S(1)} %get-tuple-element.44.refs_8_), channel_id=1, source_target_pairs={{0,2},{1,15},{2,4},{3,1},{4,6},{5,3},{6,8},{7,5},{8,10},{9,7},{10,... | collective-permute-start | bytes 786440 | tf_op jit(solution)/shard_map/gather/ppermute | solution.py:29
  35.4 2.1 %collective-permute-start.13 = (bf16[4,256,128]{2,1,0:T(8,128)(2,1)S(1)}, bf16[4,256,128]{2,1,0:T(8,128)(2,1)S(1)}, u32[]{:S(2)}, u32[]{:S(2)}) collective-permute-start(bf16[4,256,128]{2,1,0:T(8,128)(2,1)S(1)} %get-tuple-element.43.refs_7_), channel_id=1, source_target_pairs={{0,2},{1,15},{2,4},{3,1},{4,6},{5,3},{6,8},{7,5},{8,10},{9,7},{10,... | collective-permute-start | bytes 786440 | tf_op jit(solution)/shard_map/gather/ppermute | solution.py:29
  37.5 3.7 %copy-done = s32[3,48,128,128]{3,2,1,0:T(8,128)S(1)} copy-done((s32[3,48,128,128]{3,2,1,0:T(8,128)S(1)}, s32[3,48,128,128]{3,2,1,0:T(8,128)}, u32[]{:S(2)}) %copy-start) | copy-done | bytes 9437208
  41.1 3.5 %dequant.3 = (bf16[64,128,256]{2,1,0:T(8,128)(2,1)S(1)}, bf16[64,128,128]{2,1,0:T(8,128)(2,1)S(1)}, s32[1]{0:T(128)}) custom-call(bf16[16,128,256]{2,1,0:T(8,128)(2,1)S(1)} %merge_c.1.refs_0_, s32[3,48,128,128]{3,2,1,0:T(8,128)S(1)} %copy-done, s32[3,48]{1,0:T(4,128)S(1)} %copy-done.4, s32[3]{0:T(128)S(1)} %copy-done.5, f32[3,3,48,128]{3,2,1,0:T(8,128)S(1)} %copy-done.1), custom_call_target="tpu_custom_call" | custom-call | flops 12000000 | bytes 10485760 | tf_op jit(solution)/shard_map/gather/dequant/pallas_call | solution.py:104
  44.8 0.4 collective-permute-start.14
  45.2 7.1 %collective-permute-done.17.refs_3_ = bf16[4,256,128]{2,1,0:T(8,128)(2,1)S(1)} collective-permute-done((bf16[4,256,128]{2,1,0:T(8,128)(2,1)S(1)}, bf16[4,256,128]{2,1,0:T(8,128)(2,1)S(1)}, u32[]{:S(2)}, u32[]{:S(2)}) %collective-permute-start.17) | collective-permute-done | bytes 262176 | tf_op jit(solution)/shard_map/gather/ppermute | solution.py:29
  52.4 2.8 %collective-permute-done.14.refs_2_ = bf16[4,256,128]{2,1,0:T(8,128)(2,1)S(1)} collective-permute-done((bf16[4,256,128]{2,1,0:T(8,128)(2,1)S(1)}, bf16[4,256,128]{2,1,0:T(8,128)(2,1)S(1)}, u32[]{:S(2)}, u32[]{:S(2)}) %collective-permute-start.14) | collective-permute-done | bytes 262176 | tf_op jit(solution)/shard_map/gather/ppermute | solution.py:29
  55.2 0.3 collective-permute-start.20
  55.5 0.5 collective-permute-start.21
  56.0 0.6 part.1
  56.6 1.4 %collective-permute-start.10 = (bf16[8,128,256]{2,1,0:T(8,128)(2,1)S(1)}, bf16[8,128,256]{2,1,0:T(8,128)(2,1)S(1)}, u32[]{:S(2)}, u32[]{:S(2)}) collective-permute-start(bf16[8,128,256]{2,1,0:T(8,128)(2,1)S(1)} %part.1), channel_id=1, source_target_pairs={{0,16},{1,49},{2,18},{3,51},{4,20},{5,53},{6,22},{7,55},{8,24},{9,... | collective-permute-start | bytes 1572872 | tf_op jit(solution)/shard_map/gather/ppermute | solution.py:29
  58.0 2.7 %dequant.4 = (bf16[64,128,256]{2,1,0:T(8,128)(2,1)S(1)}, bf16[64,128,128]{2,1,0:T(8,128)(2,1)S(1)}, s32[1]{0:T(128)}) custom-call(bf16[16,128,256]{2,1,0:T(8,128)(2,1)S(1)} %merge_c.1.refs_0_, s32[3,48,128,128]{3,2,1,0:T(8,128)S(1)} %copy-done, s32[3,48]{1,0:T(4,128)S(1)} %copy-done.4, s32[3]{0:T(128)S(1)} %copy-done.5, f32[3,3,48,128]{3,2,1,0:T(8,128)S(1)} %copy-done.1), custom_call_target="tpu_custom_call" | custom-call | flops 12000000 | bytes 10485760 | tf_op jit(solution)/shard_map/gather/dequant/pallas_call | solution.py:104
  60.7 3.7 %dequant.5 = (bf16[64,128,256]{2,1,0:T(8,128)(2,1)S(1)}, bf16[64,128,128]{2,1,0:T(8,128)(2,1)S(1)}, s32[1]{0:T(128)}) custom-call(bf16[16,128,256]{2,1,0:T(8,128)(2,1)S(1)} %merge_c.1.refs_0_, s32[3,48,128,128]{3,2,1,0:T(8,128)S(1)} %copy-done, s32[3,48]{1,0:T(4,128)S(1)} %copy-done.4, s32[3]{0:T(128)S(1)} %copy-done.5, f32[3,3,48,128]{3,2,1,0:T(8,128)S(1)} %copy-done.1), custom_call_target="tpu_custom_call" | custom-call | flops 12000000 | bytes 10485760 | tf_op jit(solution)/shard_map/gather/dequant/pallas_call | solution.py:104
  64.4 1.2 collective-permute-done.18.refs_4_.refs_1_
  65.6 2.8 %collective-permute-done.15.refs_3_.refs_0_ = bf16[4,256,128]{2,1,0:T(8,128)(2,1)S(1)} collective-permute-done((bf16[4,256,128]{2,1,0:T(8,128)(2,1)S(1)}, bf16[4,256,128]{2,1,0:T(8,128)(2,1)S(1)}, u32[]{:S(2)}, u32[]{:S(2)}) %collective-permute-start.15) | collective-permute-done | bytes 262176 | tf_op jit(solution)/shard_map/gather/ppermute | solution.py:29
  68.4 1.8 %pick.1 = bf16[4,256,128]{2,1,0:T(8,128)(2,1)S(1)} custom-call(s32[1]{0:T(128)} %get-tuple-element.41.refs_0_.refs_1_, s32[1]{0:T(128)} %get-tuple-element.42.refs_1_.refs_2_, s32[3]{0:T(128)S(1)} %pad_add_fusion.pos_ref.refs_2_.refs_3_, bf16[4,256,128]{2,1,0:T(8,128)(2,1)S(1)} %collective-permute-done.15.refs_3_.refs_0_, ...), custom_call_target="tpu_custom_call" | custom-call | bytes 786444 | tf_op jit(solution)/shard_map/gather/pick/pallas_call | solution.py:49
  70.4 0.5 collective-permute-start.11
  70.9 4.6 %gate_up.2 = (f32[3,256,256]{2,1,0:T(8,128)S(1)}, s32[1]{0:T(128)}) custom-call(s32[1]{0:T(128)} %get-tuple-element.47.refs_0_, s32[1]{0:T(128)} %get-tuple-element.41.refs_0_.refs_1_, s32[1]{0:T(128)} %get-tuple-element.42.refs_1_.refs_2_, s32[3]{0:T(128)S(1)} %pad_add_fusion.pos_ref.refs_2_.refs_3_, ...), custom_call_target="tpu_custom_call" | custom-call | flops 2013265920 | bytes 15990800 | tf_op jit(solution)/shard_map/gather/gate_up/pallas_call | solution.py:49
  75.6 2.0 %hidden.2.refs_2_ = f32[384,256]{1,0:T(8,128)S(1)} custom-call(s32[3]{0:T(128)S(1)} %pad_add_fusion.pos_ref.refs_2_.refs_3_, bf16[64,128,128]{2,1,0:T(8,128)(2,1)S(1)} %get-tuple-element.38.w0, bf16[64,128,128]{2,1,0:T(8,128)(2,1)S(1)} %get-tuple-element.39.w1, bf16[64,128,128]{2,1,0:T(8,128)(2,1)S(1)} %get-tuple-element.40.w2, ...), custom_call_target="tpu_custom_call" | custom-call | flops 1207959552 | bytes 9830412 | tf_op jit(solution)/shard_map/gather/hidden/pallas_call | solution.py:49
  77.5 0.3 collective-permute-done.19.refs_2_
  78.1 1.3 collective-permute-done.23.refs_3_
  79.4 2.2 %gate_up.3 = (f32[3,256,256]{2,1,0:T(8,128)S(1)}, s32[1]{0:T(128)}) custom-call(s32[3]{0:T(128)S(1)} %pad_add_fusion.pos_ref.refs_2_.refs_3_, bf16[64,128,256]{2,1,0:T(8,128)(2,1)S(1)} %get-tuple-element.48.refs_4_.w0, bf16[64,128,256]{2,1,0:T(8,128)(2,1)S(1)} %get-tuple-element.49.refs_5_.w1, bf16[64,128,256]{2,1,0:T(8,128)(2,1)S(1)} %get-tuple-element.50.refs_6_.w2, ...), custom_call_target="tpu_custom_call" | custom-call | flops 1207959552 | bytes 15728656 | tf_op jit(solution)/shard_map/gather/gate_up/pallas_call | solution.py:49
  81.6 1.3 hidden.3
  82.9 1.5 %input_away.2 = bf16[16,128,256]{2,1,0:T(8,128)(2,1)S(1)} custom-call(s32[3]{0:T(128)S(1)} %pad_add_fusion.pos_ref.refs_2_.refs_3_, bf16[3,256,256]{2,1,0:T(8,128)(2,1)S(1)} %get-tuple-element.56.grad_ref, bf16[64,128,256]{2,1,0:T(8,128)(2,1)S(1)} %get-tuple-element.48.refs_4_.w0, bf16[64,128,256]{2,1,0:T(8,128)(2,1)S(1)} %get-tuple-element.49.refs_5_.w1, ...), custom_call_target="tpu_custom_call" | custom-call | flops 805306368 | bytes 14024716 | tf_op jit(solution)/shard_map/scatter/input_away/pallas_call | solution.py:49
  84.5 0.2 collective-permute-start.24
  84.7 1.5 %input_away.3 = bf16[16,128,256]{2,1,0:T(8,128)(2,1)S(1)} custom-call(s32[3]{0:T(128)S(1)} %pad_add_fusion.pos_ref.refs_2_.refs_3_, bf16[3,256,256]{2,1,0:T(8,128)(2,1)S(1)} %get-tuple-element.56.grad_ref, bf16[64,128,256]{2,1,0:T(8,128)(2,1)S(1)} %get-tuple-element.48.refs_4_.w0, bf16[64,128,256]{2,1,0:T(8,128)(2,1)S(1)} %get-tuple-element.49.refs_5_.w1, ...), custom_call_target="tpu_custom_call" | custom-call | flops 805306368 | bytes 14024716 | tf_op jit(solution)/shard_map/scatter/input_away/pallas_call | solution.py:49
  86.2 0.5 collective-permute-start.30
  86.7 0.5 collective-permute-done.24.refs_0_
  87.2 1.5 %input_here.2 = (bf16[4,128,256]{2,1,0:T(8,128)(2,1)S(1)}, bf16[4,128,256]{2,1,0:T(8,128)(2,1)S(1)}, f32[4,128,256]{2,1,0:T(8,128)S(1)}, f32[4,128,256]{2,1,0:T(8,128)S(1)}) custom-call(s32[3]{0:T(128)S(1)} %pad_add_fusion.pos_ref.refs_2_.refs_3_, bf16[3,256,256]{2,1,0:T(8,128)(2,1)S(1)} %get-tuple-element.56.grad_ref, ...), custom_call_target="tpu_custom_call" | custom-call | flops 805306368 | bytes 15597580 | tf_op jit(solution)/shard_map/scatter/input_here/pallas_call | solution.py:49
  88.7 0.3 collective-permute-start.25
  89.0 1.5 %input_here.3 = (bf16[4,128,256]{2,1,0:T(8,128)(2,1)S(1)}, bf16[4,128,256]{2,1,0:T(8,128)(2,1)S(1)}, f32[4,128,256]{2,1,0:T(8,128)S(1)}, f32[4,128,256]{2,1,0:T(8,128)S(1)}) custom-call(s32[3]{0:T(128)S(1)} %pad_add_fusion.pos_ref.refs_2_.refs_3_, bf16[3,256,256]{2,1,0:T(8,128)(2,1)S(1)} %get-tuple-element.56.grad_ref, ...), custom_call_target="tpu_custom_call" | custom-call | flops 805306368 | bytes 15597580 | tf_op jit(solution)/shard_map/scatter/input_here/pallas_call | solution.py:49
  90.6 1.9 %collective-permute-start.32 = (bf16[4,128,256]{2,1,0:T(8,128)(2,1)S(1)}, bf16[4,128,256]{2,1,0:T(8,128)(2,1)S(1)}, u32[]{:S(2)}, u32[]{:S(2)}) collective-permute-start(bf16[4,128,256]{2,1,0:T(8,128)(2,1)S(1)} %get-tuple-element.66), channel_id=1, source_target_pairs={{0,48},{1,49},{2,50},{3,51},{4,52},{5,53},{6,54},{7,55},{8,56},{9,... | collective-permute-start | bytes 786440 | tf_op jit(solution)/shard_map/scatter/ppermute | solution.py:29
  92.4 1.4 %collective-permute-start.31 = (bf16[4,128,256]{2,1,0:T(8,128)(2,1)S(1)}, bf16[4,128,256]{2,1,0:T(8,128)(2,1)S(1)}, u32[]{:S(2)}, u32[]{:S(2)}) collective-permute-start(bf16[4,128,256]{2,1,0:T(8,128)(2,1)S(1)} %get-tuple-element.64), channel_id=1, source_target_pairs={{0,16},{1,17},{2,18},{3,19},{4,20},{5,21},{6,22},{7,23},{8,24},{9,... | collective-permute-start | bytes 786440 | tf_op jit(solution)/shard_map/scatter/ppermute | solution.py:29
  93.9 4.1 %collective-permute-done.25.r = bf16[4,128,256]{2,1,0:T(8,128)(2,1)S(1)} collective-permute-done((bf16[4,128,256]{2,1,0:T(8,128)(2,1)S(1)}, bf16[4,128,256]{2,1,0:T(8,128)(2,1)S(1)}, u32[]{:S(2)}, u32[]{:S(2)}) %collective-permute-start.25) | collective-permute-done | bytes 262176 | tf_op jit(solution)/shard_map/scatter/ppermute | solution.py:29
  98.0 1.5 %collective-permute-start.26 = (bf16[4,128,256]{2,1,0:T(8,128)(2,1)S(1)}, bf16[4,128,256]{2,1,0:T(8,128)(2,1)S(1)}, u32[]{:S(2)}, u32[]{:S(2)}) collective-permute-start(bf16[4,128,256]{2,1,0:T(8,128)(2,1)S(1)} %add.17), channel_id=1, source_target_pairs={{0,16},{1,17},{2,18},{3,19},{4,20},{5,21},{6,22},{7,23},{8,24},{9,... | collective-permute-start | bytes 786440 | tf_op jit(solution)/shard_map/scatter/ppermute | solution.py:29
  99.5 0.6 collective-permute-start.29
  100.1 0.2 collective-permute-done.32.r
  100.4 0.6 collective-permute-start.33
  101.0 1.6 %collective-permute-start.27 = (f32[384]{0:T(512)S(1)}, f32[384]{0:T(512)S(1)}, u32[]{:S(2)}, u32[]{:S(2)}) collective-permute-start(f32[384]{0:T(512)S(1)} %reduce), channel_id=1, source_target_pairs={{0,64},{64,0},{128,192},{192,128},{1,65},{65,1},{129,193},{193,129... | collective-permute-start | bytes 4616 | tf_op jit(solution)/shard_map/ia3/ppermute | solution.py:424
  102.6 2.1 %collective-permute-done.27 = f32[384]{0:T(512)S(1)} collective-permute-done((f32[384]{0:T(512)S(1)}, f32[384]{0:T(512)S(1)}, u32[]{:S(2)}, u32[]{:S(2)}) %collective-permute-start.27) | collective-permute-done | bytes 1568 | tf_op jit(solution)/shard_map/ia3/ppermute | solution.py:424
  104.7 2.8 %collective-permute-start.28 = (f32[384]{0:T(512)S(1)}, f32[384]{0:T(512)S(1)}, u32[]{:S(2)}, u32[]{:S(2)}) collective-permute-start(f32[384]{0:T(512)S(1)} %add.10), channel_id=1, source_target_pairs={{0,192},{192,0},{64,128},{128,64},{1,193},{193,1},{65,129},{129,65... | collective-permute-start | bytes 4616 | tf_op jit(solution)/shard_map/ia3/ppermute | solution.py:425
  107.4 2.0 %collective-permute-done.28 = f32[384]{0:T(512)S(1)} collective-permute-done((f32[384]{0:T(512)S(1)}, f32[384]{0:T(512)S(1)}, u32[]{:S(2)}, u32[]{:S(2)}) %collective-permute-start.28) | collective-permute-done | bytes 1568 | tf_op jit(solution)/shard_map/ia3/ppermute | solution.py:425
  109.5 0.6 add.11
  110.0 3.2 %collective-permute-done.33.rb3 = bf16[4,128,256]{2,1,0:T(8,128)(2,1)S(1)} collective-permute-done((bf16[4,128,256]{2,1,0:T(8,128)(2,1)S(1)}, bf16[4,128,256]{2,1,0:T(8,128)(2,1)S(1)}, u32[]{:S(2)}, u32[]{:S(2)}) %collective-permute-start.33) | collective-permute-done | bytes 262176 | tf_op jit(solution)/shard_map/scatter/ppermute | solution.py:29
  113.3 0.7 y_sum.1
  114.0 19.8 %all_to_all.5.parts = bf16[8,128,256]{2,1,0:T(8,128)(2,1)S(1)} all-to-all(bf16[8,128,256]{2,1,0:T(8,128)(2,1)S(1)} %y_sum.1), channel_id=1, replica_groups={{0,2,4,6,8,10,12,14},{1,3,5,7,9,11,13,15},{16,18,20,22,24,26,28,30},{17..., dimensions={0} | all-to-all | bytes 1048576 | tf_op jit(solution)/shard_map/scatter/all_to_all | solution.py:443
  133.8 0.8 z_sum.1
  (48 shorter events, 1.3 us)
Async XLA Ops:
  0.6 36.8 %copy-start.1 = (f32[3,3,48,128]{3,2,1,0:T(8,128)S(1)}, f32[3,3,48,128]{3,2,1,0:T(8,128)}, u32[]{:S(2)}) copy-start(f32[3,3,48,128]{3,2,1,0:T(8,128)} %refs_4_.5) | copy-start | bytes 663556
  0.6 1.7 %collective-permute-start = (bf16[256,128]{1,0:T(8,128)(2,1)}, bf16[256,128]{1,0:T(8,128)(2,1)S(1)}, u32[]{:S(2)}, u32[]{:S(2)}) collective-permute-start(bf16[256,128]{1,0:T(8,128)(2,1)} %tok.1), channel_id=1, source_target_pairs={{0,1},{1,0},{2,3},{3,2},{4,5},{5,4},{6,7},{7,6},{8,9},{9,8},{10,11... | collective-permute-start | bytes 196616 | tf_op jit(solution)/shard_map/gather/ppermute | solution.py:29
  0.7 17.0 %collective-permute-start.3 = (bf16[256,128]{1,0:T(8,128)(2,1)}, bf16[256,128]{1,0:T(8,128)(2,1)S(1)}, u32[]{:S(2)}, u32[]{:S(2)}) collective-permute-start(bf16[256,128]{1,0:T(8,128)(2,1)} %tok.1), channel_id=1, source_target_pairs={{0,32},{1,33},{2,34},{3,35},{4,36},{5,37},{6,38},{7,39},{8,40},{9,... | collective-permute-start | bytes 196616 | tf_op jit(solution)/shard_map/gather/ppermute | solution.py:29
  2.1 1.5 %collective-permute-start.1 = (bf16[256,128]{1,0:T(8,128)(2,1)}, bf16[256,128]{1,0:T(8,128)(2,1)S(1)}, u32[]{:S(2)}, u32[]{:S(2)}) collective-permute-start(bf16[256,128]{1,0:T(8,128)(2,1)} %cot.1), channel_id=1, source_target_pairs={{0,1},{1,0},{2,3},{3,2},{4,5},{5,4},{6,7},{7,6},{8,9},{9,8},{10,11... | collective-permute-start | bytes 196616 | tf_op jit(solution)/shard_map/gather/ppermute | solution.py:29
  3.5 0.8 copy-start.2
  4.4 0.8 copy-start.3
  5.2 32.2 %copy-start.4 = (s32[3,48]{1,0:T(4,128)S(1)}, s32[3,48]{1,0:T(4,128)}, u32[]{:S(2)}) copy-start(s32[3,48]{1,0:T(4,128)} %refs_2_.5) | copy-start | bytes 1732
  5.2 32.2 %copy-start.5 = (s32[3]{0:T(128)S(1)}, s32[3]{0:T(128)}, u32[]{:S(2)}) copy-start(s32[3]{0:T(128)} %refs_3_.5) | copy-start | bytes 40
  6.3 12.0 %collective-permute-start.2 = (bf16[2,256,128]{2,1,0:T(8,128)(2,1)S(1)}, bf16[2,256,128]{2,1,0:T(8,128)(2,1)S(1)}, u32[]{:S(2)}, u32[]{:S(2)}) collective-permute-start(bf16[2,256,128]{2,1,0:T(8,128)(2,1)S(1)} %get-tuple-element.36.chip), channel_id=1, source_target_pairs={{0,16},{1,49},{2,18},{3,51},{4,20},{5,53},{6,22},{7,55},{8,24},{9,... | collective-permute-start | bytes 393224 | tf_op jit(solution)/shard_map/gather/ppermute | solution.py:29
  8.6 18.8 %collective-permute-start.4 = (bf16[2,128,256]{2,1,0:T(8,128)(2,1)S(1)}, bf16[2,128,256]{2,1,0:T(8,128)(2,1)S(1)}, u32[]{:S(2)}, u32[]{:S(2)}) collective-permute-start(bf16[2,128,256]{2,1,0:T(8,128)(2,1)S(1)} %get-tuple-element.35.chip), channel_id=1, source_target_pairs={{0,2},{1,15},{2,4},{3,1},{4,6},{5,3},{6,8},{7,5},{8,10},{9,7},{10,... | collective-permute-start | bytes 393224 | tf_op jit(solution)/shard_map/gather/ppermute | solution.py:29
  10.5 16.9 %collective-permute-start.5 = (bf16[2,128,256]{2,1,0:T(8,128)(2,1)S(1)}, bf16[2,128,256]{2,1,0:T(8,128)(2,1)S(1)}, u32[]{:S(2)}, u32[]{:S(2)}) collective-permute-start(bf16[2,128,256]{2,1,0:T(8,128)(2,1)S(1)} %get-tuple-element.35.chip), channel_id=1, source_target_pairs={{0,4},{1,13},{2,6},{3,15},{4,8},{5,1},{6,10},{7,3},{8,12},{9,5},{1... | collective-permute-start | bytes 393224 | tf_op jit(solution)/shard_map/gather/ppermute | solution.py:29
  13.7 14.2 %collective-permute-start.6 = (bf16[2,128,256]{2,1,0:T(8,128)(2,1)S(1)}, bf16[2,128,256]{2,1,0:T(8,128)(2,1)S(1)}, u32[]{:S(2)}, u32[]{:S(2)}) collective-permute-start(bf16[2,128,256]{2,1,0:T(8,128)(2,1)S(1)} %get-tuple-element.35.chip), channel_id=1, source_target_pairs={{0,6},{1,11},{2,8},{3,13},{4,10},{5,15},{6,12},{7,1},{8,14},{9,3},... | collective-permute-start | bytes 393224 | tf_op jit(solution)/shard_map/gather/ppermute | solution.py:29
  17.8 9.6 %collective-permute-start.7 = (bf16[128,256]{1,0:T(8,128)(2,1)S(1)}, bf16[128,256]{1,0:T(8,128)(2,1)S(1)}, u32[]{:S(2)}, u32[]{:S(2)}) collective-permute-start(bf16[128,256]{1,0:T(8,128)(2,1)S(1)} %get-tuple-element.37), channel_id=1, source_target_pairs={{0,8},{1,9},{2,10},{3,11},{4,12},{5,13},{6,14},{7,15},{8,0},{9,1},... | collective-permute-start | bytes 196616 | tf_op jit(solution)/shard_map/gather/ppermute | solution.py:29
  28.0 1.9 %collective-permute-start.8 = (bf16[7,128,256]{2,1,0:T(8,128)(2,1)S(1)}, bf16[7,128,256]{2,1,0:T(8,128)(2,1)S(1)}, u32[]{:S(2)}, u32[]{:S(2)}) collective-permute-start(bf16[7,128,256]{2,1,0:T(8,128)(2,1)S(1)} %stack.21.mine), channel_id=1, source_target_pairs={{0,1},{1,0},{2,3},{3,2},{4,5},{5,4},{6,7},{7,6},{8,9},{9,8},{10,11... | collective-permute-start | bytes 1376264 | tf_op jit(solution)/shard_map/gather/ppermute | solution.py:29
  30.5 25.0 %collective-permute-start.9 = (bf16[16,128,256]{2,1,0:T(8,128)(2,1)S(1)}, bf16[16,128,256]{2,1,0:T(8,128)(2,1)S(1)}, u32[]{:S(2)}, u32[]{:S(2)}) collective-permute-start(bf16[16,128,256]{2,1,0:T(8,128)(2,1)S(1)} %merge_c.1.refs_0_), channel_id=1, source_target_pairs={{0,16},{1,49},{2,18},{3,51},{4,20},{5,53},{6,22},{7,55},{8,24},{9,... | collective-permute-start | bytes 3145736 | tf_op jit(solution)/shard_map/gather/ppermute | solution.py:29
  31.7 1.4 %collective-permute-start.12 = (bf16[3,256,128]{2,1,0:T(8,128)(2,1)S(1)}, bf16[3,256,128]{2,1,0:T(8,128)(2,1)S(1)}, u32[]{:S(2)}, u32[]{:S(2)}) collective-permute-start(bf16[3,256,128]{2,1,0:T(8,128)(2,1)S(1)} %stack.20.refs_0_.mine), channel_id=1, source_target_pairs={{0,1},{1,0},{2,3},{3,2},{4,5},{5,4},{6,7},{7,6},{8,9},{9,8},{10,11... | collective-permute-start | bytes 589832 | tf_op jit(solution)/shard_map/gather/ppermute | solution.py:29
  33.7 11.0 %collective-permute-start.16 = (bf16[4,256,128]{2,1,0:T(8,128)(2,1)S(1)}, bf16[4,256,128]{2,1,0:T(8,128)(2,1)S(1)}, u32[]{:S(2)}, u32[]{:S(2)}) collective-permute-start(bf16[4,256,128]{2,1,0:T(8,128)(2,1)S(1)} %get-tuple-element.44.refs_8_), channel_id=1, source_target_pairs={{0,2},{1,15},{2,4},{3,1},{4,6},{5,3},{6,8},{7,5},{8,10},{9,7},{10,... | collective-permute-start | bytes 786440 | tf_op jit(solution)/shard_map/gather/ppermute | solution.py:29
  35.4 9.4 %collective-permute-start.13 = (bf16[4,256,128]{2,1,0:T(8,128)(2,1)S(1)}, bf16[4,256,128]{2,1,0:T(8,128)(2,1)S(1)}, u32[]{:S(2)}, u32[]{:S(2)}) collective-permute-start(bf16[4,256,128]{2,1,0:T(8,128)(2,1)S(1)} %get-tuple-element.43.refs_7_), channel_id=1, source_target_pairs={{0,2},{1,15},{2,4},{3,1},{4,6},{5,3},{6,8},{7,5},{8,10},{9,7},{10,... | collective-permute-start | bytes 786440 | tf_op jit(solution)/shard_map/gather/ppermute | solution.py:29
  37.5 3.7 %copy-start = (s32[3,48,128,128]{3,2,1,0:T(8,128)S(1)}, s32[3,48,128,128]{3,2,1,0:T(8,128)}, u32[]{:S(2)}) copy-start(s32[3,48,128,128]{3,2,1,0:T(8,128)} %refs_1_.5) | copy-start | bytes 28311556
  44.7 7.7 %collective-permute-start.17 = (bf16[4,256,128]{2,1,0:T(8,128)(2,1)S(1)}, bf16[4,256,128]{2,1,0:T(8,128)(2,1)S(1)}, u32[]{:S(2)}, u32[]{:S(2)}) collective-permute-start(bf16[4,256,128]{2,1,0:T(8,128)(2,1)S(1)} %collective-permute-done.16.refs_1_), channel_id=1, source_target_pairs={{0,2},{1,15},{2,4},{3,1},{4,6},{5,3},{6,8},{7,5},{8,10},{9,7},{10,... | collective-permute-start | bytes 786440 | tf_op jit(solution)/shard_map/gather/ppermute | solution.py:29
  44.8 10.4 %collective-permute-start.14 = (bf16[4,256,128]{2,1,0:T(8,128)(2,1)S(1)}, bf16[4,256,128]{2,1,0:T(8,128)(2,1)S(1)}, u32[]{:S(2)}, u32[]{:S(2)}) collective-permute-start(bf16[4,256,128]{2,1,0:T(8,128)(2,1)S(1)} %collective-permute-done.13.refs_0_), channel_id=1, source_target_pairs={{0,2},{1,15},{2,4},{3,1},{4,6},{5,3},{6,8},{7,5},{8,10},{9,7},{10,... | collective-permute-start | bytes 786440 | tf_op jit(solution)/shard_map/gather/ppermute | solution.py:29
  55.2 15.6 %collective-permute-start.20 = (bf16[16,256,128]{2,1,0:T(8,128)(2,1)S(1)}, bf16[16,256,128]{2,1,0:T(8,128)(2,1)S(1)}, u32[]{:S(2)}, u32[]{:S(2)}) collective-permute-start(bf16[16,256,128]{2,1,0:T(8,128)(2,1)S(1)} %stack.22.refs_9_), channel_id=1, source_target_pairs={{0,1},{1,0},{2,3},{3,2},{4,5},{5,4},{6,7},{7,6},{8,9},{9,8},{10,11... | collective-permute-start | bytes 3145736 | tf_op jit(solution)/shard_map/gather/ppermute | solution.py:29
  55.5 20.0 %collective-permute-start.21 = (bf16[16,128,256]{2,1,0:T(8,128)(2,1)S(1)}, bf16[16,128,256]{2,1,0:T(8,128)(2,1)S(1)}, u32[]{:S(2)}, u32[]{:S(2)}) collective-permute-start(bf16[16,128,256]{2,1,0:T(8,128)(2,1)S(1)} %collective-permute-done.9.a.refs_1_), channel_id=1, source_target_pairs={{0,1},{1,0},{2,3},{3,2},{4,5},{5,4},{6,7},{7,6},{8,9},{9,8},{10,11... | collective-permute-start | bytes 3145736 | tf_op jit(solution)/shard_map/gather/ppermute | solution.py:29
  56.6 13.8 %collective-permute-start.10 = (bf16[8,128,256]{2,1,0:T(8,128)(2,1)S(1)}, bf16[8,128,256]{2,1,0:T(8,128)(2,1)S(1)}, u32[]{:S(2)}, u32[]{:S(2)}) collective-permute-start(bf16[8,128,256]{2,1,0:T(8,128)(2,1)S(1)} %part.1), channel_id=1, source_target_pairs={{0,16},{1,49},{2,18},{3,51},{4,20},{5,53},{6,22},{7,55},{8,24},{9,... | collective-permute-start | bytes 1572872 | tf_op jit(solution)/shard_map/gather/ppermute | solution.py:29
  58.0 7.6 %collective-permute-start.18 = (bf16[4,256,128]{2,1,0:T(8,128)(2,1)S(1)}, bf16[4,256,128]{2,1,0:T(8,128)(2,1)S(1)}, u32[]{:S(2)}, u32[]{:S(2)}) collective-permute-start(bf16[4,256,128]{2,1,0:T(8,128)(2,1)S(1)} %collective-permute-done.17.refs_3_), channel_id=1, source_target_pairs={{0,2},{1,15},{2,4},{3,1},{4,6},{5,3},{6,8},{7,5},{8,10},{9,7},{10,... | collective-permute-start | bytes 786440 | tf_op jit(solution)/shard_map/gather/ppermute | solution.py:29
  58.0 10.4 %collective-permute-start.15 = (bf16[4,256,128]{2,1,0:T(8,128)(2,1)S(1)}, bf16[4,256,128]{2,1,0:T(8,128)(2,1)S(1)}, u32[]{:S(2)}, u32[]{:S(2)}) collective-permute-start(bf16[4,256,128]{2,1,0:T(8,128)(2,1)S(1)} %collective-permute-done.14.refs_2_), channel_id=1, source_target_pairs={{0,2},{1,15},{2,4},{3,1},{4,6},{5,3},{6,8},{7,5},{8,10},{9,7},{10,... | collective-permute-start | bytes 786440 | tf_op jit(solution)/shard_map/gather/ppermute | solution.py:29
  70.1 7.7 %collective-permute-start.19 = (bf16[4,256,128]{2,1,0:T(8,128)(2,1)S(1)}, bf16[4,256,128]{2,1,0:T(8,128)(2,1)S(1)}, u32[]{:S(2)}, u32[]{:S(2)}) collective-permute-start(bf16[4,256,128]{2,1,0:T(8,128)(2,1)S(1)} %pick.1), channel_id=1, source_target_pairs={{0,2},{1,15},{2,4},{3,1},{4,6},{5,3},{6,8},{7,5},{8,10},{9,7},{10,... | collective-permute-start | bytes 786440 | tf_op jit(solution)/shard_map/gather/ppermute | solution.py:29
  70.3 7.8 %collective-permute-start.22 = (bf16[8,256,128]{2,1,0:T(8,128)(2,1)S(1)}, bf16[8,256,128]{2,1,0:T(8,128)(2,1)S(1)}, u32[]{:S(2)}, u32[]{:S(2)}) collective-permute-start(bf16[8,256,128]{2,1,0:T(8,128)(2,1)S(1)} %stack.23.refs_0_), channel_id=1, source_target_pairs={{0,1},{1,0},{2,3},{3,2},{4,5},{5,4},{6,7},{7,6},{8,9},{9,8},{10,11... | collective-permute-start | bytes 1572872 | tf_op jit(solution)/shard_map/gather/ppermute | solution.py:29
  70.4 11.2 %collective-permute-start.11 = (bf16[8,128,256]{2,1,0:T(8,128)(2,1)S(1)}, bf16[8,128,256]{2,1,0:T(8,128)(2,1)S(1)}, u32[]{:S(2)}, u32[]{:S(2)}) collective-permute-start(bf16[8,128,256]{2,1,0:T(8,128)(2,1)S(1)} %collective-permute-done.10.refs_0_), channel_id=1, source_target_pairs={{0,1},{1,0},{2,3},{3,2},{4,5},{5,4},{6,7},{7,6},{8,9},{9,8},{10,11... | collective-permute-start | bytes 1572872 | tf_op jit(solution)/shard_map/gather/ppermute | solution.py:29
  75.5 2.4 %copy-start.6 = (f32[384]{0:T(512)S(1)}, f32[384]{0:T(512)}, u32[]{:S(2)}) copy-start(f32[384]{0:T(512)} %param.13) | copy-start | bytes 4612
  77.8 1.6 %collective-permute-start.23 = (bf16[4,256,128]{2,1,0:T(8,128)(2,1)S(1)}, bf16[4,256,128]{2,1,0:T(8,128)(2,1)S(1)}, u32[]{:S(2)}, u32[]{:S(2)}) collective-permute-start(bf16[4,256,128]{2,1,0:T(8,128)(2,1)S(1)} %collective-permute-done.19.refs_2_), channel_id=1, source_target_pairs={{0,1},{1,0},{2,3},{3,2},{4,5},{5,4},{6,7},{7,6},{8,9},{9,8},{10,11... | collective-permute-start | bytes 786440 | tf_op jit(solution)/shard_map/gather/ppermute | solution.py:29
  84.5 2.7 %collective-permute-start.24 = (bf16[16,128,256]{2,1,0:T(8,128)(2,1)S(1)}, bf16[16,128,256]{2,1,0:T(8,128)(2,1)S(1)}, u32[]{:S(2)}, u32[]{:S(2)}) collective-permute-start(bf16[16,128,256]{2,1,0:T(8,128)(2,1)S(1)} %input_away.2), channel_id=1, source_target_pairs={{0,1},{1,0},{2,3},{3,2},{4,5},{5,4},{6,7},{7,6},{8,9},{9,8},{10,11... | collective-permute-start | bytes 3145736 | tf_op jit(solution)/shard_map/scatter/ppermute | solution.py:29
  86.2 2.8 %collective-permute-start.30 = (bf16[16,128,256]{2,1,0:T(8,128)(2,1)S(1)}, bf16[16,128,256]{2,1,0:T(8,128)(2,1)S(1)}, u32[]{:S(2)}, u32[]{:S(2)}) collective-permute-start(bf16[16,128,256]{2,1,0:T(8,128)(2,1)S(1)} %input_away.3), channel_id=1, source_target_pairs={{0,1},{1,0},{2,3},{3,2},{4,5},{5,4},{6,7},{7,6},{8,9},{9,8},{10,11... | collective-permute-start | bytes 3145736 | tf_op jit(solution)/shard_map/scatter/ppermute | solution.py:29
  88.7 9.2 %collective-permute-start.25 = (bf16[4,128,256]{2,1,0:T(8,128)(2,1)S(1)}, bf16[4,128,256]{2,1,0:T(8,128)(2,1)S(1)}, u32[]{:S(2)}, u32[]{:S(2)}) collective-permute-start(bf16[4,128,256]{2,1,0:T(8,128)(2,1)S(1)} %get-tuple-element.59), channel_id=1, source_target_pairs={{0,16},{1,17},{2,18},{3,19},{4,20},{5,21},{6,22},{7,23},{8,24},{9,... | collective-permute-start | bytes 786440 | tf_op jit(solution)/shard_map/scatter/ppermute | solution.py:29
  90.6 9.8 %collective-permute-start.32 = (bf16[4,128,256]{2,1,0:T(8,128)(2,1)S(1)}, bf16[4,128,256]{2,1,0:T(8,128)(2,1)S(1)}, u32[]{:S(2)}, u32[]{:S(2)}) collective-permute-start(bf16[4,128,256]{2,1,0:T(8,128)(2,1)S(1)} %get-tuple-element.66), channel_id=1, source_target_pairs={{0,48},{1,49},{2,50},{3,51},{4,52},{5,53},{6,54},{7,55},{8,56},{9,... | collective-permute-start | bytes 786440 | tf_op jit(solution)/shard_map/scatter/ppermute | solution.py:29
  92.4 17.6 %collective-permute-start.31 = (bf16[4,128,256]{2,1,0:T(8,128)(2,1)S(1)}, bf16[4,128,256]{2,1,0:T(8,128)(2,1)S(1)}, u32[]{:S(2)}, u32[]{:S(2)}) collective-permute-start(bf16[4,128,256]{2,1,0:T(8,128)(2,1)S(1)} %get-tuple-element.64), channel_id=1, source_target_pairs={{0,16},{1,17},{2,18},{3,19},{4,20},{5,21},{6,22},{7,23},{8,24},{9,... | collective-permute-start | bytes 786440 | tf_op jit(solution)/shard_map/scatter/ppermute | solution.py:29
  98.0 12.0 %collective-permute-start.26 = (bf16[4,128,256]{2,1,0:T(8,128)(2,1)S(1)}, bf16[4,128,256]{2,1,0:T(8,128)(2,1)S(1)}, u32[]{:S(2)}, u32[]{:S(2)}) collective-permute-start(bf16[4,128,256]{2,1,0:T(8,128)(2,1)S(1)} %add.17), channel_id=1, source_target_pairs={{0,16},{1,17},{2,18},{3,19},{4,20},{5,21},{6,22},{7,23},{8,24},{9,... | collective-permute-start | bytes 786440 | tf_op jit(solution)/shard_map/scatter/ppermute | solution.py:29
  99.5 10.5 %collective-permute-start.29 = (bf16[4,128,256]{2,1,0:T(8,128)(2,1)S(1)}, bf16[4,128,256]{2,1,0:T(8,128)(2,1)S(1)}, u32[]{:S(2)}, u32[]{:S(2)}) collective-permute-start(bf16[4,128,256]{2,1,0:T(8,128)(2,1)S(1)} %get-tuple-element.62), channel_id=1, source_target_pairs={{0,48},{1,49},{2,50},{3,51},{4,52},{5,53},{6,54},{7,55},{8,56},{9,... | collective-permute-start | bytes 786440 | tf_op jit(solution)/shard_map/scatter/ppermute | solution.py:29
  100.4 12.9 %collective-permute-start.33 = (bf16[4,128,256]{2,1,0:T(8,128)(2,1)S(1)}, bf16[4,128,256]{2,1,0:T(8,128)(2,1)S(1)}, u32[]{:S(2)}, u32[]{:S(2)}) collective-permute-start(bf16[4,128,256]{2,1,0:T(8,128)(2,1)S(1)} %add.18), channel_id=1, source_target_pairs={{0,48},{1,49},{2,50},{3,51},{4,52},{5,53},{6,54},{7,55},{8,56},{9,... | collective-permute-start | bytes 786440 | tf_op jit(solution)/shard_map/scatter/ppermute | solution.py:29
  101.0 3.7 %collective-permute-start.27 = (f32[384]{0:T(512)S(1)}, f32[384]{0:T(512)S(1)}, u32[]{:S(2)}, u32[]{:S(2)}) collective-permute-start(f32[384]{0:T(512)S(1)} %reduce), channel_id=1, source_target_pairs={{0,64},{64,0},{128,192},{192,128},{1,65},{65,1},{129,193},{193,129... | collective-permute-start | bytes 4616 | tf_op jit(solution)/shard_map/ia3/ppermute | solution.py:424
  104.7 4.8 %collective-permute-start.28 = (f32[384]{0:T(512)S(1)}, f32[384]{0:T(512)S(1)}, u32[]{:S(2)}, u32[]{:S(2)}) collective-permute-start(f32[384]{0:T(512)S(1)} %add.10), channel_id=1, source_target_pairs={{0,192},{192,0},{64,128},{128,64},{1,193},{193,1},{65,129},{129,65... | collective-permute-start | bytes 4616 | tf_op jit(solution)/shard_map/ia3/ppermute | solution.py:425

commit v2 on v1

--- a/solution.py
+++ b/solution.py
@@ -367,7 +367,8 @@
         t0, t1 = call(merge_t_kernel, "merge_t", (pos, chip_t, near_t, swap(near_t)), [array((4, 256, 128), BF16)] * 2)
         near_c = stack([send(chip_c, dz=d, signed=True) for d in (1, 2, 3)] + [send(own_c, dz=4)], after=(near_t,))
         c0 = call(
-            merge_c_kernel, "merge_c", (pos, chip_c, near_c, swap(near_c)), [array((16, 128, 256), BF16)]
+            merge_c_kernel, "merge_c", (pos, chip_c, near_c, swap(near_c)), [array((16, 128, 256), BF16)],
+            after=(t0,),
         )[0]
         e1 = send(c0, dy=1, signed=True)
         ws = [dequant(h, weight_codes, block_scales, block_index, block_count, (c0,)) for h in range(3)]

time: 135 us -> 134 us (level)
  waiting for transfers between devices: 41.8 us -> 38.3 us
  starting transfers between devices: 33.4 us -> 35.5 us
    ppermute x32, waiting for transfers between devices: 37.7 us -> 34.2 us  [send(): return lax.ppermute(a, 'mp', pairs)]
    ppermute x32, starting transfers between devices: 29 us -> 31.2 us  [send(): return lax.ppermute(a, 'mp', pairs)]
where the time goes in v2:
time: 134 us; the launch traced here: 133 us
  waiting for transfers between devices  38.3 us (29%)
  starting transfers between devices  35.5 us (26%)
  Pallas kernels  32.3 us (24%)
  blocking collectives  20.1 us (15%)
  local copies, waits for them, and re-layouts  5.48 us (4%)
    ppermute x32, waiting for transfers between devices, send(): return lax.ppermute(a, 'mp', pairs)  34.2 us
    ppermute x32, starting transfers between devices, send(): return lax.ppermute(a, 'mp', pairs)  31.2 us
    pallas_call x20, Pallas kernels, call(): pl.pallas_call((lambda *refs: kernel(*refs[skip:])) if skip else kernel,...  21.4 us
    all_to_all x1, blocking collectives, on_device(): lax.all_to_all(total, 'mp', 0, 0, axis_index_groups=columns, tiled=True)  20.1 us
    pallas_call x3, Pallas kernels, dequant(): pl.pallas_call((lambda *refs: kernel(*refs[skip:])) if skip else kernel,...  9.77 us
    unnamed x14, local copies, waits for them, and re-layouts  5.37 us
    ppermute x1, starting transfers between devices, on_device(): lax.ppermute(ia3_part, 'dp', [(0, 3), (3, 0), (1, 2), (2, 1)])  2.76 us
  transfers between devices with their start and end apart: 34, of which 17 were waited for; matrix products, arithmetic and copies ran while one was open for 1% of the time, Pallas kernels for 20%

profile of v2, /device:TPU:24, one launch (start us, length us, event | category | flops | bytes accessed | tf_op | source)
XLA Modules:
  0.0 133.3 jit_solution(14114438607467126897)
XLA Ops:
  0.7 1.3 collective-permute-start.3
  2.3 1.2 collective-permute-done.1.sib_c
  3.5 0.8 copy-done.2
  4.4 0.8 copy-done.3
  5.2 1.1 own.1
  6.3 2.3 %collective-permute-start.2 = (bf16[2,256,128]{2,1,0:T(8,128)(2,1)S(1)}, bf16[2,256,128]{2,1,0:T(8,128)(2,1)S(1)}, u32[]{:S(2)}, u32[]{:S(2)}) collective-permute-start(bf16[2,256,128]{2,1,0:T(8,128)(2,1)S(1)} %get-tuple-element.35.chip), channel_id=1, source_target_pairs={{0,16},{1,49},{2,18},{3,51},{4,20},{5,53},{6,22},{7,55},{8,24},{9,... | collective-permute-start | bytes 393224 | tf_op jit(solution)/shard_map/gather/ppermute | solution.py:29
  8.6 1.9 %collective-permute-start.5 = (bf16[2,128,256]{2,1,0:T(8,128)(2,1)S(1)}, bf16[2,128,256]{2,1,0:T(8,128)(2,1)S(1)}, u32[]{:S(2)}, u32[]{:S(2)}) collective-permute-start(bf16[2,128,256]{2,1,0:T(8,128)(2,1)S(1)} %get-tuple-element.37.refs_2_), channel_id=1, source_target_pairs={{0,2},{1,15},{2,4},{3,1},{4,6},{5,3},{6,8},{7,5},{8,10},{9,7},{10,... | collective-permute-start | bytes 393224 | tf_op jit(solution)/shard_map/gather/ppermute | solution.py:29
  10.5 3.3 %collective-permute-start.6 = (bf16[2,128,256]{2,1,0:T(8,128)(2,1)S(1)}, bf16[2,128,256]{2,1,0:T(8,128)(2,1)S(1)}, u32[]{:S(2)}, u32[]{:S(2)}) collective-permute-start(bf16[2,128,256]{2,1,0:T(8,128)(2,1)S(1)} %get-tuple-element.37.refs_2_), channel_id=1, source_target_pairs={{0,4},{1,13},{2,6},{3,15},{4,8},{5,1},{6,10},{7,3},{8,12},{9,5},{1... | collective-permute-start | bytes 393224 | tf_op jit(solution)/shard_map/gather/ppermute | solution.py:29
  13.7 4.0 %collective-permute-start.7 = (bf16[2,128,256]{2,1,0:T(8,128)(2,1)S(1)}, bf16[2,128,256]{2,1,0:T(8,128)(2,1)S(1)}, u32[]{:S(2)}, u32[]{:S(2)}) collective-permute-start(bf16[2,128,256]{2,1,0:T(8,128)(2,1)S(1)} %get-tuple-element.37.refs_2_), channel_id=1, source_target_pairs={{0,6},{1,11},{2,8},{3,13},{4,10},{5,15},{6,12},{7,1},{8,14},{9,3},... | collective-permute-start | bytes 393224 | tf_op jit(solution)/shard_map/gather/ppermute | solution.py:29
  17.8 0.5 collective-permute-start.8
  18.3 9.0 %collective-permute-done.8.refs_4_ = bf16[128,256]{1,0:T(8,128)(2,1)S(1)} collective-permute-done((bf16[128,256]{1,0:T(8,128)(2,1)S(1)}, bf16[128,256]{1,0:T(8,128)(2,1)S(1)}, u32[]{:S(2)}, u32[]{:S(2)}) %collective-permute-start.8) | collective-permute-done | bytes 65568 | tf_op jit(solution)/shard_map/gather/ppermute | solution.py:29
  27.4 0.6 collective-permute-done.7.refs_3_
  28.1 0.5 collective-permute-start.4
  28.6 1.6 %collective-permute-done.4.other = bf16[3,256,128]{2,1,0:T(8,128)(2,1)S(1)} collective-permute-done((bf16[3,256,128]{2,1,0:T(8,128)(2,1)S(1)}, bf16[3,256,128]{2,1,0:T(8,128)(2,1)S(1)}, u32[]{:S(2)}, u32[]{:S(2)}) %collective-permute-start.4) | collective-permute-done | bytes 196640 | tf_op jit(solution)/shard_map/gather/ppermute | solution.py:29
  30.2 0.6 merge_t.1
  30.8 0.6 merge_c.1.refs_0_
  31.4 1.2 collective-permute-start.10
  32.6 1.6 %collective-permute-start.16 = (bf16[4,256,128]{2,1,0:T(8,128)(2,1)S(1)}, bf16[4,256,128]{2,1,0:T(8,128)(2,1)S(1)}, u32[]{:S(2)}, u32[]{:S(2)}) collective-permute-start(bf16[4,256,128]{2,1,0:T(8,128)(2,1)S(1)} %get-tuple-element.44.refs_8_), channel_id=1, source_target_pairs={{0,2},{1,15},{2,4},{3,1},{4,6},{5,3},{6,8},{7,5},{8,10},{9,7},{10,... | collective-permute-start | bytes 786440 | tf_op jit(solution)/shard_map/gather/ppermute | solution.py:29
  34.1 2.1 %collective-permute-start.13 = (bf16[4,256,128]{2,1,0:T(8,128)(2,1)S(1)}, bf16[4,256,128]{2,1,0:T(8,128)(2,1)S(1)}, u32[]{:S(2)}, u32[]{:S(2)}) collective-permute-start(bf16[4,256,128]{2,1,0:T(8,128)(2,1)S(1)} %get-tuple-element.36.refs_0_.refs_7_), channel_id=1, source_target_pairs={{0,2},{1,15},{2,4},{3,1},{4,6},{5,3},{6,8},{7,5},{8,10},{9,7},{10,... | collective-permute-start | bytes 786440 | tf_op jit(solution)/shard_map/gather/ppermute | solution.py:29
  36.2 3.7 %copy-done = s32[3,48,128,128]{3,2,1,0:T(8,128)S(1)} copy-done((s32[3,48,128,128]{3,2,1,0:T(8,128)S(1)}, s32[3,48,128,128]{3,2,1,0:T(8,128)}, u32[]{:S(2)}) %copy-start) | copy-done | bytes 9437208
  39.9 3.2 %dequant.3 = (bf16[64,128,256]{2,1,0:T(8,128)(2,1)S(1)}, bf16[64,128,128]{2,1,0:T(8,128)(2,1)S(1)}, s32[1]{0:T(128)}) custom-call(bf16[16,128,256]{2,1,0:T(8,128)(2,1)S(1)} %merge_c.1.refs_0_, s32[3,48,128,128]{3,2,1,0:T(8,128)S(1)} %copy-done, s32[3,48]{1,0:T(4,128)S(1)} %copy-done.4, s32[3]{0:T(128)S(1)} %copy-done.5, f32[3,3,48,128]{3,2,1,0:T(8,128)S(1)} %copy-done.1), custom_call_target="tpu_custom_call" | custom-call | flops 12000000 | bytes 10485760 | tf_op jit(solution)/shard_map/gather/dequant/pallas_call | solution.py:104
  43.2 0.4 collective-permute-start.17
  43.6 0.3 collective-permute-start.14
  43.8 7.0 %collective-permute-done.17.refs_3_ = bf16[4,256,128]{2,1,0:T(8,128)(2,1)S(1)} collective-permute-done((bf16[4,256,128]{2,1,0:T(8,128)(2,1)S(1)}, bf16[4,256,128]{2,1,0:T(8,128)(2,1)S(1)}, u32[]{:S(2)}, u32[]{:S(2)}) %collective-permute-start.17) | collective-permute-done | bytes 262176 | tf_op jit(solution)/shard_map/gather/ppermute | solution.py:29
  50.8 2.8 %collective-permute-done.14.refs_2_ = bf16[4,256,128]{2,1,0:T(8,128)(2,1)S(1)} collective-permute-done((bf16[4,256,128]{2,1,0:T(8,128)(2,1)S(1)}, bf16[4,256,128]{2,1,0:T(8,128)(2,1)S(1)}, u32[]{:S(2)}, u32[]{:S(2)}) %collective-permute-start.14) | collective-permute-done | bytes 262176 | tf_op jit(solution)/shard_map/gather/ppermute | solution.py:29
  53.7 0.3 collective-permute-start.20
  54.0 0.5 collective-permute-start.21
  54.5 0.6 part.1
  55.4 3.4 %dequant.4 = (bf16[64,128,256]{2,1,0:T(8,128)(2,1)S(1)}, bf16[64,128,128]{2,1,0:T(8,128)(2,1)S(1)}, s32[1]{0:T(128)}) custom-call(bf16[16,128,256]{2,1,0:T(8,128)(2,1)S(1)} %merge_c.1.refs_0_, s32[3,48,128,128]{3,2,1,0:T(8,128)S(1)} %copy-done, s32[3,48]{1,0:T(4,128)S(1)} %copy-done.4, s32[3]{0:T(128)S(1)} %copy-done.5, f32[3,3,48,128]{3,2,1,0:T(8,128)S(1)} %copy-done.1), custom_call_target="tpu_custom_call" | custom-call | flops 12000000 | bytes 10485760 | tf_op jit(solution)/shard_map/gather/dequant/pallas_call | solution.py:104
  58.8 3.1 %dequant.5 = (bf16[64,128,256]{2,1,0:T(8,128)(2,1)S(1)}, bf16[64,128,128]{2,1,0:T(8,128)(2,1)S(1)}, s32[1]{0:T(128)}) custom-call(bf16[16,128,256]{2,1,0:T(8,128)(2,1)S(1)} %merge_c.1.refs_0_, s32[3,48,128,128]{3,2,1,0:T(8,128)S(1)} %copy-done, s32[3,48]{1,0:T(4,128)S(1)} %copy-done.4, s32[3]{0:T(128)S(1)} %copy-done.5, f32[3,3,48,128]{3,2,1,0:T(8,128)S(1)} %copy-done.1), custom_call_target="tpu_custom_call" | custom-call | flops 12000000 | bytes 10485760 | tf_op jit(solution)/shard_map/gather/dequant/pallas_call | solution.py:104
  61.9 0.9 collective-permute-done.18.refs_4_.refs_1_
  62.8 2.8 %collective-permute-done.15.refs_3_.refs_0_ = bf16[4,256,128]{2,1,0:T(8,128)(2,1)S(1)} collective-permute-done((bf16[4,256,128]{2,1,0:T(8,128)(2,1)S(1)}, bf16[4,256,128]{2,1,0:T(8,128)(2,1)S(1)}, u32[]{:S(2)}, u32[]{:S(2)}) %collective-permute-start.15) | collective-permute-done | bytes 262176 | tf_op jit(solution)/shard_map/gather/ppermute | solution.py:29
  65.6 1.8 %pick.1 = bf16[4,256,128]{2,1,0:T(8,128)(2,1)S(1)} custom-call(s32[1]{0:T(128)} %get-tuple-element.42.refs_0_.refs_1_, s32[1]{0:T(128)} %get-tuple-element.43.refs_1_.refs_2_, s32[3]{0:T(128)S(1)} %pad_add_fusion.pos_ref.refs_1_.refs_2_.refs_3_, bf16[4,256,128]{2,1,0:T(8,128)(2,1)S(1)} %collective-permute-done.15.refs_3_.refs_0_, ...), custom_call_target="tpu_custom_call" | custom-call | bytes 786444 | tf_op jit(solution)/shard_map/gather/pick/pallas_call | solution.py:49
  67.7 0.5 collective-permute-start.12
  68.1 4.6 %gate_up.2 = (f32[3,256,256]{2,1,0:T(8,128)S(1)}, s32[1]{0:T(128)}) custom-call(s32[1]{0:T(128)} %get-tuple-element.47.refs_0_, s32[1]{0:T(128)} %get-tuple-element.42.refs_0_.refs_1_, s32[1]{0:T(128)} %get-tuple-element.43.refs_1_.refs_2_, s32[3]{0:T(128)S(1)} %pad_add_fusion.pos_ref.refs_1_.refs_2_.refs_3_, ...), custom_call_target="tpu_custom_call" | custom-call | flops 2013265920 | bytes 15990800 | tf_op jit(solution)/shard_map/gather/gate_up/pallas_call | solution.py:49
  72.8 1.9 %hidden.2.refs_2_ = f32[384,256]{1,0:T(8,128)S(1)} custom-call(s32[3]{0:T(128)S(1)} %pad_add_fusion.pos_ref.refs_1_.refs_2_.refs_3_, bf16[64,128,128]{2,1,0:T(8,128)(2,1)S(1)} %get-tuple-element.39.w0, bf16[64,128,128]{2,1,0:T(8,128)(2,1)S(1)} %get-tuple-element.40.w1, bf16[64,128,128]{2,1,0:T(8,128)(2,1)S(1)} %get-tuple-element.41.w2, ...), custom_call_target="tpu_custom_call" | custom-call | flops 1207959552 | bytes 9830412 | tf_op jit(solution)/shard_map/gather/hidden/pallas_call | solution.py:49
  74.8 0.3 collective-permute-done.19.refs_2_
  75.3 1.3 collective-permute-done.23.refs_3_
  76.6 2.2 %gate_up.3 = (f32[3,256,256]{2,1,0:T(8,128)S(1)}, s32[1]{0:T(128)}) custom-call(s32[3]{0:T(128)S(1)} %pad_add_fusion.pos_ref.refs_1_.refs_2_.refs_3_, bf16[64,128,256]{2,1,0:T(8,128)(2,1)S(1)} %get-tuple-element.48.refs_4_.w0, bf16[64,128,256]{2,1,0:T(8,128)(2,1)S(1)} %get-tuple-element.49.refs_5_.w1, ...), custom_call_target="tpu_custom_call" | custom-call | flops 1207959552 | bytes 15728656 | tf_op jit(solution)/shard_map/gather/gate_up/pallas_call | solution.py:49
  78.9 1.3 hidden.3
  80.2 1.5 %input_away.2 = bf16[16,128,256]{2,1,0:T(8,128)(2,1)S(1)} custom-call(s32[3]{0:T(128)S(1)} %pad_add_fusion.pos_ref.refs_1_.refs_2_.refs_3_, bf16[3,256,256]{2,1,0:T(8,128)(2,1)S(1)} %get-tuple-element.56.grad_ref, bf16[64,128,256]{2,1,0:T(8,128)(2,1)S(1)} %get-tuple-element.48.refs_4_.w0, bf16[64,128,256]{2,1,0:T(8,128)(2,1)S(1)} %get-tuple-element.49.refs_5_.w1, ...), custom_call_target="tpu_custom_call" | custom-call | flops 805306368 | bytes 14024716 | tf_op jit(solution)/shard_map/scatter/input_away/pallas_call | solution.py:49
  81.7 0.2 collective-permute-start.24
  81.9 1.5 %input_away.3 = bf16[16,128,256]{2,1,0:T(8,128)(2,1)S(1)} custom-call(s32[3]{0:T(128)S(1)} %pad_add_fusion.pos_ref.refs_1_.refs_2_.refs_3_, bf16[3,256,256]{2,1,0:T(8,128)(2,1)S(1)} %get-tuple-element.56.grad_ref, bf16[64,128,256]{2,1,0:T(8,128)(2,1)S(1)} %get-tuple-element.48.refs_4_.w0, bf16[64,128,256]{2,1,0:T(8,128)(2,1)S(1)} %get-tuple-element.49.refs_5_.w1, ...), custom_call_target="tpu_custom_call" | custom-call | flops 805306368 | bytes 14024716 | tf_op jit(solution)/shard_map/scatter/input_away/pallas_call | solution.py:49
  83.5 0.5 collective-permute-start.30
  83.9 0.5 collective-permute-done.24.refs_0_
  84.5 1.5 %input_here.2 = (bf16[4,128,256]{2,1,0:T(8,128)(2,1)S(1)}, bf16[4,128,256]{2,1,0:T(8,128)(2,1)S(1)}, f32[4,128,256]{2,1,0:T(8,128)S(1)}, f32[4,128,256]{2,1,0:T(8,128)S(1)}) custom-call(s32[3]{0:T(128)S(1)} %pad_add_fusion.pos_ref.refs_1_.refs_2_.refs_3_, bf16[3,256,256]{2,1,0:T(8,128)(2,1)S(1)} %get-tuple-element.56.grad_ref, ...), custom_call_target="tpu_custom_call" | custom-call | flops 805306368 | bytes 15597580 | tf_op jit(solution)/shard_map/scatter/input_here/pallas_call | solution.py:49
  86.0 1.9 %collective-permute-start.25 = (bf16[4,128,256]{2,1,0:T(8,128)(2,1)S(1)}, bf16[4,128,256]{2,1,0:T(8,128)(2,1)S(1)}, u32[]{:S(2)}, u32[]{:S(2)}) collective-permute-start(bf16[4,128,256]{2,1,0:T(8,128)(2,1)S(1)} %get-tuple-element.59), channel_id=1, source_target_pairs={{0,16},{1,17},{2,18},{3,19},{4,20},{5,21},{6,22},{7,23},{8,24},{9,... | collective-permute-start | bytes 786440 | tf_op jit(solution)/shard_map/scatter/ppermute | solution.py:29
  87.9 1.5 %input_here.3 = (bf16[4,128,256]{2,1,0:T(8,128)(2,1)S(1)}, bf16[4,128,256]{2,1,0:T(8,128)(2,1)S(1)}, f32[4,128,256]{2,1,0:T(8,128)S(1)}, f32[4,128,256]{2,1,0:T(8,128)S(1)}) custom-call(s32[3]{0:T(128)S(1)} %pad_add_fusion.pos_ref.refs_1_.refs_2_.refs_3_, bf16[3,256,256]{2,1,0:T(8,128)(2,1)S(1)} %get-tuple-element.56.grad_ref, ...), custom_call_target="tpu_custom_call" | custom-call | flops 805306368 | bytes 15597580 | tf_op jit(solution)/shard_map/scatter/input_here/pallas_call | solution.py:49
  89.4 0.3 collective-permute-start.32
  89.8 3.0 %collective-permute-start.31 = (bf16[4,128,256]{2,1,0:T(8,128)(2,1)S(1)}, bf16[4,128,256]{2,1,0:T(8,128)(2,1)S(1)}, u32[]{:S(2)}, u32[]{:S(2)}) collective-permute-start(bf16[4,128,256]{2,1,0:T(8,128)(2,1)S(1)} %get-tuple-element.64), channel_id=1, source_target_pairs={{0,16},{1,17},{2,18},{3,19},{4,20},{5,21},{6,22},{7,23},{8,24},{9,... | collective-permute-start | bytes 786440 | tf_op jit(solution)/shard_map/scatter/ppermute | solution.py:29
  92.8 2.4 %collective-permute-done.25.r = bf16[4,128,256]{2,1,0:T(8,128)(2,1)S(1)} collective-permute-done((bf16[4,128,256]{2,1,0:T(8,128)(2,1)S(1)}, bf16[4,128,256]{2,1,0:T(8,128)(2,1)S(1)}, u32[]{:S(2)}, u32[]{:S(2)}) %collective-permute-start.25) | collective-permute-done | bytes 262176 | tf_op jit(solution)/shard_map/scatter/ppermute | solution.py:29
  95.2 3.2 %collective-permute-start.26 = (bf16[4,128,256]{2,1,0:T(8,128)(2,1)S(1)}, bf16[4,128,256]{2,1,0:T(8,128)(2,1)S(1)}, u32[]{:S(2)}, u32[]{:S(2)}) collective-permute-start(bf16[4,128,256]{2,1,0:T(8,128)(2,1)S(1)} %add.17), channel_id=1, source_target_pairs={{0,16},{1,17},{2,18},{3,19},{4,20},{5,21},{6,22},{7,23},{8,24},{9,... | collective-permute-start | bytes 786440 | tf_op jit(solution)/shard_map/scatter/ppermute | solution.py:29
  98.4 0.4 collective-permute-done.32.r
  98.9 0.6 collective-permute-start.33
  99.5 1.6 %collective-permute-start.27 = (f32[384]{0:T(512)S(1)}, f32[384]{0:T(512)S(1)}, u32[]{:S(2)}, u32[]{:S(2)}) collective-permute-start(f32[384]{0:T(512)S(1)} %reduce), channel_id=1, source_target_pairs={{0,64},{64,0},{128,192},{192,128},{1,65},{65,1},{129,193},{193,129... | collective-permute-start | bytes 4616 | tf_op jit(solution)/shard_map/ia3/ppermute | solution.py:425
  101.0 2.1 %collective-permute-done.27 = f32[384]{0:T(512)S(1)} collective-permute-done((f32[384]{0:T(512)S(1)}, f32[384]{0:T(512)S(1)}, u32[]{:S(2)}, u32[]{:S(2)}) %collective-permute-start.27) | collective-permute-done | bytes 1568 | tf_op jit(solution)/shard_map/ia3/ppermute | solution.py:425
  103.1 2.8 %collective-permute-start.28 = (f32[384]{0:T(512)S(1)}, f32[384]{0:T(512)S(1)}, u32[]{:S(2)}, u32[]{:S(2)}) collective-permute-start(f32[384]{0:T(512)S(1)} %add.10), channel_id=1, source_target_pairs={{0,192},{192,0},{64,128},{128,64},{1,193},{193,1},{65,129},{129,65... | collective-permute-start | bytes 4616 | tf_op jit(solution)/shard_map/ia3/ppermute | solution.py:426
  105.9 2.0 %collective-permute-done.28 = f32[384]{0:T(512)S(1)} collective-permute-done((f32[384]{0:T(512)S(1)}, f32[384]{0:T(512)S(1)}, u32[]{:S(2)}, u32[]{:S(2)}) %collective-permute-start.28) | collective-permute-done | bytes 1568 | tf_op jit(solution)/shard_map/ia3/ppermute | solution.py:426
  107.9 0.6 add.11
  108.5 0.3 collective-permute-done.29.ra3
  108.9 2.8 %collective-permute-done.33.rb3 = bf16[4,128,256]{2,1,0:T(8,128)(2,1)S(1)} collective-permute-done((bf16[4,128,256]{2,1,0:T(8,128)(2,1)S(1)}, bf16[4,128,256]{2,1,0:T(8,128)(2,1)S(1)}, u32[]{:S(2)}, u32[]{:S(2)}) %collective-permute-start.33) | collective-permute-done | bytes 262176 | tf_op jit(solution)/shard_map/scatter/ppermute | solution.py:29
  111.7 0.7 y_sum.1
  112.4 20.1 %all_to_all.5.parts = bf16[8,128,256]{2,1,0:T(8,128)(2,1)S(1)} all-to-all(bf16[8,128,256]{2,1,0:T(8,128)(2,1)S(1)} %y_sum.1), channel_id=1, replica_groups={{0,2,4,6,8,10,12,14},{1,3,5,7,9,11,13,15},{16,18,20,22,24,26,28,30},{17..., dimensions={0} | all-to-all | bytes 1048576 | tf_op jit(solution)/shard_map/scatter/all_to_all | solution.py:444
  132.5 0.8 z_sum.1
  (48 shorter events, 1.4 us)
Async XLA Ops:
  0.6 35.6 %copy-start.1 = (f32[3,3,48,128]{3,2,1,0:T(8,128)S(1)}, f32[3,3,48,128]{3,2,1,0:T(8,128)}, u32[]{:S(2)}) copy-start(f32[3,3,48,128]{3,2,1,0:T(8,128)} %refs_4_.5) | copy-start | bytes 663556
  0.6 1.7 %collective-permute-start = (bf16[256,128]{1,0:T(8,128)(2,1)}, bf16[256,128]{1,0:T(8,128)(2,1)S(1)}, u32[]{:S(2)}, u32[]{:S(2)}) collective-permute-start(bf16[256,128]{1,0:T(8,128)(2,1)} %tok.1), channel_id=1, source_target_pairs={{0,1},{1,0},{2,3},{3,2},{4,5},{5,4},{6,7},{7,6},{8,9},{9,8},{10,11... | collective-permute-start | bytes 196616 | tf_op jit(solution)/shard_map/gather/ppermute | solution.py:29
  0.7 17.0 %collective-permute-start.3 = (bf16[256,128]{1,0:T(8,128)(2,1)}, bf16[256,128]{1,0:T(8,128)(2,1)S(1)}, u32[]{:S(2)}, u32[]{:S(2)}) collective-permute-start(bf16[256,128]{1,0:T(8,128)(2,1)} %tok.1), channel_id=1, source_target_pairs={{0,32},{1,33},{2,34},{3,35},{4,36},{5,37},{6,38},{7,39},{8,40},{9,... | collective-permute-start | bytes 196616 | tf_op jit(solution)/shard_map/gather/ppermute | solution.py:29
  2.1 1.5 %collective-permute-start.1 = (bf16[256,128]{1,0:T(8,128)(2,1)}, bf16[256,128]{1,0:T(8,128)(2,1)S(1)}, u32[]{:S(2)}, u32[]{:S(2)}) collective-permute-start(bf16[256,128]{1,0:T(8,128)(2,1)} %cot.1), channel_id=1, source_target_pairs={{0,1},{1,0},{2,3},{3,2},{4,5},{5,4},{6,7},{7,6},{8,9},{9,8},{10,11... | collective-permute-start | bytes 196616 | tf_op jit(solution)/shard_map/gather/ppermute | solution.py:29
  3.5 0.8 copy-start.2
  4.4 0.8 copy-start.3
  5.2 31.0 %copy-start.4 = (s32[3,48]{1,0:T(4,128)S(1)}, s32[3,48]{1,0:T(4,128)}, u32[]{:S(2)}) copy-start(s32[3,48]{1,0:T(4,128)} %refs_2_.5) | copy-start | bytes 1732
  5.2 31.0 %copy-start.5 = (s32[3]{0:T(128)S(1)}, s32[3]{0:T(128)}, u32[]{:S(2)}) copy-start(s32[3]{0:T(128)} %refs_3_.5) | copy-start | bytes 40
  6.3 12.0 %collective-permute-start.2 = (bf16[2,256,128]{2,1,0:T(8,128)(2,1)S(1)}, bf16[2,256,128]{2,1,0:T(8,128)(2,1)S(1)}, u32[]{:S(2)}, u32[]{:S(2)}) collective-permute-start(bf16[2,256,128]{2,1,0:T(8,128)(2,1)S(1)} %get-tuple-element.35.chip), channel_id=1, source_target_pairs={{0,16},{1,49},{2,18},{3,51},{4,20},{5,53},{6,22},{7,55},{8,24},{9,... | collective-permute-start | bytes 393224 | tf_op jit(solution)/shard_map/gather/ppermute | solution.py:29
  8.6 18.8 %collective-permute-start.5 = (bf16[2,128,256]{2,1,0:T(8,128)(2,1)S(1)}, bf16[2,128,256]{2,1,0:T(8,128)(2,1)S(1)}, u32[]{:S(2)}, u32[]{:S(2)}) collective-permute-start(bf16[2,128,256]{2,1,0:T(8,128)(2,1)S(1)} %get-tuple-element.37.refs_2_), channel_id=1, source_target_pairs={{0,2},{1,15},{2,4},{3,1},{4,6},{5,3},{6,8},{7,5},{8,10},{9,7},{10,... | collective-permute-start | bytes 393224 | tf_op jit(solution)/shard_map/gather/ppermute | solution.py:29
  10.5 16.9 %collective-permute-start.6 = (bf16[2,128,256]{2,1,0:T(8,128)(2,1)S(1)}, bf16[2,128,256]{2,1,0:T(8,128)(2,1)S(1)}, u32[]{:S(2)}, u32[]{:S(2)}) collective-permute-start(bf16[2,128,256]{2,1,0:T(8,128)(2,1)S(1)} %get-tuple-element.37.refs_2_), channel_id=1, source_target_pairs={{0,4},{1,13},{2,6},{3,15},{4,8},{5,1},{6,10},{7,3},{8,12},{9,5},{1... | collective-permute-start | bytes 393224 | tf_op jit(solution)/shard_map/gather/ppermute | solution.py:29
  13.7 14.2 %collective-permute-start.7 = (bf16[2,128,256]{2,1,0:T(8,128)(2,1)S(1)}, bf16[2,128,256]{2,1,0:T(8,128)(2,1)S(1)}, u32[]{:S(2)}, u32[]{:S(2)}) collective-permute-start(bf16[2,128,256]{2,1,0:T(8,128)(2,1)S(1)} %get-tuple-element.37.refs_2_), channel_id=1, source_target_pairs={{0,6},{1,11},{2,8},{3,13},{4,10},{5,15},{6,12},{7,1},{8,14},{9,3},... | collective-permute-start | bytes 393224 | tf_op jit(solution)/shard_map/gather/ppermute | solution.py:29
  17.8 9.6 %collective-permute-start.8 = (bf16[128,256]{1,0:T(8,128)(2,1)S(1)}, bf16[128,256]{1,0:T(8,128)(2,1)S(1)}, u32[]{:S(2)}, u32[]{:S(2)}) collective-permute-start(bf16[128,256]{1,0:T(8,128)(2,1)S(1)} %get-tuple-element.38), channel_id=1, source_target_pairs={{0,8},{1,9},{2,10},{3,11},{4,12},{5,13},{6,14},{7,15},{8,0},{9,1},... | collective-permute-start | bytes 196616 | tf_op jit(solution)/shard_map/gather/ppermute | solution.py:29
  28.0 2.8 %collective-permute-start.9 = (bf16[7,128,256]{2,1,0:T(8,128)(2,1)S(1)}, bf16[7,128,256]{2,1,0:T(8,128)(2,1)S(1)}, u32[]{:S(2)}, u32[]{:S(2)}) collective-permute-start(bf16[7,128,256]{2,1,0:T(8,128)(2,1)S(1)} %stack.21.refs_3_), channel_id=1, source_target_pairs={{0,1},{1,0},{2,3},{3,2},{4,5},{5,4},{6,7},{7,6},{8,9},{9,8},{10,11... | collective-permute-start | bytes 1376264 | tf_op jit(solution)/shard_map/gather/ppermute | solution.py:29
  28.1 2.1 %collective-permute-start.4 = (bf16[3,256,128]{2,1,0:T(8,128)(2,1)S(1)}, bf16[3,256,128]{2,1,0:T(8,128)(2,1)S(1)}, u32[]{:S(2)}, u32[]{:S(2)}) collective-permute-start(bf16[3,256,128]{2,1,0:T(8,128)(2,1)S(1)} %stack.20.mine.refs_0_), channel_id=1, source_target_pairs={{0,1},{1,0},{2,3},{3,2},{4,5},{5,4},{6,7},{7,6},{8,9},{9,8},{10,11... | collective-permute-start | bytes 589832 | tf_op jit(solution)/shard_map/gather/ppermute | solution.py:29
  31.4 22.6 %collective-permute-start.10 = (bf16[16,128,256]{2,1,0:T(8,128)(2,1)S(1)}, bf16[16,128,256]{2,1,0:T(8,128)(2,1)S(1)}, u32[]{:S(2)}, u32[]{:S(2)}) collective-permute-start(bf16[16,128,256]{2,1,0:T(8,128)(2,1)S(1)} %merge_c.1.refs_0_), channel_id=1, source_target_pairs={{0,16},{1,49},{2,18},{3,51},{4,20},{5,53},{6,22},{7,55},{8,24},{9,... | collective-permute-start | bytes 3145736 | tf_op jit(solution)/shard_map/gather/ppermute | solution.py:29
  32.6 10.6 %collective-permute-start.16 = (bf16[4,256,128]{2,1,0:T(8,128)(2,1)S(1)}, bf16[4,256,128]{2,1,0:T(8,128)(2,1)S(1)}, u32[]{:S(2)}, u32[]{:S(2)}) collective-permute-start(bf16[4,256,128]{2,1,0:T(8,128)(2,1)S(1)} %get-tuple-element.44.refs_8_), channel_id=1, source_target_pairs={{0,2},{1,15},{2,4},{3,1},{4,6},{5,3},{6,8},{7,5},{8,10},{9,7},{10,... | collective-permute-start | bytes 786440 | tf_op jit(solution)/shard_map/gather/ppermute | solution.py:29
  34.1 9.5 %collective-permute-start.13 = (bf16[4,256,128]{2,1,0:T(8,128)(2,1)S(1)}, bf16[4,256,128]{2,1,0:T(8,128)(2,1)S(1)}, u32[]{:S(2)}, u32[]{:S(2)}) collective-permute-start(bf16[4,256,128]{2,1,0:T(8,128)(2,1)S(1)} %get-tuple-element.36.refs_0_.refs_7_), channel_id=1, source_target_pairs={{0,2},{1,15},{2,4},{3,1},{4,6},{5,3},{6,8},{7,5},{8,10},{9,7},{10,... | collective-permute-start | bytes 786440 | tf_op jit(solution)/shard_map/gather/ppermute | solution.py:29
  36.2 3.7 %copy-start = (s32[3,48,128,128]{3,2,1,0:T(8,128)S(1)}, s32[3,48,128,128]{3,2,1,0:T(8,128)}, u32[]{:S(2)}) copy-start(s32[3,48,128,128]{3,2,1,0:T(8,128)} %refs_1_.5) | copy-start | bytes 28311556
  43.2 7.7 %collective-permute-start.17 = (bf16[4,256,128]{2,1,0:T(8,128)(2,1)S(1)}, bf16[4,256,128]{2,1,0:T(8,128)(2,1)S(1)}, u32[]{:S(2)}, u32[]{:S(2)}) collective-permute-start(bf16[4,256,128]{2,1,0:T(8,128)(2,1)S(1)} %collective-permute-done.16.refs_1_), channel_id=1, source_target_pairs={{0,2},{1,15},{2,4},{3,1},{4,6},{5,3},{6,8},{7,5},{8,10},{9,7},{10,... | collective-permute-start | bytes 786440 | tf_op jit(solution)/shard_map/gather/ppermute | solution.py:29
  43.6 10.1 %collective-permute-start.14 = (bf16[4,256,128]{2,1,0:T(8,128)(2,1)S(1)}, bf16[4,256,128]{2,1,0:T(8,128)(2,1)S(1)}, u32[]{:S(2)}, u32[]{:S(2)}) collective-permute-start(bf16[4,256,128]{2,1,0:T(8,128)(2,1)S(1)} %collective-permute-done.13.refs_0_), channel_id=1, source_target_pairs={{0,2},{1,15},{2,4},{3,1},{4,6},{5,3},{6,8},{7,5},{8,10},{9,7},{10,... | collective-permute-start | bytes 786440 | tf_op jit(solution)/shard_map/gather/ppermute | solution.py:29
  53.7 14.4 %collective-permute-start.20 = (bf16[16,256,128]{2,1,0:T(8,128)(2,1)S(1)}, bf16[16,256,128]{2,1,0:T(8,128)(2,1)S(1)}, u32[]{:S(2)}, u32[]{:S(2)}) collective-permute-start(bf16[16,256,128]{2,1,0:T(8,128)(2,1)S(1)} %stack.22.refs_9_), channel_id=1, source_target_pairs={{0,1},{1,0},{2,3},{3,2},{4,5},{5,4},{6,7},{7,6},{8,9},{9,8},{10,11... | collective-permute-start | bytes 3145736 | tf_op jit(solution)/shard_map/gather/ppermute | solution.py:29
  54.0 18.8 %collective-permute-start.21 = (bf16[16,128,256]{2,1,0:T(8,128)(2,1)S(1)}, bf16[16,128,256]{2,1,0:T(8,128)(2,1)S(1)}, u32[]{:S(2)}, u32[]{:S(2)}) collective-permute-start(bf16[16,128,256]{2,1,0:T(8,128)(2,1)S(1)} %collective-permute-done.10.a.refs_1_), channel_id=1, source_target_pairs={{0,1},{1,0},{2,3},{3,2},{4,5},{5,4},{6,7},{7,6},{8,9},{9,8},{10,11... | collective-permute-start | bytes 3145736 | tf_op jit(solution)/shard_map/gather/ppermute | solution.py:29
  55.1 12.6 %collective-permute-start.11 = (bf16[8,128,256]{2,1,0:T(8,128)(2,1)S(1)}, bf16[8,128,256]{2,1,0:T(8,128)(2,1)S(1)}, u32[]{:S(2)}, u32[]{:S(2)}) collective-permute-start(bf16[8,128,256]{2,1,0:T(8,128)(2,1)S(1)} %part.1), channel_id=1, source_target_pairs={{0,16},{1,49},{2,18},{3,51},{4,20},{5,53},{6,22},{7,55},{8,24},{9,... | collective-permute-start | bytes 1572872 | tf_op jit(solution)/shard_map/gather/ppermute | solution.py:29
  55.2 7.6 %collective-permute-start.18 = (bf16[4,256,128]{2,1,0:T(8,128)(2,1)S(1)}, bf16[4,256,128]{2,1,0:T(8,128)(2,1)S(1)}, u32[]{:S(2)}, u32[]{:S(2)}) collective-permute-start(bf16[4,256,128]{2,1,0:T(8,128)(2,1)S(1)} %collective-permute-done.17.refs_3_), channel_id=1, source_target_pairs={{0,2},{1,15},{2,4},{3,1},{4,6},{5,3},{6,8},{7,5},{8,10},{9,7},{10,... | collective-permute-start | bytes 786440 | tf_op jit(solution)/shard_map/gather/ppermute | solution.py:29
  55.3 10.4 %collective-permute-start.15 = (bf16[4,256,128]{2,1,0:T(8,128)(2,1)S(1)}, bf16[4,256,128]{2,1,0:T(8,128)(2,1)S(1)}, u32[]{:S(2)}, u32[]{:S(2)}) collective-permute-start(bf16[4,256,128]{2,1,0:T(8,128)(2,1)S(1)} %collective-permute-done.14.refs_2_), channel_id=1, source_target_pairs={{0,2},{1,15},{2,4},{3,1},{4,6},{5,3},{6,8},{7,5},{8,10},{9,7},{10,... | collective-permute-start | bytes 786440 | tf_op jit(solution)/shard_map/gather/ppermute | solution.py:29
  67.4 7.7 %collective-permute-start.19 = (bf16[4,256,128]{2,1,0:T(8,128)(2,1)S(1)}, bf16[4,256,128]{2,1,0:T(8,128)(2,1)S(1)}, u32[]{:S(2)}, u32[]{:S(2)}) collective-permute-start(bf16[4,256,128]{2,1,0:T(8,128)(2,1)S(1)} %pick.1), channel_id=1, source_target_pairs={{0,2},{1,15},{2,4},{3,1},{4,6},{5,3},{6,8},{7,5},{8,10},{9,7},{10,... | collective-permute-start | bytes 786440 | tf_op jit(solution)/shard_map/gather/ppermute | solution.py:29
  67.5 7.8 %collective-permute-start.22 = (bf16[8,256,128]{2,1,0:T(8,128)(2,1)S(1)}, bf16[8,256,128]{2,1,0:T(8,128)(2,1)S(1)}, u32[]{:S(2)}, u32[]{:S(2)}) collective-permute-start(bf16[8,256,128]{2,1,0:T(8,128)(2,1)S(1)} %stack.23.refs_0_), channel_id=1, source_target_pairs={{0,1},{1,0},{2,3},{3,2},{4,5},{5,4},{6,7},{7,6},{8,9},{9,8},{10,11... | collective-permute-start | bytes 1572872 | tf_op jit(solution)/shard_map/gather/ppermute | solution.py:29
  67.7 11.2 %collective-permute-start.12 = (bf16[8,128,256]{2,1,0:T(8,128)(2,1)S(1)}, bf16[8,128,256]{2,1,0:T(8,128)(2,1)S(1)}, u32[]{:S(2)}, u32[]{:S(2)}) collective-permute-start(bf16[8,128,256]{2,1,0:T(8,128)(2,1)S(1)} %collective-permute-done.11.refs_0_), channel_id=1, source_target_pairs={{0,1},{1,0},{2,3},{3,2},{4,5},{5,4},{6,7},{7,6},{8,9},{9,8},{10,11... | collective-permute-start | bytes 1572872 | tf_op jit(solution)/shard_map/gather/ppermute | solution.py:29
  72.8 2.4 %copy-start.6 = (f32[384]{0:T(512)S(1)}, f32[384]{0:T(512)}, u32[]{:S(2)}) copy-start(f32[384]{0:T(512)} %param.13) | copy-start | bytes 4612
  75.1 1.5 %collective-permute-start.23 = (bf16[4,256,128]{2,1,0:T(8,128)(2,1)S(1)}, bf16[4,256,128]{2,1,0:T(8,128)(2,1)S(1)}, u32[]{:S(2)}, u32[]{:S(2)}) collective-permute-start(bf16[4,256,128]{2,1,0:T(8,128)(2,1)S(1)} %collective-permute-done.19.refs_2_), channel_id=1, source_target_pairs={{0,1},{1,0},{2,3},{3,2},{4,5},{5,4},{6,7},{7,6},{8,9},{9,8},{10,11... | collective-permute-start | bytes 786440 | tf_op jit(solution)/shard_map/gather/ppermute | solution.py:29
  81.7 2.7 %collective-permute-start.24 = (bf16[16,128,256]{2,1,0:T(8,128)(2,1)S(1)}, bf16[16,128,256]{2,1,0:T(8,128)(2,1)S(1)}, u32[]{:S(2)}, u32[]{:S(2)}) collective-permute-start(bf16[16,128,256]{2,1,0:T(8,128)(2,1)S(1)} %input_away.2), channel_id=1, source_target_pairs={{0,1},{1,0},{2,3},{3,2},{4,5},{5,4},{6,7},{7,6},{8,9},{9,8},{10,11... | collective-permute-start | bytes 3145736 | tf_op jit(solution)/shard_map/scatter/ppermute | solution.py:29
  83.5 4.5 %collective-permute-start.30 = (bf16[16,128,256]{2,1,0:T(8,128)(2,1)S(1)}, bf16[16,128,256]{2,1,0:T(8,128)(2,1)S(1)}, u32[]{:S(2)}, u32[]{:S(2)}) collective-permute-start(bf16[16,128,256]{2,1,0:T(8,128)(2,1)S(1)} %input_away.3), channel_id=1, source_target_pairs={{0,1},{1,0},{2,3},{3,2},{4,5},{5,4},{6,7},{7,6},{8,9},{9,8},{10,11... | collective-permute-start | bytes 3145736 | tf_op jit(solution)/shard_map/scatter/ppermute | solution.py:29
  86.0 9.2 %collective-permute-start.25 = (bf16[4,128,256]{2,1,0:T(8,128)(2,1)S(1)}, bf16[4,128,256]{2,1,0:T(8,128)(2,1)S(1)}, u32[]{:S(2)}, u32[]{:S(2)}) collective-permute-start(bf16[4,128,256]{2,1,0:T(8,128)(2,1)S(1)} %get-tuple-element.59), channel_id=1, source_target_pairs={{0,16},{1,17},{2,18},{3,19},{4,20},{5,21},{6,22},{7,23},{8,24},{9,... | collective-permute-start | bytes 786440 | tf_op jit(solution)/shard_map/scatter/ppermute | solution.py:29
  89.4 9.4 %collective-permute-start.32 = (bf16[4,128,256]{2,1,0:T(8,128)(2,1)S(1)}, bf16[4,128,256]{2,1,0:T(8,128)(2,1)S(1)}, u32[]{:S(2)}, u32[]{:S(2)}) collective-permute-start(bf16[4,128,256]{2,1,0:T(8,128)(2,1)S(1)} %get-tuple-element.66), channel_id=1, source_target_pairs={{0,48},{1,49},{2,50},{3,51},{4,52},{5,53},{6,54},{7,55},{8,56},{9,... | collective-permute-start | bytes 786440 | tf_op jit(solution)/shard_map/scatter/ppermute | solution.py:29
  89.8 18.8 %collective-permute-start.31 = (bf16[4,128,256]{2,1,0:T(8,128)(2,1)S(1)}, bf16[4,128,256]{2,1,0:T(8,128)(2,1)S(1)}, u32[]{:S(2)}, u32[]{:S(2)}) collective-permute-start(bf16[4,128,256]{2,1,0:T(8,128)(2,1)S(1)} %get-tuple-element.64), channel_id=1, source_target_pairs={{0,16},{1,17},{2,18},{3,19},{4,20},{5,21},{6,22},{7,23},{8,24},{9,... | collective-permute-start | bytes 786440 | tf_op jit(solution)/shard_map/scatter/ppermute | solution.py:29
  95.2 13.3 %collective-permute-start.26 = (bf16[4,128,256]{2,1,0:T(8,128)(2,1)S(1)}, bf16[4,128,256]{2,1,0:T(8,128)(2,1)S(1)}, u32[]{:S(2)}, u32[]{:S(2)}) collective-permute-start(bf16[4,128,256]{2,1,0:T(8,128)(2,1)S(1)} %add.17), channel_id=1, source_target_pairs={{0,16},{1,17},{2,18},{3,19},{4,20},{5,21},{6,22},{7,23},{8,24},{9,... | collective-permute-start | bytes 786440 | tf_op jit(solution)/shard_map/scatter/ppermute | solution.py:29
  98.4 10.5 %collective-permute-start.29 = (bf16[4,128,256]{2,1,0:T(8,128)(2,1)S(1)}, bf16[4,128,256]{2,1,0:T(8,128)(2,1)S(1)}, u32[]{:S(2)}, u32[]{:S(2)}) collective-permute-start(bf16[4,128,256]{2,1,0:T(8,128)(2,1)S(1)} %get-tuple-element.62), channel_id=1, source_target_pairs={{0,48},{1,49},{2,50},{3,51},{4,52},{5,53},{6,54},{7,55},{8,56},{9,... | collective-permute-start | bytes 786440 | tf_op jit(solution)/shard_map/scatter/ppermute | solution.py:29
  98.9 12.8 %collective-permute-start.33 = (bf16[4,128,256]{2,1,0:T(8,128)(2,1)S(1)}, bf16[4,128,256]{2,1,0:T(8,128)(2,1)S(1)}, u32[]{:S(2)}, u32[]{:S(2)}) collective-permute-start(bf16[4,128,256]{2,1,0:T(8,128)(2,1)S(1)} %add.18), channel_id=1, source_target_pairs={{0,48},{1,49},{2,50},{3,51},{4,52},{5,53},{6,54},{7,55},{8,56},{9,... | collective-permute-start | bytes 786440 | tf_op jit(solution)/shard_map/scatter/ppermute | solution.py:29
  99.5 3.7 %collective-permute-start.27 = (f32[384]{0:T(512)S(1)}, f32[384]{0:T(512)S(1)}, u32[]{:S(2)}, u32[]{:S(2)}) collective-permute-start(f32[384]{0:T(512)S(1)} %reduce), channel_id=1, source_target_pairs={{0,64},{64,0},{128,192},{192,128},{1,65},{65,1},{129,193},{193,129... | collective-permute-start | bytes 4616 | tf_op jit(solution)/shard_map/ia3/ppermute | solution.py:425
  103.1 4.8 %collective-permute-start.28 = (f32[384]{0:T(512)S(1)}, f32[384]{0:T(512)S(1)}, u32[]{:S(2)}, u32[]{:S(2)}) collective-permute-start(f32[384]{0:T(512)S(1)} %add.10), channel_id=1, source_target_pairs={{0,192},{192,0},{64,128},{128,64},{1,193},{193,1},{65,129},{129,65... | collective-permute-start | bytes 4616 | tf_op jit(solution)/shard_map/ia3/ppermute | solution.py:426

commit v3 on v2

--- a/solution.py
+++ b/solution.py
@@ -363,9 +363,9 @@
         sib_t = swap(tokens)
         sib_c = swap(cotangent)
         chip_t, chip_c, own_c = own(pos, tokens, cotangent, sib_t, sib_c)
-        near_t = stack([send(chip_t, dy=1, signed=True), send(tokens, dy=2)])
+        near_t = stack([send(chip_t, dy=1, signed=True), send(tokens, dy=2)], after=(weight_codes,))
         t0, t1 = call(merge_t_kernel, "merge_t", (pos, chip_t, near_t, swap(near_t)), [array((4, 256, 128), BF16)] * 2)
-        near_c = stack([send(chip_c, dz=d, signed=True) for d in (1, 2, 3)] + [send(own_c, dz=4)], after=(near_t,))
+        near_c = stack([send(chip_c, dz=d, signed=True) for d in (1, 2, 3)] + [send(own_c, dz=4)], after=(near_t, weight_codes))
         c0 = call(
             merge_c_kernel, "merge_c", (pos, chip_c, near_c, swap(near_c)), [array((16, 128, 256), BF16)],
             after=(t0,),

time: 134 us -> 131 us (0.978)
  waiting for transfers between devices: 38.3 us -> 33.2 us
  starting transfers between devices: 35.5 us -> 37.6 us
    ppermute x32, waiting for transfers between devices: 34.2 us -> 29.1 us  [send(): return lax.ppermute(a, 'mp', pairs)]
    ppermute x32, starting transfers between devices: 31.2 us -> 33.2 us  [send(): return lax.ppermute(a, 'mp', pairs)]
    unnamed x14 -> x20, local copies, waits for them, and re-layouts: 5.37 us -> 5.4 us
  transfers between devices with their start and end apart: 34 -> 34, of which waited for: 17 -> 18; matrix products, arithmetic and copies ran while one was open for 1% -> 1% of each run, Pallas kernels for 20% -> 21%
where the time goes in v3:
time: 131 us; the launch traced here: 130 us
  starting transfers between devices  37.6 us (29%)
  waiting for transfers between devices  33.2 us (25%)
  Pallas kernels  33 us (25%)
  blocking collectives  19.4 us (15%)
  local copies, waits for them, and re-layouts  5.5 us (4%)
    ppermute x32, starting transfers between devices, send(): return lax.ppermute(a, 'mp', pairs)  33.2 us
    ppermute x32, waiting for transfers between devices, send(): return lax.ppermute(a, 'mp', pairs)  29.1 us
    pallas_call x20, Pallas kernels, call(): pl.pallas_call((lambda *refs: kernel(*refs[skip:])) if skip else kernel,...  21.7 us
    all_to_all x1, blocking collectives, on_device(): lax.all_to_all(total, 'mp', 0, 0, axis_index_groups=columns, tiled=True)  19.4 us
    pallas_call x3, Pallas kernels, dequant(): pl.pallas_call((lambda *refs: kernel(*refs[skip:])) if skip else kernel,...  10.2 us
    unnamed x20, local copies, waits for them, and re-layouts  5.4 us
    ppermute x1, starting transfers between devices, on_device(): lax.ppermute(ia3_part, 'dp', [(0, 3), (3, 0), (1, 2), (2, 1)])  2.76 us
  transfers between devices with their start and end apart: 34, of which 18 were waited for; matrix products, arithmetic and copies ran while one was open for 1% of the time, Pallas kernels for 21%

profile of v3, /device:TPU:24, one launch (start us, length us, event | category | flops | bytes accessed | tf_op | source)
XLA Modules:
  0.0 130.3 jit_solution(15072972941451810189)
XLA Ops:
  0.7 0.5 collective-permute-start.1
  1.3 0.9 collective-permute-done.sib_t
  2.3 0.8 copy-done.2
  3.2 0.8 copy-done.3
  4.0 1.1 own.1
  5.1 2.0 %collective-permute-start.2 = (bf16[2,256,128]{2,1,0:T(8,128)(2,1)S(1)}, bf16[2,256,128]{2,1,0:T(8,128)(2,1)S(1)}, u32[]{:S(2)}, u32[]{:S(2)}) collective-permute-start(bf16[2,256,128]{2,1,0:T(8,128)(2,1)S(1)} %get-tuple-element.35.chip), channel_id=1, source_target_pairs={{0,16},{1,49},{2,18},{3,51},{4,20},{5,53},{6,22},{7,55},{8,24},{9,... | collective-permute-start | bytes 393224 | tf_op jit(solution)/shard_map/gather/ppermute | solution.py:29
  7.1 0.9 collective-permute-start.3
  8.0 1.9 %collective-permute-start.5 = (bf16[2,128,256]{2,1,0:T(8,128)(2,1)S(1)}, bf16[2,128,256]{2,1,0:T(8,128)(2,1)S(1)}, u32[]{:S(2)}, u32[]{:S(2)}) collective-permute-start(bf16[2,128,256]{2,1,0:T(8,128)(2,1)S(1)} %get-tuple-element.37.refs_2_), channel_id=1, source_target_pairs={{0,2},{1,15},{2,4},{3,1},{4,6},{5,3},{6,8},{7,5},{8,10},{9,7},{10,... | collective-permute-start | bytes 393224 | tf_op jit(solution)/shard_map/gather/ppermute | solution.py:29
  9.9 3.3 %collective-permute-start.6 = (bf16[2,128,256]{2,1,0:T(8,128)(2,1)S(1)}, bf16[2,128,256]{2,1,0:T(8,128)(2,1)S(1)}, u32[]{:S(2)}, u32[]{:S(2)}) collective-permute-start(bf16[2,128,256]{2,1,0:T(8,128)(2,1)S(1)} %get-tuple-element.37.refs_2_), channel_id=1, source_target_pairs={{0,4},{1,13},{2,6},{3,15},{4,8},{5,1},{6,10},{7,3},{8,12},{9,5},{1... | collective-permute-start | bytes 393224 | tf_op jit(solution)/shard_map/gather/ppermute | solution.py:29
  13.2 4.0 %collective-permute-start.7 = (bf16[2,128,256]{2,1,0:T(8,128)(2,1)S(1)}, bf16[2,128,256]{2,1,0:T(8,128)(2,1)S(1)}, u32[]{:S(2)}, u32[]{:S(2)}) collective-permute-start(bf16[2,128,256]{2,1,0:T(8,128)(2,1)S(1)} %get-tuple-element.37.refs_2_), channel_id=1, source_target_pairs={{0,6},{1,11},{2,8},{3,13},{4,10},{5,15},{6,12},{7,1},{8,14},{9,3},... | collective-permute-start | bytes 393224 | tf_op jit(solution)/shard_map/gather/ppermute | solution.py:29
  17.2 1.6 %collective-permute-start.8 = (bf16[128,256]{1,0:T(8,128)(2,1)S(1)}, bf16[128,256]{1,0:T(8,128)(2,1)S(1)}, u32[]{:S(2)}, u32[]{:S(2)}) collective-permute-start(bf16[128,256]{1,0:T(8,128)(2,1)S(1)} %get-tuple-element.38), channel_id=1, source_target_pairs={{0,8},{1,9},{2,10},{3,11},{4,12},{5,13},{6,14},{7,15},{8,0},{9,1},... | collective-permute-start | bytes 196616 | tf_op jit(solution)/shard_map/gather/ppermute | solution.py:29
  18.8 3.7 %copy-done = s32[3,48,128,128]{3,2,1,0:T(8,128)S(1)} copy-done((s32[3,48,128,128]{3,2,1,0:T(8,128)S(1)}, s32[3,48,128,128]{3,2,1,0:T(8,128)}, u32[]{:S(2)}) %copy-start) | copy-done | bytes 9437208
  22.5 4.3 %collective-permute-done.8.refs_5_ = bf16[128,256]{1,0:T(8,128)(2,1)S(1)} collective-permute-done((bf16[128,256]{1,0:T(8,128)(2,1)S(1)}, bf16[128,256]{1,0:T(8,128)(2,1)S(1)}, u32[]{:S(2)}, u32[]{:S(2)}) %collective-permute-start.8) | collective-permute-done | bytes 65568 | tf_op jit(solution)/shard_map/gather/ppermute | solution.py:29
  26.9 1.0 collective-permute-done.7.refs_4_
  28.0 0.5 collective-permute-start.4
  28.5 1.6 %collective-permute-done.4.other = bf16[3,256,128]{2,1,0:T(8,128)(2,1)S(1)} collective-permute-done((bf16[3,256,128]{2,1,0:T(8,128)(2,1)S(1)}, bf16[3,256,128]{2,1,0:T(8,128)(2,1)S(1)}, u32[]{:S(2)}, u32[]{:S(2)}) %collective-permute-start.4) | collective-permute-done | bytes 196640 | tf_op jit(solution)/shard_map/gather/ppermute | solution.py:29
  30.1 0.6 merge_t.1
  30.7 0.6 merge_c.1.refs_0_
  31.3 1.8 %collective-permute-start.10 = (bf16[16,128,256]{2,1,0:T(8,128)(2,1)S(1)}, bf16[16,128,256]{2,1,0:T(8,128)(2,1)S(1)}, u32[]{:S(2)}, u32[]{:S(2)}) collective-permute-start(bf16[16,128,256]{2,1,0:T(8,128)(2,1)S(1)} %merge_c.1.refs_0_), channel_id=1, source_target_pairs={{0,16},{1,49},{2,18},{3,51},{4,20},{5,53},{6,22},{7,55},{8,24},{9,... | collective-permute-start | bytes 3145736 | tf_op jit(solution)/shard_map/gather/ppermute | solution.py:29
  33.1 1.5 %collective-permute-start.16 = (bf16[4,256,128]{2,1,0:T(8,128)(2,1)S(1)}, bf16[4,256,128]{2,1,0:T(8,128)(2,1)S(1)}, u32[]{:S(2)}, u32[]{:S(2)}) collective-permute-start(bf16[4,256,128]{2,1,0:T(8,128)(2,1)S(1)} %get-tuple-element.44.refs_8_), channel_id=1, source_target_pairs={{0,2},{1,15},{2,4},{3,1},{4,6},{5,3},{6,8},{7,5},{8,10},{9,7},{10,... | collective-permute-start | bytes 786440 | tf_op jit(solution)/shard_map/gather/ppermute | solution.py:29
  34.7 2.2 %collective-permute-start.13 = (bf16[4,256,128]{2,1,0:T(8,128)(2,1)S(1)}, bf16[4,256,128]{2,1,0:T(8,128)(2,1)S(1)}, u32[]{:S(2)}, u32[]{:S(2)}) collective-permute-start(bf16[4,256,128]{2,1,0:T(8,128)(2,1)S(1)} %get-tuple-element.36.refs_0_.refs_7_), channel_id=1, source_target_pairs={{0,2},{1,15},{2,4},{3,1},{4,6},{5,3},{6,8},{7,5},{8,10},{9,7},{10,... | collective-permute-start | bytes 786440 | tf_op jit(solution)/shard_map/gather/ppermute | solution.py:29
  36.9 3.0 %dequant.3 = (bf16[64,128,256]{2,1,0:T(8,128)(2,1)S(1)}, bf16[64,128,128]{2,1,0:T(8,128)(2,1)S(1)}, s32[1]{0:T(128)}) custom-call(bf16[16,128,256]{2,1,0:T(8,128)(2,1)S(1)} %merge_c.1.refs_0_, s32[3,48,128,128]{3,2,1,0:T(8,128)S(1)} %bitcast.4, s32[3,48]{1,0:T(4,128)S(1)} %copy-done.4, s32[3]{0:T(128)S(1)} %copy-done.5, f32[3,3,48,128]{3,2,1,0:T(8,128)S(1)} %copy-done.1), custom_call_target="tpu_custom_call" | custom-call | flops 12000000 | bytes 10485760 | tf_op jit(solution)/shard_map/gather/dequant/pallas_call | solution.py:104
  39.9 0.9 collective-permute-done.16.refs_1_
  40.7 0.3 collective-permute-start.17
  41.1 2.5 %collective-permute-done.13.refs_0_ = bf16[4,256,128]{2,1,0:T(8,128)(2,1)S(1)} collective-permute-done((bf16[4,256,128]{2,1,0:T(8,128)(2,1)S(1)}, bf16[4,256,128]{2,1,0:T(8,128)(2,1)S(1)}, u32[]{:S(2)}, u32[]{:S(2)}) %collective-permute-start.13) | collective-permute-done | bytes 262176 | tf_op jit(solution)/shard_map/gather/ppermute | solution.py:29
  43.5 0.3 collective-permute-start.14
  43.9 4.4 %collective-permute-done.17.refs_3_ = bf16[4,256,128]{2,1,0:T(8,128)(2,1)S(1)} collective-permute-done((bf16[4,256,128]{2,1,0:T(8,128)(2,1)S(1)}, bf16[4,256,128]{2,1,0:T(8,128)(2,1)S(1)}, u32[]{:S(2)}, u32[]{:S(2)}) %collective-permute-start.17) | collective-permute-done | bytes 262176 | tf_op jit(solution)/shard_map/gather/ppermute | solution.py:29
  48.3 2.8 %collective-permute-done.14.refs_2_ = bf16[4,256,128]{2,1,0:T(8,128)(2,1)S(1)} collective-permute-done((bf16[4,256,128]{2,1,0:T(8,128)(2,1)S(1)}, bf16[4,256,128]{2,1,0:T(8,128)(2,1)S(1)}, u32[]{:S(2)}, u32[]{:S(2)}) %collective-permute-start.14) | collective-permute-done | bytes 262176 | tf_op jit(solution)/shard_map/gather/ppermute | solution.py:29
  51.2 0.3 collective-permute-start.20
  51.5 0.5 collective-permute-start.21
  52.0 0.6 part.1
  52.7 1.3 collective-permute-start.15
  54.0 3.7 %dequant.4 = (bf16[64,128,256]{2,1,0:T(8,128)(2,1)S(1)}, bf16[64,128,128]{2,1,0:T(8,128)(2,1)S(1)}, s32[1]{0:T(128)}) custom-call(bf16[16,128,256]{2,1,0:T(8,128)(2,1)S(1)} %merge_c.1.refs_0_, s32[3,48,128,128]{3,2,1,0:T(8,128)S(1)} %bitcast.4, s32[3,48]{1,0:T(4,128)S(1)} %copy-done.4, s32[3]{0:T(128)S(1)} %copy-done.5, f32[3,3,48,128]{3,2,1,0:T(8,128)S(1)} %copy-done.1), custom_call_target="tpu_custom_call" | custom-call | flops 12000000 | bytes 10485760 | tf_op jit(solution)/shard_map/gather/dequant/pallas_call | solution.py:104
  57.7 3.6 %dequant.5 = (bf16[64,128,256]{2,1,0:T(8,128)(2,1)S(1)}, bf16[64,128,128]{2,1,0:T(8,128)(2,1)S(1)}, s32[1]{0:T(128)}) custom-call(bf16[16,128,256]{2,1,0:T(8,128)(2,1)S(1)} %merge_c.1.refs_0_, s32[3,48,128,128]{3,2,1,0:T(8,128)S(1)} %bitcast.4, s32[3,48]{1,0:T(4,128)S(1)} %copy-done.4, s32[3]{0:T(128)S(1)} %copy-done.5, f32[3,3,48,128]{3,2,1,0:T(8,128)S(1)} %copy-done.1), custom_call_target="tpu_custom_call" | custom-call | flops 12000000 | bytes 10485760 | tf_op jit(solution)/shard_map/gather/dequant/pallas_call | solution.py:104
  61.3 1.8 %collective-permute-done.15.refs_3_.refs_0_ = bf16[4,256,128]{2,1,0:T(8,128)(2,1)S(1)} collective-permute-done((bf16[4,256,128]{2,1,0:T(8,128)(2,1)S(1)}, bf16[4,256,128]{2,1,0:T(8,128)(2,1)S(1)}, u32[]{:S(2)}, u32[]{:S(2)}) %collective-permute-start.15) | collective-permute-done | bytes 262176 | tf_op jit(solution)/shard_map/gather/ppermute | solution.py:29
  63.1 1.9 %pick.1 = bf16[4,256,128]{2,1,0:T(8,128)(2,1)S(1)} custom-call(s32[1]{0:T(128)} %get-tuple-element.42.refs_0_.refs_1_, s32[1]{0:T(128)} %get-tuple-element.43.refs_1_.refs_2_, s32[3]{0:T(128)S(1)} %pad_add_fusion.pos_ref.refs_1_.refs_2_.refs_3_, bf16[4,256,128]{2,1,0:T(8,128)(2,1)S(1)} %collective-permute-done.15.refs_3_.refs_0_, ...), custom_call_target="tpu_custom_call" | custom-call | bytes 786444 | tf_op jit(solution)/shard_map/gather/pick/pallas_call | solution.py:49
  65.3 0.5 collective-permute-start.12
  65.7 4.7 %gate_up.2 = (f32[3,256,256]{2,1,0:T(8,128)S(1)}, s32[1]{0:T(128)}) custom-call(s32[1]{0:T(128)} %get-tuple-element.47.refs_0_, s32[1]{0:T(128)} %get-tuple-element.42.refs_0_.refs_1_, s32[1]{0:T(128)} %get-tuple-element.43.refs_1_.refs_2_, s32[3]{0:T(128)S(1)} %pad_add_fusion.pos_ref.refs_1_.refs_2_.refs_3_, ...), custom_call_target="tpu_custom_call" | custom-call | flops 2013265920 | bytes 15990800 | tf_op jit(solution)/shard_map/gather/gate_up/pallas_call | solution.py:49
  70.5 1.9 %hidden.2.refs_2_ = f32[384,256]{1,0:T(8,128)S(1)} custom-call(s32[3]{0:T(128)S(1)} %pad_add_fusion.pos_ref.refs_1_.refs_2_.refs_3_, bf16[64,128,128]{2,1,0:T(8,128)(2,1)S(1)} %get-tuple-element.39.w0, bf16[64,128,128]{2,1,0:T(8,128)(2,1)S(1)} %get-tuple-element.40.w1, bf16[64,128,128]{2,1,0:T(8,128)(2,1)S(1)} %get-tuple-element.41.w2, ...), custom_call_target="tpu_custom_call" | custom-call | flops 1207959552 | bytes 9830412 | tf_op jit(solution)/shard_map/gather/hidden/pallas_call | solution.py:49
  73.0 1.3 collective-permute-done.23.refs_3_
  74.3 2.3 %gate_up.3 = (f32[3,256,256]{2,1,0:T(8,128)S(1)}, s32[1]{0:T(128)}) custom-call(s32[3]{0:T(128)S(1)} %pad_add_fusion.pos_ref.refs_1_.refs_2_.refs_3_, bf16[64,128,256]{2,1,0:T(8,128)(2,1)S(1)} %get-tuple-element.48.refs_4_.w0, bf16[64,128,256]{2,1,0:T(8,128)(2,1)S(1)} %get-tuple-element.49.refs_5_.w1, ...), custom_call_target="tpu_custom_call" | custom-call | flops 1207959552 | bytes 15728656 | tf_op jit(solution)/shard_map/gather/gate_up/pallas_call | solution.py:49
  76.6 1.3 %hidden.3 = (bf16[3,256,256]{2,1,0:T(8,128)(2,1)S(1)}, f32[1,384]{1,0:T(1,128)S(1)}) custom-call(s32[3]{0:T(128)S(1)} %pad_add_fusion.pos_ref.refs_1_.refs_2_.refs_3_, bf16[64,128,128]{2,1,0:T(8,128)(2,1)S(1)} %get-tuple-element.39.w0, bf16[64,128,128]{2,1,0:T(8,128)(2,1)S(1)} %get-tuple-element.40.w1, bf16[64,128,128]{2,1,0:T(8,128)(2,1)S(1)} %get-tuple-element.41.w2, ...), custom_call_target="tpu_custom_call" | custom-call | flops 402653184 | bytes 8915980 | tf_op jit(solution)/shard_map/gather/hidden/pallas_call | solution.py:49
  77.9 1.5 %input_away.2 = bf16[16,128,256]{2,1,0:T(8,128)(2,1)S(1)} custom-call(s32[3]{0:T(128)S(1)} %pad_add_fusion.pos_ref.refs_1_.refs_2_.refs_3_, bf16[3,256,256]{2,1,0:T(8,128)(2,1)S(1)} %get-tuple-element.56.grad_ref, bf16[64,128,256]{2,1,0:T(8,128)(2,1)S(1)} %get-tuple-element.48.refs_4_.w0, bf16[64,128,256]{2,1,0:T(8,128)(2,1)S(1)} %get-tuple-element.49.refs_5_.w1, ...), custom_call_target="tpu_custom_call" | custom-call | flops 805306368 | bytes 14024716 | tf_op jit(solution)/shard_map/scatter/input_away/pallas_call | solution.py:49
  79.6 1.5 %input_away.3 = bf16[16,128,256]{2,1,0:T(8,128)(2,1)S(1)} custom-call(s32[3]{0:T(128)S(1)} %pad_add_fusion.pos_ref.refs_1_.refs_2_.refs_3_, bf16[3,256,256]{2,1,0:T(8,128)(2,1)S(1)} %get-tuple-element.56.grad_ref, bf16[64,128,256]{2,1,0:T(8,128)(2,1)S(1)} %get-tuple-element.48.refs_4_.w0, bf16[64,128,256]{2,1,0:T(8,128)(2,1)S(1)} %get-tuple-element.49.refs_5_.w1, ...), custom_call_target="tpu_custom_call" | custom-call | flops 805306368 | bytes 14024716 | tf_op jit(solution)/shard_map/scatter/input_away/pallas_call | solution.py:49
  81.2 0.5 collective-permute-start.30
  81.6 0.5 collective-permute-done.24.refs_0_
  82.2 1.5 %input_here.2 = (bf16[4,128,256]{2,1,0:T(8,128)(2,1)S(1)}, bf16[4,128,256]{2,1,0:T(8,128)(2,1)S(1)}, f32[4,128,256]{2,1,0:T(8,128)S(1)}, f32[4,128,256]{2,1,0:T(8,128)S(1)}) custom-call(s32[3]{0:T(128)S(1)} %pad_add_fusion.pos_ref.refs_1_.refs_2_.refs_3_, bf16[3,256,256]{2,1,0:T(8,128)(2,1)S(1)} %get-tuple-element.56.grad_ref, ...), custom_call_target="tpu_custom_call" | custom-call | flops 805306368 | bytes 15597580 | tf_op jit(solution)/shard_map/scatter/input_here/pallas_call | solution.py:49
  83.7 1.5 %collective-permute-start.25 = (bf16[4,128,256]{2,1,0:T(8,128)(2,1)S(1)}, bf16[4,128,256]{2,1,0:T(8,128)(2,1)S(1)}, u32[]{:S(2)}, u32[]{:S(2)}) collective-permute-start(bf16[4,128,256]{2,1,0:T(8,128)(2,1)S(1)} %get-tuple-element.59), channel_id=1, source_target_pairs={{0,16},{1,17},{2,18},{3,19},{4,20},{5,21},{6,22},{7,23},{8,24},{9,... | collective-permute-start | bytes 786440 | tf_op jit(solution)/shard_map/scatter/ppermute | solution.py:29
  85.2 1.5 %input_here.3 = (bf16[4,128,256]{2,1,0:T(8,128)(2,1)S(1)}, bf16[4,128,256]{2,1,0:T(8,128)(2,1)S(1)}, f32[4,128,256]{2,1,0:T(8,128)S(1)}, f32[4,128,256]{2,1,0:T(8,128)S(1)}) custom-call(s32[3]{0:T(128)S(1)} %pad_add_fusion.pos_ref.refs_1_.refs_2_.refs_3_, bf16[3,256,256]{2,1,0:T(8,128)(2,1)S(1)} %get-tuple-element.56.grad_ref, ...), custom_call_target="tpu_custom_call" | custom-call | flops 805306368 | bytes 15597580 | tf_op jit(solution)/shard_map/scatter/input_here/pallas_call | solution.py:49
  86.7 0.7 collective-permute-start.32
  87.5 2.6 %collective-permute-start.31 = (bf16[4,128,256]{2,1,0:T(8,128)(2,1)S(1)}, bf16[4,128,256]{2,1,0:T(8,128)(2,1)S(1)}, u32[]{:S(2)}, u32[]{:S(2)}) collective-permute-start(bf16[4,128,256]{2,1,0:T(8,128)(2,1)S(1)} %get-tuple-element.64), channel_id=1, source_target_pairs={{0,16},{1,17},{2,18},{3,19},{4,20},{5,21},{6,22},{7,23},{8,24},{9,... | collective-permute-start | bytes 786440 | tf_op jit(solution)/shard_map/scatter/ppermute | solution.py:29
  90.1 2.8 %collective-permute-done.25.r = bf16[4,128,256]{2,1,0:T(8,128)(2,1)S(1)} collective-permute-done((bf16[4,128,256]{2,1,0:T(8,128)(2,1)S(1)}, bf16[4,128,256]{2,1,0:T(8,128)(2,1)S(1)}, u32[]{:S(2)}, u32[]{:S(2)}) %collective-permute-start.25) | collective-permute-done | bytes 262176 | tf_op jit(solution)/shard_map/scatter/ppermute | solution.py:29
  92.9 2.7 %collective-permute-start.26 = (bf16[4,128,256]{2,1,0:T(8,128)(2,1)S(1)}, bf16[4,128,256]{2,1,0:T(8,128)(2,1)S(1)}, u32[]{:S(2)}, u32[]{:S(2)}) collective-permute-start(bf16[4,128,256]{2,1,0:T(8,128)(2,1)S(1)} %add.17), channel_id=1, source_target_pairs={{0,16},{1,17},{2,18},{3,19},{4,20},{5,21},{6,22},{7,23},{8,24},{9,... | collective-permute-start | bytes 786440 | tf_op jit(solution)/shard_map/scatter/ppermute | solution.py:29
  95.7 0.6 collective-permute-done.32.r
  96.4 0.8 collective-permute-start.33
  97.2 1.6 %collective-permute-start.27 = (f32[384]{0:T(512)S(1)}, f32[384]{0:T(512)S(1)}, u32[]{:S(2)}, u32[]{:S(2)}) collective-permute-start(f32[384]{0:T(512)S(1)} %reduce), channel_id=1, source_target_pairs={{0,64},{64,0},{128,192},{192,128},{1,65},{65,1},{129,193},{193,129... | collective-permute-start | bytes 4616 | tf_op jit(solution)/shard_map/ia3/ppermute | solution.py:425
  98.7 2.1 %collective-permute-done.27 = f32[384]{0:T(512)S(1)} collective-permute-done((f32[384]{0:T(512)S(1)}, f32[384]{0:T(512)S(1)}, u32[]{:S(2)}, u32[]{:S(2)}) %collective-permute-start.27) | collective-permute-done | bytes 1568 | tf_op jit(solution)/shard_map/ia3/ppermute | solution.py:425
  100.8 2.8 %collective-permute-start.28 = (f32[384]{0:T(512)S(1)}, f32[384]{0:T(512)S(1)}, u32[]{:S(2)}, u32[]{:S(2)}) collective-permute-start(f32[384]{0:T(512)S(1)} %add.10), channel_id=1, source_target_pairs={{0,192},{192,0},{64,128},{128,64},{1,193},{193,1},{65,129},{129,65... | collective-permute-start | bytes 4616 | tf_op jit(solution)/shard_map/ia3/ppermute | solution.py:426
  103.6 2.0 %collective-permute-done.28 = f32[384]{0:T(512)S(1)} collective-permute-done((f32[384]{0:T(512)S(1)}, f32[384]{0:T(512)S(1)}, u32[]{:S(2)}, u32[]{:S(2)}) %collective-permute-start.28) | collective-permute-done | bytes 1568 | tf_op jit(solution)/shard_map/ia3/ppermute | solution.py:426
  105.6 0.6 add.11
  106.2 3.2 %collective-permute-done.33.rb3 = bf16[4,128,256]{2,1,0:T(8,128)(2,1)S(1)} collective-permute-done((bf16[4,128,256]{2,1,0:T(8,128)(2,1)S(1)}, bf16[4,128,256]{2,1,0:T(8,128)(2,1)S(1)}, u32[]{:S(2)}, u32[]{:S(2)}) %collective-permute-start.33) | collective-permute-done | bytes 262176 | tf_op jit(solution)/shard_map/scatter/ppermute | solution.py:29
  109.4 0.7 y_sum.1
  110.1 19.4 %all_to_all.5.parts = bf16[8,128,256]{2,1,0:T(8,128)(2,1)S(1)} all-to-all(bf16[8,128,256]{2,1,0:T(8,128)(2,1)S(1)} %y_sum.1), channel_id=1, replica_groups={{0,2,4,6,8,10,12,14},{1,3,5,7,9,11,13,15},{16,18,20,22,24,26,28,30},{17..., dimensions={0} | all-to-all | bytes 1048576 | tf_op jit(solution)/shard_map/scatter/all_to_all | solution.py:444
  129.6 0.8 z_sum.1
  (55 shorter events, 1.9 us)
Async XLA Ops:
  0.6 1.6 %collective-permute-start = (bf16[256,128]{1,0:T(8,128)(2,1)}, bf16[256,128]{1,0:T(8,128)(2,1)S(1)}, u32[]{:S(2)}, u32[]{:S(2)}) collective-permute-start(bf16[256,128]{1,0:T(8,128)(2,1)} %tok.1), channel_id=1, source_target_pairs={{0,1},{1,0},{2,3},{3,2},{4,5},{5,4},{6,7},{7,6},{8,9},{9,8},{10,11... | collective-permute-start | bytes 196616 | tf_op jit(solution)/shard_map/gather/ppermute | solution.py:29
  0.7 1.6 %collective-permute-start.1 = (bf16[256,128]{1,0:T(8,128)(2,1)}, bf16[256,128]{1,0:T(8,128)(2,1)S(1)}, u32[]{:S(2)}, u32[]{:S(2)}) collective-permute-start(bf16[256,128]{1,0:T(8,128)(2,1)} %cot.1), channel_id=1, source_target_pairs={{0,1},{1,0},{2,3},{3,2},{4,5},{5,4},{6,7},{7,6},{8,9},{9,8},{10,11... | collective-permute-start | bytes 196616 | tf_op jit(solution)/shard_map/gather/ppermute | solution.py:29
  2.3 0.8 copy-start.2
  3.2 0.8 copy-start.3
  5.1 13.7 %collective-permute-start.2 = (bf16[2,256,128]{2,1,0:T(8,128)(2,1)S(1)}, bf16[2,256,128]{2,1,0:T(8,128)(2,1)S(1)}, u32[]{:S(2)}, u32[]{:S(2)}) collective-permute-start(bf16[2,256,128]{2,1,0:T(8,128)(2,1)S(1)} %get-tuple-element.35.chip), channel_id=1, source_target_pairs={{0,16},{1,49},{2,18},{3,51},{4,20},{5,53},{6,22},{7,55},{8,24},{9,... | collective-permute-start | bytes 393224 | tf_op jit(solution)/shard_map/gather/ppermute | solution.py:29
  7.1 10.1 %collective-permute-start.3 = (bf16[256,128]{1,0:T(8,128)(2,1)S(1)}, bf16[256,128]{1,0:T(8,128)(2,1)S(1)}, u32[]{:S(2)}, u32[]{:S(2)}) collective-permute-start(bf16[256,128]{1,0:T(8,128)(2,1)S(1)} %copy-done.3), channel_id=1, source_target_pairs={{0,32},{1,33},{2,34},{3,35},{4,36},{5,37},{6,38},{7,39},{8,40},{9,... | collective-permute-start | bytes 196616 | tf_op jit(solution)/shard_map/gather/ppermute | solution.py:29
  8.0 18.9 %collective-permute-start.5 = (bf16[2,128,256]{2,1,0:T(8,128)(2,1)S(1)}, bf16[2,128,256]{2,1,0:T(8,128)(2,1)S(1)}, u32[]{:S(2)}, u32[]{:S(2)}) collective-permute-start(bf16[2,128,256]{2,1,0:T(8,128)(2,1)S(1)} %get-tuple-element.37.refs_2_), channel_id=1, source_target_pairs={{0,2},{1,15},{2,4},{3,1},{4,6},{5,3},{6,8},{7,5},{8,10},{9,7},{10,... | collective-permute-start | bytes 393224 | tf_op jit(solution)/shard_map/gather/ppermute | solution.py:29
  9.9 17.0 %collective-permute-start.6 = (bf16[2,128,256]{2,1,0:T(8,128)(2,1)S(1)}, bf16[2,128,256]{2,1,0:T(8,128)(2,1)S(1)}, u32[]{:S(2)}, u32[]{:S(2)}) collective-permute-start(bf16[2,128,256]{2,1,0:T(8,128)(2,1)S(1)} %get-tuple-element.37.refs_2_), channel_id=1, source_target_pairs={{0,4},{1,13},{2,6},{3,15},{4,8},{5,1},{6,10},{7,3},{8,12},{9,5},{1... | collective-permute-start | bytes 393224 | tf_op jit(solution)/shard_map/gather/ppermute | solution.py:29
  13.2 14.7 %collective-permute-start.7 = (bf16[2,128,256]{2,1,0:T(8,128)(2,1)S(1)}, bf16[2,128,256]{2,1,0:T(8,128)(2,1)S(1)}, u32[]{:S(2)}, u32[]{:S(2)}) collective-permute-start(bf16[2,128,256]{2,1,0:T(8,128)(2,1)S(1)} %get-tuple-element.37.refs_2_), channel_id=1, source_target_pairs={{0,6},{1,11},{2,8},{3,13},{4,10},{5,15},{6,12},{7,1},{8,14},{9,3},... | collective-permute-start | bytes 393224 | tf_op jit(solution)/shard_map/gather/ppermute | solution.py:29
  17.2 9.6 %collective-permute-start.8 = (bf16[128,256]{1,0:T(8,128)(2,1)S(1)}, bf16[128,256]{1,0:T(8,128)(2,1)S(1)}, u32[]{:S(2)}, u32[]{:S(2)}) collective-permute-start(bf16[128,256]{1,0:T(8,128)(2,1)S(1)} %get-tuple-element.38), channel_id=1, source_target_pairs={{0,8},{1,9},{2,10},{3,11},{4,12},{5,13},{6,14},{7,15},{8,0},{9,1},... | collective-permute-start | bytes 196616 | tf_op jit(solution)/shard_map/gather/ppermute | solution.py:29
  18.8 3.7 %copy-start = (s32[3,48,128,128]{3,2,1,0:T(8,128)S(1)}, s32[3,48,128,128]{3,2,1,0:T(8,128)}, u32[]{:S(2)}) copy-start(s32[3,48,128,128]{3,2,1,0:T(8,128)} %refs_1_.7) | copy-start | bytes 28311556
  22.5 14.4 %slice-start = ((s8[9437184]{0:T(1024)(128)(4,1)}), s8[4194304]{0:T(1024)(128)(4,1)S(1)}, s32[]{:S(2)}) async-start(s8[9437184]{0:T(1024)(128)(4,1)} %bitcast.3), calls=%async_computation.1 | async-start | bytes 8388608
  22.5 14.4 %slice-start.1 = ((s8[9437184]{0:T(1024)(128)(4,1)}), s8[4194304]{0:T(1024)(128)(4,1)S(1)}, s32[]{:S(2)}) async-start(s8[9437184]{0:T(1024)(128)(4,1)} %bitcast.3), calls=%async_computation.2 | async-start | bytes 8388608
  22.5 14.4 %slice-start.2 = ((s8[9437184]{0:T(1024)(128)(4,1)}), s8[1048576]{0:T(1024)(128)(4,1)S(1)}, s32[]{:S(2)}) async-start(s8[9437184]{0:T(1024)(128)(4,1)} %bitcast.3), calls=%async_computation.3 | async-start | bytes 2097152
  22.5 14.4 %copy-start.1 = (f32[3,3,48,128]{3,2,1,0:T(8,128)S(1)}, f32[3,3,48,128]{3,2,1,0:T(8,128)}, u32[]{:S(2)}) copy-start(f32[3,3,48,128]{3,2,1,0:T(8,128)} %refs_4_.5) | copy-start | bytes 663556
  22.5 14.4 %copy-start.4 = (s32[3,48]{1,0:T(4,128)S(1)}, s32[3,48]{1,0:T(4,128)}, u32[]{:S(2)}) copy-start(s32[3,48]{1,0:T(4,128)} %refs_2_.5) | copy-start | bytes 1732
  22.5 14.4 %copy-start.5 = (s32[3]{0:T(128)S(1)}, s32[3]{0:T(128)}, u32[]{:S(2)}) copy-start(s32[3]{0:T(128)} %refs_3_.5) | copy-start | bytes 40
  27.9 2.8 %collective-permute-start.9 = (bf16[7,128,256]{2,1,0:T(8,128)(2,1)S(1)}, bf16[7,128,256]{2,1,0:T(8,128)(2,1)S(1)}, u32[]{:S(2)}, u32[]{:S(2)}) collective-permute-start(bf16[7,128,256]{2,1,0:T(8,128)(2,1)S(1)} %stack.21.refs_3_), channel_id=1, source_target_pairs={{0,1},{1,0},{2,3},{3,2},{4,5},{5,4},{6,7},{7,6},{8,9},{9,8},{10,11... | collective-permute-start | bytes 1376264 | tf_op jit(solution)/shard_map/gather/ppermute | solution.py:29
  28.0 2.1 %collective-permute-start.4 = (bf16[3,256,128]{2,1,0:T(8,128)(2,1)S(1)}, bf16[3,256,128]{2,1,0:T(8,128)(2,1)S(1)}, u32[]{:S(2)}, u32[]{:S(2)}) collective-permute-start(bf16[3,256,128]{2,1,0:T(8,128)(2,1)S(1)} %stack.20.mine.refs_0_), channel_id=1, source_target_pairs={{0,1},{1,0},{2,3},{3,2},{4,5},{5,4},{6,7},{7,6},{8,9},{9,8},{10,11... | collective-permute-start | bytes 589832 | tf_op jit(solution)/shard_map/gather/ppermute | solution.py:29
  31.3 20.2 %collective-permute-start.10 = (bf16[16,128,256]{2,1,0:T(8,128)(2,1)S(1)}, bf16[16,128,256]{2,1,0:T(8,128)(2,1)S(1)}, u32[]{:S(2)}, u32[]{:S(2)}) collective-permute-start(bf16[16,128,256]{2,1,0:T(8,128)(2,1)S(1)} %merge_c.1.refs_0_), channel_id=1, source_target_pairs={{0,16},{1,49},{2,18},{3,51},{4,20},{5,53},{6,22},{7,55},{8,24},{9,... | collective-permute-start | bytes 3145736 | tf_op jit(solution)/shard_map/gather/ppermute | solution.py:29
  33.1 7.6 %collective-permute-start.16 = (bf16[4,256,128]{2,1,0:T(8,128)(2,1)S(1)}, bf16[4,256,128]{2,1,0:T(8,128)(2,1)S(1)}, u32[]{:S(2)}, u32[]{:S(2)}) collective-permute-start(bf16[4,256,128]{2,1,0:T(8,128)(2,1)S(1)} %get-tuple-element.44.refs_8_), channel_id=1, source_target_pairs={{0,2},{1,15},{2,4},{3,1},{4,6},{5,3},{6,8},{7,5},{8,10},{9,7},{10,... | collective-permute-start | bytes 786440 | tf_op jit(solution)/shard_map/gather/ppermute | solution.py:29
  34.7 8.9 %collective-permute-start.13 = (bf16[4,256,128]{2,1,0:T(8,128)(2,1)S(1)}, bf16[4,256,128]{2,1,0:T(8,128)(2,1)S(1)}, u32[]{:S(2)}, u32[]{:S(2)}) collective-permute-start(bf16[4,256,128]{2,1,0:T(8,128)(2,1)S(1)} %get-tuple-element.36.refs_0_.refs_7_), channel_id=1, source_target_pairs={{0,2},{1,15},{2,4},{3,1},{4,6},{5,3},{6,8},{7,5},{8,10},{9,7},{10,... | collective-permute-start | bytes 786440 | tf_op jit(solution)/shard_map/gather/ppermute | solution.py:29
  40.7 7.6 %collective-permute-start.17 = (bf16[4,256,128]{2,1,0:T(8,128)(2,1)S(1)}, bf16[4,256,128]{2,1,0:T(8,128)(2,1)S(1)}, u32[]{:S(2)}, u32[]{:S(2)}) collective-permute-start(bf16[4,256,128]{2,1,0:T(8,128)(2,1)S(1)} %collective-permute-done.16.refs_1_), channel_id=1, source_target_pairs={{0,2},{1,15},{2,4},{3,1},{4,6},{5,3},{6,8},{7,5},{8,10},{9,7},{10,... | collective-permute-start | bytes 786440 | tf_op jit(solution)/shard_map/gather/ppermute | solution.py:29
  43.5 7.6 %collective-permute-start.14 = (bf16[4,256,128]{2,1,0:T(8,128)(2,1)S(1)}, bf16[4,256,128]{2,1,0:T(8,128)(2,1)S(1)}, u32[]{:S(2)}, u32[]{:S(2)}) collective-permute-start(bf16[4,256,128]{2,1,0:T(8,128)(2,1)S(1)} %collective-permute-done.13.refs_0_), channel_id=1, source_target_pairs={{0,2},{1,15},{2,4},{3,1},{4,6},{5,3},{6,8},{7,5},{8,10},{9,7},{10,... | collective-permute-start | bytes 786440 | tf_op jit(solution)/shard_map/gather/ppermute | solution.py:29
  51.2 14.6 %collective-permute-start.20 = (bf16[16,256,128]{2,1,0:T(8,128)(2,1)S(1)}, bf16[16,256,128]{2,1,0:T(8,128)(2,1)S(1)}, u32[]{:S(2)}, u32[]{:S(2)}) collective-permute-start(bf16[16,256,128]{2,1,0:T(8,128)(2,1)S(1)} %stack.22.refs_9_), channel_id=1, source_target_pairs={{0,1},{1,0},{2,3},{3,2},{4,5},{5,4},{6,7},{7,6},{8,9},{9,8},{10,11... | collective-permute-start | bytes 3145736 | tf_op jit(solution)/shard_map/gather/ppermute | solution.py:29
  51.5 19.0 %collective-permute-start.21 = (bf16[16,128,256]{2,1,0:T(8,128)(2,1)S(1)}, bf16[16,128,256]{2,1,0:T(8,128)(2,1)S(1)}, u32[]{:S(2)}, u32[]{:S(2)}) collective-permute-start(bf16[16,128,256]{2,1,0:T(8,128)(2,1)S(1)} %collective-permute-done.10.a.refs_1_), channel_id=1, source_target_pairs={{0,1},{1,0},{2,3},{3,2},{4,5},{5,4},{6,7},{7,6},{8,9},{9,8},{10,11... | collective-permute-start | bytes 3145736 | tf_op jit(solution)/shard_map/gather/ppermute | solution.py:29
  52.6 12.7 %collective-permute-start.11 = (bf16[8,128,256]{2,1,0:T(8,128)(2,1)S(1)}, bf16[8,128,256]{2,1,0:T(8,128)(2,1)S(1)}, u32[]{:S(2)}, u32[]{:S(2)}) collective-permute-start(bf16[8,128,256]{2,1,0:T(8,128)(2,1)S(1)} %part.1), channel_id=1, source_target_pairs={{0,16},{1,49},{2,18},{3,51},{4,20},{5,53},{6,22},{7,55},{8,24},{9,... | collective-permute-start | bytes 1572872 | tf_op jit(solution)/shard_map/gather/ppermute | solution.py:29
  52.7 8.6 %collective-permute-start.18 = (bf16[4,256,128]{2,1,0:T(8,128)(2,1)S(1)}, bf16[4,256,128]{2,1,0:T(8,128)(2,1)S(1)}, u32[]{:S(2)}, u32[]{:S(2)}) collective-permute-start(bf16[4,256,128]{2,1,0:T(8,128)(2,1)S(1)} %collective-permute-done.17.refs_3_), channel_id=1, source_target_pairs={{0,2},{1,15},{2,4},{3,1},{4,6},{5,3},{6,8},{7,5},{8,10},{9,7},{10,... | collective-permute-start | bytes 786440 | tf_op jit(solution)/shard_map/gather/ppermute | solution.py:29
  52.7 10.4 %collective-permute-start.15 = (bf16[4,256,128]{2,1,0:T(8,128)(2,1)S(1)}, bf16[4,256,128]{2,1,0:T(8,128)(2,1)S(1)}, u32[]{:S(2)}, u32[]{:S(2)}) collective-permute-start(bf16[4,256,128]{2,1,0:T(8,128)(2,1)S(1)} %collective-permute-done.14.refs_2_), channel_id=1, source_target_pairs={{0,2},{1,15},{2,4},{3,1},{4,6},{5,3},{6,8},{7,5},{8,10},{9,7},{10,... | collective-permute-start | bytes 786440 | tf_op jit(solution)/shard_map/gather/ppermute | solution.py:29
  65.0 7.7 %collective-permute-start.19 = (bf16[4,256,128]{2,1,0:T(8,128)(2,1)S(1)}, bf16[4,256,128]{2,1,0:T(8,128)(2,1)S(1)}, u32[]{:S(2)}, u32[]{:S(2)}) collective-permute-start(bf16[4,256,128]{2,1,0:T(8,128)(2,1)S(1)} %pick.1), channel_id=1, source_target_pairs={{0,2},{1,15},{2,4},{3,1},{4,6},{5,3},{6,8},{7,5},{8,10},{9,7},{10,... | collective-permute-start | bytes 786440 | tf_op jit(solution)/shard_map/gather/ppermute | solution.py:29
  65.1 7.9 %collective-permute-start.22 = (bf16[8,256,128]{2,1,0:T(8,128)(2,1)S(1)}, bf16[8,256,128]{2,1,0:T(8,128)(2,1)S(1)}, u32[]{:S(2)}, u32[]{:S(2)}) collective-permute-start(bf16[8,256,128]{2,1,0:T(8,128)(2,1)S(1)} %stack.23.refs_0_), channel_id=1, source_target_pairs={{0,1},{1,0},{2,3},{3,2},{4,5},{5,4},{6,7},{7,6},{8,9},{9,8},{10,11... | collective-permute-start | bytes 1572872 | tf_op jit(solution)/shard_map/gather/ppermute | solution.py:29
  65.3 11.3 %collective-permute-start.12 = (bf16[8,128,256]{2,1,0:T(8,128)(2,1)S(1)}, bf16[8,128,256]{2,1,0:T(8,128)(2,1)S(1)}, u32[]{:S(2)}, u32[]{:S(2)}) collective-permute-start(bf16[8,128,256]{2,1,0:T(8,128)(2,1)S(1)} %collective-permute-done.11.refs_0_), channel_id=1, source_target_pairs={{0,1},{1,0},{2,3},{3,2},{4,5},{5,4},{6,7},{7,6},{8,9},{9,8},{10,11... | collective-permute-start | bytes 1572872 | tf_op jit(solution)/shard_map/gather/ppermute | solution.py:29
  70.5 2.4 %copy-start.6 = (f32[384]{0:T(512)S(1)}, f32[384]{0:T(512)}, u32[]{:S(2)}) copy-start(f32[384]{0:T(512)} %param.13) | copy-start | bytes 4612
  72.7 1.6 %collective-permute-start.23 = (bf16[4,256,128]{2,1,0:T(8,128)(2,1)S(1)}, bf16[4,256,128]{2,1,0:T(8,128)(2,1)S(1)}, u32[]{:S(2)}, u32[]{:S(2)}) collective-permute-start(bf16[4,256,128]{2,1,0:T(8,128)(2,1)S(1)} %collective-permute-done.19.refs_2_), channel_id=1, source_target_pairs={{0,1},{1,0},{2,3},{3,2},{4,5},{5,4},{6,7},{7,6},{8,9},{9,8},{10,11... | collective-permute-start | bytes 786440 | tf_op jit(solution)/shard_map/gather/ppermute | solution.py:29
  79.4 2.7 %collective-permute-start.24 = (bf16[16,128,256]{2,1,0:T(8,128)(2,1)S(1)}, bf16[16,128,256]{2,1,0:T(8,128)(2,1)S(1)}, u32[]{:S(2)}, u32[]{:S(2)}) collective-permute-start(bf16[16,128,256]{2,1,0:T(8,128)(2,1)S(1)} %input_away.2), channel_id=1, source_target_pairs={{0,1},{1,0},{2,3},{3,2},{4,5},{5,4},{6,7},{7,6},{8,9},{9,8},{10,11... | collective-permute-start | bytes 3145736 | tf_op jit(solution)/shard_map/scatter/ppermute | solution.py:29
  81.2 4.1 %collective-permute-start.30 = (bf16[16,128,256]{2,1,0:T(8,128)(2,1)S(1)}, bf16[16,128,256]{2,1,0:T(8,128)(2,1)S(1)}, u32[]{:S(2)}, u32[]{:S(2)}) collective-permute-start(bf16[16,128,256]{2,1,0:T(8,128)(2,1)S(1)} %input_away.3), channel_id=1, source_target_pairs={{0,1},{1,0},{2,3},{3,2},{4,5},{5,4},{6,7},{7,6},{8,9},{9,8},{10,11... | collective-permute-start | bytes 3145736 | tf_op jit(solution)/shard_map/scatter/ppermute | solution.py:29
  83.7 9.2 %collective-permute-start.25 = (bf16[4,128,256]{2,1,0:T(8,128)(2,1)S(1)}, bf16[4,128,256]{2,1,0:T(8,128)(2,1)S(1)}, u32[]{:S(2)}, u32[]{:S(2)}) collective-permute-start(bf16[4,128,256]{2,1,0:T(8,128)(2,1)S(1)} %get-tuple-element.59), channel_id=1, source_target_pairs={{0,16},{1,17},{2,18},{3,19},{4,20},{5,21},{6,22},{7,23},{8,24},{9,... | collective-permute-start | bytes 786440 | tf_op jit(solution)/shard_map/scatter/ppermute | solution.py:29
  86.7 9.6 %collective-permute-start.32 = (bf16[4,128,256]{2,1,0:T(8,128)(2,1)S(1)}, bf16[4,128,256]{2,1,0:T(8,128)(2,1)S(1)}, u32[]{:S(2)}, u32[]{:S(2)}) collective-permute-start(bf16[4,128,256]{2,1,0:T(8,128)(2,1)S(1)} %get-tuple-element.66), channel_id=1, source_target_pairs={{0,48},{1,49},{2,50},{3,51},{4,52},{5,53},{6,54},{7,55},{8,56},{9,... | collective-permute-start | bytes 786440 | tf_op jit(solution)/shard_map/scatter/ppermute | solution.py:29
  87.5 18.8 %collective-permute-start.31 = (bf16[4,128,256]{2,1,0:T(8,128)(2,1)S(1)}, bf16[4,128,256]{2,1,0:T(8,128)(2,1)S(1)}, u32[]{:S(2)}, u32[]{:S(2)}) collective-permute-start(bf16[4,128,256]{2,1,0:T(8,128)(2,1)S(1)} %get-tuple-element.64), channel_id=1, source_target_pairs={{0,16},{1,17},{2,18},{3,19},{4,20},{5,21},{6,22},{7,23},{8,24},{9,... | collective-permute-start | bytes 786440 | tf_op jit(solution)/shard_map/scatter/ppermute | solution.py:29
  92.9 13.3 %collective-permute-start.26 = (bf16[4,128,256]{2,1,0:T(8,128)(2,1)S(1)}, bf16[4,128,256]{2,1,0:T(8,128)(2,1)S(1)}, u32[]{:S(2)}, u32[]{:S(2)}) collective-permute-start(bf16[4,128,256]{2,1,0:T(8,128)(2,1)S(1)} %add.17), channel_id=1, source_target_pairs={{0,16},{1,17},{2,18},{3,19},{4,20},{5,21},{6,22},{7,23},{8,24},{9,... | collective-permute-start | bytes 786440 | tf_op jit(solution)/shard_map/scatter/ppermute | solution.py:29
  95.7 10.5 %collective-permute-start.29 = (bf16[4,128,256]{2,1,0:T(8,128)(2,1)S(1)}, bf16[4,128,256]{2,1,0:T(8,128)(2,1)S(1)}, u32[]{:S(2)}, u32[]{:S(2)}) collective-permute-start(bf16[4,128,256]{2,1,0:T(8,128)(2,1)S(1)} %get-tuple-element.62), channel_id=1, source_target_pairs={{0,48},{1,49},{2,50},{3,51},{4,52},{5,53},{6,54},{7,55},{8,56},{9,... | collective-permute-start | bytes 786440 | tf_op jit(solution)/shard_map/scatter/ppermute | solution.py:29
  96.4 13.1 %collective-permute-start.33 = (bf16[4,128,256]{2,1,0:T(8,128)(2,1)S(1)}, bf16[4,128,256]{2,1,0:T(8,128)(2,1)S(1)}, u32[]{:S(2)}, u32[]{:S(2)}) collective-permute-start(bf16[4,128,256]{2,1,0:T(8,128)(2,1)S(1)} %add.18), channel_id=1, source_target_pairs={{0,48},{1,49},{2,50},{3,51},{4,52},{5,53},{6,54},{7,55},{8,56},{9,... | collective-permute-start | bytes 786440 | tf_op jit(solution)/shard_map/scatter/ppermute | solution.py:29
  97.2 3.7 %collective-permute-start.27 = (f32[384]{0:T(512)S(1)}, f32[384]{0:T(512)S(1)}, u32[]{:S(2)}, u32[]{:S(2)}) collective-permute-start(f32[384]{0:T(512)S(1)} %reduce), channel_id=1, source_target_pairs={{0,64},{64,0},{128,192},{192,128},{1,65},{65,1},{129,193},{193,129... | collective-permute-start | bytes 4616 | tf_op jit(solution)/shard_map/ia3/ppermute | solution.py:425
  100.8 4.8 %collective-permute-start.28 = (f32[384]{0:T(512)S(1)}, f32[384]{0:T(512)S(1)}, u32[]{:S(2)}, u32[]{:S(2)}) collective-permute-start(f32[384]{0:T(512)S(1)} %add.10), channel_id=1, source_target_pairs={{0,192},{192,0},{64,128},{128,64},{1,193},{193,1},{65,129},{129,65... | collective-permute-start | bytes 4616 | tf_op jit(solution)/shard_map/ia3/ppermute | solution.py:426
